TPU v7x, 256 devices: a whole 4x4x8 slice. The times are simulated.
256 devices in a mesh: ctx: 32 (over x, z), tp: 8 (over y, core).
Axes of the slice: x: 4, y: 4, z: 8, core: 2. Of those that a mesh axis runs over, the one named last changes fastest.
Arguments:
- features: bfloat16 [16384, 3, 4096], P('ctx', None, 'tp'), may hold values from -6 to 6
- short_filter: float32 [7, 3, 4096], P(None, None, 'tp'), may hold values from -2 to 2
- medium_filter: float32 [128, 256], replicated, may hold values from -4 to 4
- skip_bias: float32 [4096], P('tp'), may hold values from -4 to 4
- cotangent: bfloat16 [16384, 4096], P('ctx', 'tp'), may hold values from -6 to 6
- doc_lengths: int32 [64], replicated, may hold values from 1 to 1024, 16384 in all
Outputs:
- grad_features: bfloat16 [16384, 3, 4096], P('ctx', None, 'tp')
- grad_short_filter: float32 [7, 3, 4096], P(None, None, 'tp')
- grad_medium_filter: float32 [128, 256], replicated
- grad_skip: float32 [4096], P('tp')
Inputs may be any that keep to these rules, and one draw needn't show every extreme that they name: `doc_lengths`: the lengths sum to 16384; the longest is exactly 1024.
All inputs are finite; a program needn't handle non-finite values.
Results may differ from a plain program's by a relative error of at most 0.0073.
Values may be sent and summed in bfloat16 or wider, within the bound.
No kernel may reach another device: no remote copies, remote signals or barrier semaphores. Data moves between devices by JAX's collectives and lax.ppermute only.
A program may use at most 192 MiB of HBM per device.

v0:
```python
import functools
import math

import jax
import jax.numpy as jnp
from jax import lax
from jax.experimental import pallas as pl
from jax.experimental.pallas import tpu as pltpu
from jax.sharding import PartitionSpec as P

STRETCH = 256
TILE = 128
GROUP = 16
PER_TILE = TILE // GROUP
LAGS = 128
TAPS = 7
EDGE = 16
TAIL = 128 + 3 * EDGE
HEAD = 144 + 4 * EDGE
DOCS = 64
F32 = jnp.float32
BF16 = jnp.bfloat16


def base_of(device, members, member):
    first = device * STRETCH
    second = (2 * members - 1 - device) * STRETCH
    if isinstance(member, int):
        return first if member == 0 else second
    return jnp.where(member == 0, first, second)


def lane_starts(lengths_ref, base, count):
    position = (base + lax.broadcasted_iota(jnp.int32, (8, count), 1)).astype(F32)
    found = jnp.zeros((8, count), F32)
    running = jnp.int32(0)
    for doc in range(DOCS):
        here = running.astype(F32)
        found = jnp.where(position >= here, here, found)
        running = running + lengths_ref[doc]
    return found


def row_starts(starts, block):
    row = starts[0:1, block * 128 : (block + 1) * 128]
    return jnp.broadcast_to(row, (128, 128)).T


def row_positions(base, block):
    return (base + block * 128 + lax.broadcasted_iota(jnp.int32, (128, 128), 0)).astype(F32)


def own_kernel(
    members, device_ref, lengths_ref, feat_ref, cot_ref, taps_ref,
    kvg_ref, up_ref, down_ref, masks, rows,
):
    device = device_ref[0]

    @pl.when(pl.program_id(0) == 0)
    def _():
        for member in range(2):
            base = base_of(device, members, member)
            starts = lane_starts(lengths_ref, base, STRETCH)
            for block in range(2):
                offset = row_positions(base, block) - row_starts(starts, block)
                for lag in range(1, TAPS):
                    masks[member, lag - 1, pl.ds(block * 128, 128), :] = jnp.where(
                        offset >= lag, 1.0, 0.0
                    )

    for member in range(2):
        first = member * STRETCH
        for stream in range(3):
            rows[pl.ds(0, 8), :] = jnp.zeros((8, TILE), F32)
            rows[pl.ds(8, STRETCH), :] = feat_ref[stream, pl.ds(first, STRETCH), :].astype(F32)
            weights = taps_ref[stream]
            for chunk in range(0, STRETCH, 64):
                total = rows[pl.ds(8 + chunk, 64), :] * weights[0:1, :]
                for lag in range(1, TAPS):
                    moved = rows[pl.ds(8 + chunk - lag, 64), :] * weights[lag : lag + 1, :]
                    total = total + moved * masks[member, lag - 1, pl.ds(chunk, 64), :]
                rounded = total.astype(BF16)
                if stream == 0:
                    cot = cot_ref[pl.ds(first + chunk, 64), :].astype(F32)
                    rounded = (cot * rounded.astype(F32)).astype(BF16)
                    kvg_ref[2, pl.ds(first + chunk, 64), :] = rounded
                else:
                    kvg_ref[stream - 1, pl.ds(first + chunk, 64), :] = rounded
    for member in range(2):
        first = member * STRETCH
        tail_ref = up_ref if member == 0 else down_ref
        head_ref = down_ref if member == 0 else up_ref
        last = first + 128
        mixed = kvg_ref[0, pl.ds(last, 128), :].astype(F32) * kvg_ref[1, pl.ds(last, 128), :].astype(F32)
        tail_ref[pl.ds(0, 128), :] = mixed.astype(BF16)
        for stream in range(3):
            tail_ref[pl.ds(128 + stream * EDGE, EDGE), :] = feat_ref[
                stream, pl.ds(first + STRETCH - EDGE, EDGE), :
            ]
            head_ref[pl.ds(TAIL + 144 + stream * EDGE, EDGE), :] = feat_ref[
                stream, pl.ds(first, EDGE), :
            ]
        head_ref[pl.ds(TAIL, 144), :] = kvg_ref[2, pl.ds(first, 144), :]
        head_ref[pl.ds(TAIL + 144 + 3 * EDGE, EDGE), :] = cot_ref[pl.ds(first, EDGE), :]


def tables_kernel(
    members, device_ref, lengths_ref, medium_ref,
    forward_ref, backward_ref, keep_f_ref, keep_b_ref, keep_r_ref, shifted_ref, edge_ref,
    forward_rows, backward_rows, offsets,
):
    device = device_ref[0]

    @pl.when(pl.program_id(0) == 0)
    def _():
        lag = lax.broadcasted_iota(jnp.int32, (LAGS, 256), 0)
        lane = lax.broadcasted_iota(jnp.int32, (LAGS, 256), 1)
        taps = medium_ref[...].astype(BF16)
        dims = (((0,), (0,)), ((), ()))
        place_f = jnp.where(lane == LAGS - lag, 1.0, 0.0).astype(BF16)
        place_b = jnp.where(lane == lag, 1.0, 0.0).astype(BF16)
        forward_rows[...] = lax.dot_general(taps, place_f, dims, preferred_element_type=F32)
        backward_rows[...] = lax.dot_general(taps, place_b, dims, preferred_element_type=F32)
        wide = lax.broadcasted_iota(jnp.int32, (128, 256), 1)
        tall = lax.broadcasted_iota(jnp.int32, (128, 256), 0)
        for member in range(2):
            base = base_of(device, members, member)
            starts = lane_starts(lengths_ref, base, 512)
            for block in range(3):
                begin = row_starts(starts, block)
                begin = jnp.concatenate([begin, begin], axis=1)
                source = (base + (block - 1) * 128 + wide).astype(F32)
                keep_f_ref[member, block] = jnp.where(source >= begin, 1.0, 0.0).astype(BF16)
                if block < 2:
                    turned = (base + (block - 1) * 128 + 255 - wide).astype(F32)
                    keep_r_ref[member, block] = jnp.where(turned >= begin, 1.0, 0.0)
                own = (base + block * 128 + tall).astype(F32)
                target = jnp.broadcast_to(starts[0:1, block * 128 : block * 128 + 256], (128, 256))
                keep_b_ref[member, block] = jnp.where(own >= target, 1.0, 0.0).astype(BF16)
                offsets[pl.ds(block * 128, 128), :] = row_positions(base, block) - begin[:, :128]
            for lag in range(1, TAPS):
                shifted_ref[member, lag - 1] = jnp.where(
                    offsets[pl.ds(lag, STRETCH), :] >= lag, 1.0, 0.0
                )
                for side in range(2):
                    edge_ref[member, side, lag - 1] = jnp.where(
                        offsets[pl.ds(side * STRETCH, EDGE), :] >= lag, 1.0, 0.0
                    )

    first = pl.multiple_of(device_ref[1] * 32 + pl.program_id(0) * PER_TILE, PER_TILE)
    rows_f = forward_rows[pl.ds(first, PER_TILE), :]
    rows_b = backward_rows[pl.ds(first, PER_TILE), :]
    for group in range(PER_TILE):
        for rows, out_ref in ((rows_f, forward_ref), (rows_b, backward_ref)):
            spread = jnp.broadcast_to(rows[group : group + 1, :], (128, 256))
            out_ref[group] = pltpu.roll(spread, 0, 1, stride=1, stride_axis=0).astype(BF16)


def edge_conv(rows, weights, edge_ref, side):
    total = rows[pl.ds(EDGE, EDGE), :] * weights[0:1, :]
    for lag in range(1, TAPS):
        moved = rows[pl.ds(EDGE - lag, EDGE), :] * weights[lag : lag + 1, :]
        total = total + moved * edge_ref[side, lag - 1]
    return total.astype(BF16).astype(F32)


def main_kernel(
    members, device_ref, feat_ref, kvg_ref, cot_ref, own_up_ref, up_ref, down_ref, taps_ref, skip_ref,
    forward_ref, backward_ref, keep_f_ref, keep_b_ref, keep_r_ref, shifted_ref, edge_ref,
    out_ref, sums_ref,
    left, right, rows, keys, values, mixed, grads, cots, stack, pairs,
):
    member = pl.program_id(1)
    is_last = device_ref[0] == members - 1

    @pl.when(member == 0)
    def _():
        left[...] = up_ref[pl.ds(0, TAIL), :]

    @pl.when((member == 1) & is_last)
    def _():
        left[...] = own_up_ref[pl.ds(0, TAIL), :]

    @pl.when((member == 1) & jnp.logical_not(is_last))
    def _():
        left[...] = down_ref[pl.ds(0, TAIL), :]

    @pl.when(member == 1)
    def _():
        right[...] = up_ref[pl.ds(TAIL, HEAD), :]

    @pl.when((member == 0) & is_last)
    def _():
        right[...] = own_up_ref[pl.ds(TAIL, HEAD), :]

    @pl.when((member == 0) & jnp.logical_not(is_last))
    def _():
        right[...] = down_ref[pl.ds(TAIL, HEAD), :]

    keys[pl.ds(EDGE, STRETCH - EDGE), :] = kvg_ref[0, pl.ds(EDGE, STRETCH - EDGE), :].astype(F32)
    values[pl.ds(EDGE, STRETCH - EDGE), :] = kvg_ref[1, pl.ds(EDGE, STRETCH - EDGE), :].astype(F32)
    cots[pl.ds(0, STRETCH), :] = cot_ref[...].astype(F32)
    cots[pl.ds(STRETCH, EDGE), :] = right[pl.ds(144 + 3 * EDGE, EDGE), :].astype(F32)
    for stream in range(3):
        weights = taps_ref[stream]
        for side in range(2):
            if side == 0:
                before = left[pl.ds(128 + stream * EDGE, EDGE), :]
                after = feat_ref[stream, pl.ds(0, EDGE), :]
            else:
                before = feat_ref[stream, pl.ds(STRETCH - EDGE, EDGE), :]
                after = right[pl.ds(144 + stream * EDGE, EDGE), :]
            rows[pl.ds(0, EDGE), :] = before.astype(F32)
            rows[pl.ds(EDGE, EDGE), :] = after.astype(F32)
            fixed = edge_conv(rows, weights, edge_ref.at[0], side)
            place = pl.ds(side * STRETCH, EDGE)
            if stream == 0:
                grads[place, :] = (cots[place, :] * fixed).astype(BF16)
            elif stream == 1:
                keys[place, :] = fixed
            else:
                values[place, :] = fixed
    mixed[pl.ds(0, 128), :] = left[pl.ds(0, 128), :]
    mixed[pl.ds(128, STRETCH + EDGE), :] = (keys[...] * values[...]).astype(BF16)
    mixed[pl.ds(400, 112), :] = jnp.zeros((112, TILE), BF16)
    grads[pl.ds(EDGE, STRETCH - EDGE), :] = kvg_ref[2, pl.ds(EDGE, STRETCH - EDGE), :]
    grads[pl.ds(STRETCH + EDGE, 128), :] = right[pl.ds(EDGE, 128), :]
    grads[pl.ds(400, 112), :] = jnp.zeros((112, TILE), BF16)

    lane_group = lax.broadcasted_iota(jnp.int32, (128, TILE), 1) // GROUP
    skip = skip_ref[...]
    turn = jnp.where(
        lax.broadcasted_iota(jnp.int32, (256, 256), 0) + lax.broadcasted_iota(jnp.int32, (256, 256), 1) == 255,
        1.0, 0.0,
    ).astype(BF16)

    def convolved(table_ref, keep_ref, window, block):
        height = 128 if block < 2 else EDGE
        keep = keep_ref[0, block, pl.ds(0, height), :]
        result = jnp.zeros((height, TILE), F32)
        for group in range(PER_TILE):
            matrix = table_ref[group, pl.ds(0, height), :] * keep
            product = jnp.dot(matrix, window, preferred_element_type=F32)
            result = jnp.where(lane_group[:height] == group, product, result)
        return result

    for block in range(3):
        height = 128 if block < 2 else EDGE
        place = pl.ds(block * 128, height)
        window = mixed[pl.ds(block * 128, 256), :]
        medium = convolved(forward_ref, keep_f_ref, window, block)
        medium = medium + skip * mixed[pl.ds(block * 128 + 128, height), :].astype(F32)
        grad_conv = convolved(backward_ref, keep_b_ref, grads[pl.ds(block * 128, 256), :], block)
        grad_conv = grad_conv + skip * grads[place, :].astype(F32)
        stack[0, place, :] = (cots[place, :] * medium).astype(BF16).astype(F32)
        stack[1, place, :] = (grad_conv * values[place, :]).astype(BF16).astype(F32)
        stack[2, place, :] = (grad_conv * keys[place, :]).astype(BF16).astype(F32)
        if block < 2:
            turned = jnp.dot(turn, window, preferred_element_type=F32).astype(BF16)
            own = grads[place, :]
            for group in range(PER_TILE):
                chosen = jnp.where(lane_group == group, own.astype(F32), 0.0).astype(BF16)
                pair = lax.dot_general(
                    chosen, turned, (((1,), (1,)), ((), ())), preferred_element_type=F32
                )
                pair = pair * keep_r_ref[0, block]
                if block == 0:
                    @pl.when(member == 0)
                    def _():
                        pairs[group] = pair

                    @pl.when(member == 1)
                    def _():
                        pairs[group] = pairs[group] + pair
                else:
                    pairs[group] = pairs[group] + pair

    @pl.when(member == 0)
    def _():
        sums_ref[...] = jnp.zeros(sums_ref.shape, F32)

    for stream in range(3):
        weights = taps_ref[stream]
        partial = [jnp.zeros((8, TILE), F32) for _ in range(TAPS)]
        for chunk in range(0, STRETCH, 64):
            source = feat_ref[stream, pl.ds(chunk, 64), :].astype(F32)
            total = jnp.zeros((64, TILE), F32)
            for lag in range(TAPS):
                later = stack[stream, pl.ds(chunk + lag, 64), :]
                if lag > 0:
                    later = later * shifted_ref[0, lag - 1, pl.ds(chunk, 64), :]
                total = total + later * weights[lag : lag + 1, :]
                partial[lag] = partial[lag] + jnp.sum((later * source).reshape(8, 8, TILE), axis=0)
            out_ref[stream, pl.ds(chunk, 64), :] = total.astype(BF16)
        for lag in range(TAPS):
            row = pl.ds(stream * 8 + lag, 1)
            sums_ref[row, :] += jnp.sum(partial[lag], axis=0, keepdims=True)
    bias = jnp.sum(
        grads[pl.ds(0, STRETCH), :].astype(F32) * mixed[pl.ds(128, STRETCH), :].astype(F32),
        axis=0, keepdims=True,
    )
    sums_ref[pl.ds(7, 1), :] += bias

    @pl.when(member == 1)
    def _():
        for group in range(PER_TILE):
            turned_back = pltpu.roll(pairs[group], 129, 1, stride=1, stride_axis=0)
            sums_ref[pl.ds(24 + group, 1), :] = jnp.sum(turned_back, axis=0, keepdims=True)[:, :LAGS]


def turn_kernel(scale, gathered_ref, out_ref):
    out_ref[...] = gathered_ref[...].T * scale


def exchange(block, axis, flip):
    size = lax.axis_size(axis)
    return lax.ppermute(block, axis, [(i, i ^ flip) for i in range(size)])


def shards(features, short_filter, medium_filter, skip_bias, cotangent, doc_lengths):
    members = lax.axis_size("ctx")
    device = lax.axis_index("ctx")
    tp = lax.axis_index("tp")
    channels = features.shape[2]
    tiles = channels // TILE
    scale = 1.0 / math.sqrt(2 * STRETCH * members)
    streams = jnp.transpose(features, (1, 0, 2))
    weights = jnp.transpose(short_filter, (1, 0, 2))
    where_am_i = jnp.stack([device, tp]).astype(jnp.int32)
    smem = pl.BlockSpec(memory_space=pltpu.SMEM)
    shape = jax.ShapeDtypeStruct
    params = pltpu.CompilerParams(vmem_limit_bytes=40 * 1024 * 1024)

    kvg, pay_up, pay_down = pl.pallas_call(
        functools.partial(own_kernel, members),
        grid=(tiles,),
        in_specs=[
            smem, smem,
            pl.BlockSpec((3, 2 * STRETCH, TILE), lambda l: (0, 0, l)),
            pl.BlockSpec((2 * STRETCH, TILE), lambda l: (0, l)),
            pl.BlockSpec((3, TAPS, TILE), lambda l: (0, 0, l)),
        ],
        out_specs=[
            pl.BlockSpec((3, 2 * STRETCH, TILE), lambda l: (0, 0, l)),
            pl.BlockSpec((TAIL + HEAD, TILE), lambda l: (0, l)),
            pl.BlockSpec((TAIL + HEAD, TILE), lambda l: (0, l)),
        ],
        out_shape=[
            shape((3, 2 * STRETCH, channels), BF16),
            shape((TAIL + HEAD, channels), BF16),
            shape((TAIL + HEAD, channels), BF16),
        ],
        scratch_shapes=[
            pltpu.VMEM((2, TAPS - 1, STRETCH, TILE), F32),
            pltpu.VMEM((STRETCH + 8, TILE), F32),
        ],
        compiler_params=params,
        cost_estimate=pl.CostEstimate(flops=40_000_000, bytes_accessed=4_500_000, transcendentals=0),
        name="own_rows",
    )(where_am_i, doc_lengths, streams, cotangent, weights)

    got_up = lax.ppermute(pay_up, "ctx", [(i, i + 1) for i in range(members - 1)])
    got_down = lax.ppermute(pay_down, "ctx", [(i + 1, i) for i in range(members - 1)])

    groups = channels // GROUP
    tables = pl.pallas_call(
        functools.partial(tables_kernel, members),
        grid=(tiles,),
        in_specs=[smem, smem, pl.BlockSpec(medium_filter.shape, lambda l: (0, 0))],
        out_specs=[
            pl.BlockSpec((PER_TILE, 128, 256), lambda l: (l, 0, 0)),
            pl.BlockSpec((PER_TILE, 128, 256), lambda l: (l, 0, 0)),
            pl.BlockSpec((2, 3, 128, 256), lambda l: (0, 0, 0, 0)),
            pl.BlockSpec((2, 3, 128, 256), lambda l: (0, 0, 0, 0)),
            pl.BlockSpec((2, 2, 128, 256), lambda l: (0, 0, 0, 0)),
            pl.BlockSpec((2, TAPS - 1, STRETCH, TILE), lambda l: (0, 0, 0, 0)),
            pl.BlockSpec((2, 2, TAPS - 1, EDGE, TILE), lambda l: (0, 0, 0, 0, 0)),
        ],
        out_shape=[
            shape((groups, 128, 256), BF16),
            shape((groups, 128, 256), BF16),
            shape((2, 3, 128, 256), BF16),
            shape((2, 3, 128, 256), BF16),
            shape((2, 2, 128, 256), F32),
            shape((2, TAPS - 1, STRETCH, TILE), F32),
            shape((2, 2, TAPS - 1, EDGE, TILE), F32),
        ],
        scratch_shapes=[
            pltpu.VMEM((256, 256), F32),
            pltpu.VMEM((256, 256), F32),
            pltpu.VMEM((384, TILE), F32),
        ],
        compiler_params=params,
        cost_estimate=pl.CostEstimate(flops=20_000_000, bytes_accessed=7_000_000, transcendentals=0),
        name="tables",
    )(where_am_i, doc_lengths, medium_filter)

    ends = pl.BlockSpec((TAIL + HEAD, TILE), lambda l, m: (0, l))
    matrix = pl.BlockSpec((PER_TILE, 128, 256), lambda l, m: (l, 0, 0))
    grad_streams, sums = pl.pallas_call(
        functools.partial(main_kernel, members),
        grid=(tiles, 2),
        in_specs=[
            smem,
            pl.BlockSpec((3, STRETCH, TILE), lambda l, m: (0, m, l)),
            pl.BlockSpec((3, STRETCH, TILE), lambda l, m: (0, m, l)),
            pl.BlockSpec((STRETCH, TILE), lambda l, m: (m, l)),
            ends, ends, ends,
            pl.BlockSpec((3, TAPS, TILE), lambda l, m: (0, 0, l)),
            pl.BlockSpec((1, TILE), lambda l, m: (0, l)),
            matrix, matrix,
            pl.BlockSpec((1, 3, 128, 256), lambda l, m: (m, 0, 0, 0)),
            pl.BlockSpec((1, 3, 128, 256), lambda l, m: (m, 0, 0, 0)),
            pl.BlockSpec((1, 2, 128, 256), lambda l, m: (m, 0, 0, 0)),
            pl.BlockSpec((1, TAPS - 1, STRETCH, TILE), lambda l, m: (m, 0, 0, 0)),
            pl.BlockSpec((1, 2, TAPS - 1, EDGE, TILE), lambda l, m: (m, 0, 0, 0, 0)),
        ],
        out_specs=[
            pl.BlockSpec((3, STRETCH, TILE), lambda l, m: (0, m, l)),
            pl.BlockSpec((32, TILE), lambda l, m: (0, l)),
        ],
        out_shape=[shape((3, 2 * STRETCH, channels), BF16), shape((32, channels), F32)],
        scratch_shapes=[
            pltpu.VMEM((TAIL, TILE), BF16),
            pltpu.VMEM((HEAD, TILE), BF16),
            pltpu.VMEM((2 * EDGE, TILE), F32),
            pltpu.VMEM((STRETCH + EDGE, TILE), F32),
            pltpu.VMEM((STRETCH + EDGE, TILE), F32),
            pltpu.VMEM((512, TILE), BF16),
            pltpu.VMEM((512, TILE), BF16),
            pltpu.VMEM((STRETCH + EDGE, TILE), F32),
            pltpu.VMEM((3, STRETCH + EDGE, TILE), F32),
            pltpu.VMEM((PER_TILE, 128, 256), F32),
        ],
        compiler_params=params,
        cost_estimate=pl.CostEstimate(flops=900_000_000, bytes_accessed=12_000_000, transcendentals=0),
        name="main_rows",
    )(
        where_am_i, streams, kvg, cotangent, pay_up, got_up, got_down, weights,
        skip_bias.reshape(1, channels), *tables,
    )

    flip = 1
    while flip < members:
        sums = sums + exchange(sums, "ctx", flip)
        flip *= 2
    mine = sums[24:].reshape(PER_TILE, tiles, LAGS).transpose(1, 0, 2).reshape(groups, LAGS)
    gathered = mine
    flip = 1
    while flip < lax.axis_size("tp"):
        other = exchange(gathered, "tp", flip)
        upper = (tp // flip) % 2 == 1
        gathered = jnp.concatenate(
            [jnp.where(upper, other, gathered), jnp.where(upper, gathered, other)], axis=0
        )
        flip *= 2
    grad_medium = pl.pallas_call(
        functools.partial(turn_kernel, scale),
        out_shape=shape(medium_filter.shape, F32),
        name="turn",
    )(gathered)
    short = jnp.transpose(sums[:24].reshape(3, 8, channels)[:, :TAPS], (1, 0, 2)) * scale
    return (jnp.transpose(grad_streams, (1, 0, 2)), short, grad_medium, sums[7] * scale)


def solution(mesh):
    in_specs = (P("ctx", None, "tp"), P(None, None, "tp"), P(), P("tp"), P("ctx", "tp"), P())
    out_specs = (P("ctx", None, "tp"), P(None, None, "tp"), P(), P("tp"))
    return jax.shard_map(shards, mesh=mesh, in_specs=in_specs, out_specs=out_specs, check_vma=False)
```

profile of v0, /device:TPU:64, one launch (start us, length us, event | category | flops | bytes accessed | tf_op | source)
XLA Modules:
  0.0 102.7 jit_solution(6530433141008686017)
XLA Ops:
  0.6 0.0 copy-start.6
  0.6 0.1 pad_add_fusion.device_ref
  0.7 0.0 copy-start
  0.7 1.4 %copy-done = bf16[512,3,512]{2,0,1:T(8,128)(2,1)S(1)} copy-done((bf16[512,3,512]{2,0,1:T(8,128)(2,1)S(1)}, bf16[512,3,512]{2,0,1:T(8,128)(2,1)}, u32[]{:S(2)}) %copy-start) | copy-done | bytes 1572888
  2.1 0.0 copy-start.2
  2.1 1.0 %copy-done.2 = bf16[512,512]{1,0:T(8,128)(2,1)S(1)} copy-done((bf16[512,512]{1,0:T(8,128)(2,1)S(1)}, bf16[512,512]{1,0:T(8,128)(2,1)}, u32[]{:S(2)}) %copy-start.2) | copy-done | bytes 524312
  3.2 0.0 copy-start.4
  3.2 0.8 copy-done.4
  4.0 0.0 copy-start.7
  4.0 0.7 copy-done.7
  4.6 0.0 copy-start.1
  4.6 0.0 copy-start.3
  4.6 4.0 %own_rows.1 = (bf16[3,512,512]{2,1,0:T(8,128)(2,1)S(1)}, bf16[384,512]{1,0:T(8,128)(2,1)S(1)}, bf16[384,512]{1,0:T(8,128)(2,1)S(1)}) custom-call(s32[2]{0:T(128)S(1)} %pad_add_fusion.device_ref, s32[64]{0:T(128)S(1)} %copy-done.7, bf16[3,512,512]{2,1,0:T(8,128)(2,1)S(1)} %bitcast.21, bf16[512,512]{1,0:T(8,128)(2,1)S(1)} %copy-done.2, f32[3,7,512]{2,1,0:T(8,128)S(1)} %bitcast.23), custom_call_target="tpu_custom_call" | custom-call | flops 40000000 | bytes 4500000 | tf_op jit(solution)/shard_map/own_rows/pallas_call | solution.py:334
  8.7 3.8 %collective-permute-start = (bf16[384,512]{1,0:T(8,128)(2,1)S(1)}, bf16[384,512]{1,0:T(8,128)(2,1)S(1)}, u32[]{:S(2)}, u32[]{:S(2)}) collective-permute-start(bf16[384,512]{1,0:T(8,128)(2,1)S(1)} %get-tuple-element.17.own_up_ref), channel_id=1, source_target_pairs={{0,8},{8,16},{16,24},{24,32},{32,40},{40,48},{48,56},{56,64},{64,7... | collective-permute-start | bytes 1179656 | tf_op jit(solution)/shard_map/ppermute | solution.py:362
  12.5 2.0 %collective-permute-start.1 = (bf16[384,512]{1,0:T(8,128)(2,1)S(1)}, bf16[384,512]{1,0:T(8,128)(2,1)S(1)}, u32[]{:S(2)}, u32[]{:S(2)}) collective-permute-start(bf16[384,512]{1,0:T(8,128)(2,1)S(1)} %get-tuple-element.18), channel_id=1, source_target_pairs={{8,0},{16,8},{24,16},{32,24},{40,32},{48,40},{56,48},{64,56},{72,6... | collective-permute-start | bytes 1179656 | tf_op jit(solution)/shard_map/ppermute | solution.py:363
  14.5 0.0 copy-start.5
  14.5 0.9 copy-done.5
  15.4 2.6 %tables.1 = (bf16[32,128,256]{2,1,0:T(8,128)(2,1)S(1)}, bf16[32,128,256]{2,1,0:T(8,128)(2,1)S(1)}, bf16[2,3,128,256]{3,2,1,0:T(8,128)(2,1)S(1)}, bf16[2,3,128,25...) custom-call(s32[2]{0:T(128)S(1)} %pad_add_fusion.device_ref, ...), custom_call_target="tpu_custom_call" | custom-call | flops 20000000 | bytes 7000000 | tf_op jit(solution)/shard_map/tables/pallas_call | solution.py:366
  18.1 3.3 %collective-permute-done.up_ref = bf16[384,512]{1,0:T(8,128)(2,1)S(1)} collective-permute-done((bf16[384,512]{1,0:T(8,128)(2,1)S(1)}, bf16[384,512]{1,0:T(8,128)(2,1)S(1)}, u32[]{:S(2)}, u32[]{:S(2)}) %collective-permute-start) | collective-permute-done | bytes 393248 | tf_op jit(solution)/shard_map/ppermute | solution.py:362
  21.4 4.9 %collective-permute-done.1.down_ref = bf16[384,512]{1,0:T(8,128)(2,1)S(1)} collective-permute-done((bf16[384,512]{1,0:T(8,128)(2,1)S(1)}, bf16[384,512]{1,0:T(8,128)(2,1)S(1)}, u32[]{:S(2)}, u32[]{:S(2)}) %collective-permute-start.1) | collective-permute-done | bytes 393248 | tf_op jit(solution)/shard_map/ppermute | solution.py:363
  26.4 0.0 copy-done.6
  26.4 0.0 copy-done.1
  26.4 0.0 copy-done.3
  26.4 33.1 %main_rows.1 = (bf16[3,512,512]{2,1,0:T(8,128)(2,1)}, f32[32,512]{1,0:T(8,128)S(1)}) custom-call(s32[2]{0:T(128)S(1)} %pad_add_fusion.device_ref, bf16[3,512,512]{2,1,0:T(8,128)(2,1)S(1)} %bitcast.22, bf16[3,512,512]{2,1,0:T(8,128)(2,1)S(1)} %get-tuple-element.16.kvg_ref, bf16[512,512]{1,0:T(8,128)(2,1)S(1)} %copy-done.3, ...), custom_call_target="tpu_custom_call" | custom-call | flops 900000000 | bytes 12000000 | tf_op jit(solution)/shard_map/main_rows/pallas_call | solution.py:400
  59.4 2.9 %collective-permute-start.2 = (f32[32,512]{1,0:T(8,128)S(1)}, f32[32,512]{1,0:T(8,128)S(1)}, u32[]{:S(2)}, u32[]{:S(2)}) collective-permute-start(f32[32,512]{1,0:T(8,128)S(1)} %get-tuple-element.27), channel_id=1, source_target_pairs={{0,8},{8,0},{16,24},{24,16},{32,40},{40,32},{48,56},{56,48},{64,72... | collective-permute-start | bytes 196616 | tf_op jit(solution)/shard_map/ppermute | solution.py:317
  62.4 2.2 %collective-permute-done.2 = f32[32,512]{1,0:T(8,128)S(1)} collective-permute-done((f32[32,512]{1,0:T(8,128)S(1)}, f32[32,512]{1,0:T(8,128)S(1)}, u32[]{:S(2)}, u32[]{:S(2)}) %collective-permute-start.2) | collective-permute-done | bytes 65568 | tf_op jit(solution)/shard_map/ppermute | solution.py:317
  64.6 0.1 collective-permute-start.3
  64.7 5.2 %collective-permute-done.3 = f32[32,512]{1,0:T(8,128)S(1)} collective-permute-done((f32[32,512]{1,0:T(8,128)S(1)}, f32[32,512]{1,0:T(8,128)S(1)}, u32[]{:S(2)}, u32[]{:S(2)}) %collective-permute-start.3) | collective-permute-done | bytes 65568 | tf_op jit(solution)/shard_map/ppermute | solution.py:317
  69.9 2.6 %collective-permute-start.4 = (f32[32,512]{1,0:T(8,128)S(1)}, f32[32,512]{1,0:T(8,128)S(1)}, u32[]{:S(2)}, u32[]{:S(2)}) collective-permute-start(f32[32,512]{1,0:T(8,128)S(1)} %add.29), channel_id=1, source_target_pairs={{0,32},{8,40},{16,48},{24,56},{32,0},{40,8},{48,16},{56,24},{64,96... | collective-permute-start | bytes 196616 | tf_op jit(solution)/shard_map/ppermute | solution.py:317
  72.5 5.8 %collective-permute-done.4 = f32[32,512]{1,0:T(8,128)S(1)} collective-permute-done((f32[32,512]{1,0:T(8,128)S(1)}, f32[32,512]{1,0:T(8,128)S(1)}, u32[]{:S(2)}, u32[]{:S(2)}) %collective-permute-start.4) | collective-permute-done | bytes 65568 | tf_op jit(solution)/shard_map/ppermute | solution.py:317
  78.3 1.6 %collective-permute-start.5 = (f32[32,512]{1,0:T(8,128)S(1)}, f32[32,512]{1,0:T(8,128)S(1)}, u32[]{:S(2)}, u32[]{:S(2)}) collective-permute-start(f32[32,512]{1,0:T(8,128)S(1)} %add.30), channel_id=1, source_target_pairs={{0,64},{8,72},{16,80},{24,88},{32,96},{40,104},{48,112},{56,120},{... | collective-permute-start | bytes 196616 | tf_op jit(solution)/shard_map/ppermute | solution.py:317
  79.9 3.4 %collective-permute-done.5 = f32[32,512]{1,0:T(8,128)S(1)} collective-permute-done((f32[32,512]{1,0:T(8,128)S(1)}, f32[32,512]{1,0:T(8,128)S(1)}, u32[]{:S(2)}, u32[]{:S(2)}) %collective-permute-start.5) | collective-permute-done | bytes 65568 | tf_op jit(solution)/shard_map/ppermute | solution.py:317
  83.3 2.5 %collective-permute-start.6 = (f32[32,512]{1,0:T(8,128)S(1)}, f32[32,512]{1,0:T(8,128)S(1)}, u32[]{:S(2)}, u32[]{:S(2)}) collective-permute-start(f32[32,512]{1,0:T(8,128)S(1)} %add.31), channel_id=1, source_target_pairs={{0,128},{8,136},{16,144},{24,152},{32,160},{40,168},{48,176},{56,1... | collective-permute-start | bytes 196616 | tf_op jit(solution)/shard_map/ppermute | solution.py:317
  85.8 3.3 %collective-permute-done.6 = f32[32,512]{1,0:T(8,128)S(1)} collective-permute-done((f32[32,512]{1,0:T(8,128)S(1)}, f32[32,512]{1,0:T(8,128)S(1)}, u32[]{:S(2)}, u32[]{:S(2)}) %collective-permute-start.6) | collective-permute-done | bytes 65568 | tf_op jit(solution)/shard_map/ppermute | solution.py:317
  89.1 0.1 collective-permute-start.7
  89.3 1.2 %collective-permute-done.7 = f32[32,128]{1,0:T(8,128)S(1)} collective-permute-done((f32[32,128]{1,0:T(8,128)S(1)}, f32[32,128]{1,0:T(8,128)S(1)}, u32[]{:S(2)}, u32[]{:S(2)}) %collective-permute-start.7) | collective-permute-done | bytes 16416 | tf_op jit(solution)/shard_map/ppermute | solution.py:317
  90.4 1.7 %collective-permute-start.8 = (f32[64,128]{1,0:T(8,128)S(1)}, f32[64,128]{1,0:T(8,128)S(1)}, u32[]{:S(2)}, u32[]{:S(2)}) collective-permute-start(f32[64,128]{1,0:T(8,128)S(1)} %pad_maximum_fusion.2), channel_id=1, source_target_pairs={{0,2},{1,3},{2,0},{3,1},{4,6},{5,7},{6,4},{7,5},{8,10},{9,11},{10,... | collective-permute-start | bytes 98312 | tf_op jit(solution)/shard_map/ppermute | solution.py:317
  92.1 0.6 fusion
  92.7 1.7 %collective-permute-done.8 = f32[64,128]{1,0:T(8,128)S(1)} collective-permute-done((f32[64,128]{1,0:T(8,128)S(1)}, f32[64,128]{1,0:T(8,128)S(1)}, u32[]{:S(2)}, u32[]{:S(2)}) %collective-permute-start.8) | collective-permute-done | bytes 32800 | tf_op jit(solution)/shard_map/ppermute | solution.py:317
  94.5 3.3 %collective-permute-start.9 = (f32[128,128]{1,0:T(8,128)S(1)}, f32[128,128]{1,0:T(8,128)S(1)}, u32[]{:S(2)}, u32[]{:S(2)}) collective-permute-start(f32[128,128]{1,0:T(8,128)S(1)} %pad_maximum_fusion.1), channel_id=1, source_target_pairs={{0,4},{1,5},{2,6},{3,7},{4,0},{5,1},{6,2},{7,3},{8,12},{9,13},{10,... | collective-permute-start | bytes 196616 | tf_op jit(solution)/shard_map/ppermute | solution.py:317
  97.7 0.6 slice_multiply_fusion.1
  98.3 2.0 %collective-permute-done.9 = f32[128,128]{1,0:T(8,128)S(1)} collective-permute-done((f32[128,128]{1,0:T(8,128)S(1)}, f32[128,128]{1,0:T(8,128)S(1)}, u32[]{:S(2)}, u32[]{:S(2)}) %collective-permute-start.9) | collective-permute-done | bytes 65568 | tf_op jit(solution)/shard_map/ppermute | solution.py:317
  100.3 0.7 pad_maximum_fusion.gathered_ref
  101.0 1.7 %turn.1 = f32[128,256]{1,0:T(8,128)} custom-call(f32[256,128]{1,0:T(8,128)} %pad_maximum_fusion.gathered_ref), custom_call_target="tpu_custom_call" | custom-call | tf_op jit(solution)/shard_map/turn/pallas_call | solution.py:457
  (12 shorter events, 0.1 us)
Async XLA Ops:
  0.6 25.7 %copy-start.6 = (f32[512]{0:T(512)S(1)}, f32[512]{0:T(512)}, u32[]{:S(2)}) copy-start(f32[512]{0:T(512)} %param.9) | copy-start | bytes 6148
  0.7 1.4 %copy-start = (bf16[512,3,512]{2,0,1:T(8,128)(2,1)S(1)}, bf16[512,3,512]{2,0,1:T(8,128)(2,1)}, u32[]{:S(2)}) copy-start(bf16[512,3,512]{2,0,1:T(8,128)(2,1)} %param.6) | copy-start | bytes 4718596
  2.1 1.0 %copy-start.2 = (bf16[512,512]{1,0:T(8,128)(2,1)S(1)}, bf16[512,512]{1,0:T(8,128)(2,1)}, u32[]{:S(2)}) copy-start(bf16[512,512]{1,0:T(8,128)(2,1)} %cot_ref.3) | copy-start | bytes 1572868
  3.2 0.8 copy-start.4
  4.0 0.7 copy-start.7
  4.6 21.7 %copy-start.1 = (bf16[512,3,512]{2,0,1:T(8,128)(2,1)S(1)}, bf16[512,3,512]{2,0,1:T(8,128)(2,1)}, u32[]{:S(2)}) copy-start(bf16[512,3,512]{2,0,1:T(8,128)(2,1)} %param.6) | copy-start | bytes 4718596
  4.6 21.7 %copy-start.3 = (bf16[512,512]{1,0:T(8,128)(2,1)S(1)}, bf16[512,512]{1,0:T(8,128)(2,1)}, u32[]{:S(2)}) copy-start(bf16[512,512]{1,0:T(8,128)(2,1)} %cot_ref.3) | copy-start | bytes 1572868
  8.7 12.7 %collective-permute-start = (bf16[384,512]{1,0:T(8,128)(2,1)S(1)}, bf16[384,512]{1,0:T(8,128)(2,1)S(1)}, u32[]{:S(2)}, u32[]{:S(2)}) collective-permute-start(bf16[384,512]{1,0:T(8,128)(2,1)S(1)} %get-tuple-element.17.own_up_ref), channel_id=1, source_target_pairs={{0,8},{8,16},{16,24},{24,32},{32,40},{40,48},{48,56},{56,64},{64,7... | collective-permute-start | bytes 1179656 | tf_op jit(solution)/shard_map/ppermute | solution.py:362
  12.5 13.9 %collective-permute-start.1 = (bf16[384,512]{1,0:T(8,128)(2,1)S(1)}, bf16[384,512]{1,0:T(8,128)(2,1)S(1)}, u32[]{:S(2)}, u32[]{:S(2)}) collective-permute-start(bf16[384,512]{1,0:T(8,128)(2,1)S(1)} %get-tuple-element.18), channel_id=1, source_target_pairs={{8,0},{16,8},{24,16},{32,24},{40,32},{48,40},{56,48},{64,56},{72,6... | collective-permute-start | bytes 1179656 | tf_op jit(solution)/shard_map/ppermute | solution.py:363
  14.5 0.9 copy-start.5
  59.4 5.2 %collective-permute-start.2 = (f32[32,512]{1,0:T(8,128)S(1)}, f32[32,512]{1,0:T(8,128)S(1)}, u32[]{:S(2)}, u32[]{:S(2)}) collective-permute-start(f32[32,512]{1,0:T(8,128)S(1)} %get-tuple-element.27), channel_id=1, source_target_pairs={{0,8},{8,0},{16,24},{24,16},{32,40},{40,32},{48,56},{56,48},{64,72... | collective-permute-start | bytes 196616 | tf_op jit(solution)/shard_map/ppermute | solution.py:317
  64.6 5.3 %collective-permute-start.3 = (f32[32,512]{1,0:T(8,128)S(1)}, f32[32,512]{1,0:T(8,128)S(1)}, u32[]{:S(2)}, u32[]{:S(2)}) collective-permute-start(f32[32,512]{1,0:T(8,128)S(1)} %add.28), channel_id=1, source_target_pairs={{0,16},{8,24},{16,0},{24,8},{32,48},{40,56},{48,32},{56,40},{64,80... | collective-permute-start | bytes 196616 | tf_op jit(solution)/shard_map/ppermute | solution.py:317
  69.9 8.4 %collective-permute-start.4 = (f32[32,512]{1,0:T(8,128)S(1)}, f32[32,512]{1,0:T(8,128)S(1)}, u32[]{:S(2)}, u32[]{:S(2)}) collective-permute-start(f32[32,512]{1,0:T(8,128)S(1)} %add.29), channel_id=1, source_target_pairs={{0,32},{8,40},{16,48},{24,56},{32,0},{40,8},{48,16},{56,24},{64,96... | collective-permute-start | bytes 196616 | tf_op jit(solution)/shard_map/ppermute | solution.py:317
  78.3 4.9 %collective-permute-start.5 = (f32[32,512]{1,0:T(8,128)S(1)}, f32[32,512]{1,0:T(8,128)S(1)}, u32[]{:S(2)}, u32[]{:S(2)}) collective-permute-start(f32[32,512]{1,0:T(8,128)S(1)} %add.30), channel_id=1, source_target_pairs={{0,64},{8,72},{16,80},{24,88},{32,96},{40,104},{48,112},{56,120},{... | collective-permute-start | bytes 196616 | tf_op jit(solution)/shard_map/ppermute | solution.py:317
  83.3 5.9 %collective-permute-start.6 = (f32[32,512]{1,0:T(8,128)S(1)}, f32[32,512]{1,0:T(8,128)S(1)}, u32[]{:S(2)}, u32[]{:S(2)}) collective-permute-start(f32[32,512]{1,0:T(8,128)S(1)} %add.31), channel_id=1, source_target_pairs={{0,128},{8,136},{16,144},{24,152},{32,160},{40,168},{48,176},{56,1... | collective-permute-start | bytes 196616 | tf_op jit(solution)/shard_map/ppermute | solution.py:317
  89.1 1.3 %collective-permute-start.7 = (f32[32,128]{1,0:T(8,128)S(1)}, f32[32,128]{1,0:T(8,128)S(1)}, u32[]{:S(2)}, u32[]{:S(2)}) collective-permute-start(f32[32,128]{1,0:T(8,128)S(1)} %slice_bitcast_fusion.1), channel_id=1, source_target_pairs={{0,1},{1,0},{2,3},{3,2},{4,5},{5,4},{6,7},{7,6},{8,9},{9,8},{10,11... | collective-permute-start | bytes 49160 | tf_op jit(solution)/shard_map/ppermute | solution.py:317
  90.4 4.0 %collective-permute-start.8 = (f32[64,128]{1,0:T(8,128)S(1)}, f32[64,128]{1,0:T(8,128)S(1)}, u32[]{:S(2)}, u32[]{:S(2)}) collective-permute-start(f32[64,128]{1,0:T(8,128)S(1)} %pad_maximum_fusion.2), channel_id=1, source_target_pairs={{0,2},{1,3},{2,0},{3,1},{4,6},{5,7},{6,4},{7,5},{8,10},{9,11},{10,... | collective-permute-start | bytes 98312 | tf_op jit(solution)/shard_map/ppermute | solution.py:317
  94.5 5.9 %collective-permute-start.9 = (f32[128,128]{1,0:T(8,128)S(1)}, f32[128,128]{1,0:T(8,128)S(1)}, u32[]{:S(2)}, u32[]{:S(2)}) collective-permute-start(f32[128,128]{1,0:T(8,128)S(1)} %pad_maximum_fusion.1), channel_id=1, source_target_pairs={{0,4},{1,5},{2,6},{3,7},{4,0},{5,1},{6,2},{7,3},{8,12},{9,13},{10,... | collective-permute-start | bytes 196616 | tf_op jit(solution)/shard_map/ppermute | solution.py:317
where the time goes:
time: 103 us
  Pallas kernels  41.4 us (40%)
  waiting for transfers between devices  33 us (32%)
  starting transfers between devices  20.6 us (20%)
  local copies, waits for them, and re-layouts  4.82 us (5%)
  other arithmetic  2.03 us (2%)
    pallas_call x1, Pallas kernels, shards(): pl.pallas_call(functools.partial(main_kernel, members), grid=(tiles, 2),...  33.1 us
    ppermute x8, waiting for transfers between devices, exchange(): return lax.ppermute(block, axis, [(i, i ^ flip) for i in range(size)])  24.7 us
    ppermute x8, starting transfers between devices, exchange(): return lax.ppermute(block, axis, [(i, i ^ flip) for i in range(size)])  14.8 us
    ppermute x1, waiting for transfers between devices, shards(): lax.ppermute(pay_down, 'ctx', [(i + 1, i) for i in range(members - 1)])  4.95 us
    unnamed x16, local copies, waits for them, and re-layouts  4.81 us
    pallas_call x1, Pallas kernels, shards(): pl.pallas_call(functools.partial(own_kernel, members), grid=(tiles,), in_...  4.03 us
    ppermute x1, starting transfers between devices, shards(): lax.ppermute(pay_up, 'ctx', [(i, i + 1) for i in range(members - 1)])  3.83 us
    ppermute x1, waiting for transfers between devices, shards(): lax.ppermute(pay_up, 'ctx', [(i, i + 1) for i in range(members - 1)])  3.34 us
  transfers between devices with their start and end apart: 10, of which 10 were waited for; matrix products, arithmetic and copies ran while one was open for 1% of the time, Pallas kernels for 3%

commit v1 on v0

v1 whole, which is shorter than its diff:
```python
import functools
import math

import jax
import jax.numpy as jnp
from jax import lax
from jax.experimental import pallas as pl
from jax.experimental.pallas import tpu as pltpu
from jax.sharding import PartitionSpec as P

STRETCH = 256
TILE = 128
GROUP = 16
PER_TILE = TILE // GROUP
LAGS = 128
TAPS = 7
EDGE = 16
TAIL = 128 + 3 * EDGE
HEAD = 144 + 4 * EDGE
DOCS = 64
F32 = jnp.float32
BF16 = jnp.bfloat16


def base_of(device, members, member):
    first = device * STRETCH
    second = (2 * members - 1 - device) * STRETCH
    if isinstance(member, int):
        return first if member == 0 else second
    return jnp.where(member == 0, first, second)


def lane_starts(lengths_ref, base, count):
    position = (base + lax.broadcasted_iota(jnp.int32, (8, count), 1)).astype(F32)
    found = jnp.zeros((8, count), F32)
    running = jnp.int32(0)
    for doc in range(DOCS):
        here = running.astype(F32)
        found = jnp.where(position >= here, here, found)
        running = running + lengths_ref[doc]
    return found


def row_starts(starts, block):
    row = starts[0:1, block * 128 : (block + 1) * 128]
    return jnp.broadcast_to(row, (128, 128)).T


def row_positions(base, block):
    return (base + block * 128 + lax.broadcasted_iota(jnp.int32, (128, 128), 0)).astype(F32)


def conv_rows(rows, weights, masks, member, first, count):
    total = rows[pl.ds(8 + first, count), :] * weights[0:1, :]
    for lag in range(1, TAPS):
        moved = rows[pl.ds(8 + first - lag, count), :] * weights[lag : lag + 1, :]
        total = total + moved * masks[member, lag - 1, pl.ds(first, count), :]
    return total.astype(BF16)


def own_masks(members, lengths_ref, masks):
    for member in range(2):
        base = base_of(lax.axis_index("ctx"), members, member)
        starts = lane_starts(lengths_ref, base, STRETCH)
        for block in range(2):
            offset = row_positions(base, block) - row_starts(starts, block)
            for lag in range(1, TAPS):
                masks[member, lag - 1, pl.ds(block * 128, 128), :] = jnp.where(offset >= lag, 1.0, 0.0)


def payload_kernel(
    members, lengths_ref, feat_hbm, cot_hbm, taps_ref, up_ref, down_ref, feat, cots, masks, rows, feat_sem, cot_sem,
):
    tiles = feat.shape[0]
    copies = []
    for tile in range(tiles):
        lanes = pl.ds(tile * TILE, TILE)
        copies.append((
            pltpu.make_async_copy(feat_hbm.at[:, :, lanes], feat.at[tile], feat_sem.at[tile]),
            pltpu.make_async_copy(cot_hbm.at[:, lanes], cots.at[tile], cot_sem.at[tile]),
        ))
        copies[-1][0].start()
        copies[-1][1].start()
    own_masks(members, lengths_ref, masks)
    rows[pl.ds(0, 8), :] = jnp.zeros((8, TILE), F32)
    for tile in range(tiles):
        lanes = pl.ds(tile * TILE, TILE)
        copies[tile][0].wait()
        copies[tile][1].wait()
        for member in range(2):
            first = member * STRETCH
            tail_ref = up_ref if member == 0 else down_ref
            head_ref = down_ref if member == 0 else up_ref
            rows[pl.ds(8, 144), :] = feat[tile, 0, pl.ds(first, 144), :].astype(F32)
            weights = taps_ref[0, :, lanes]
            for chunk in range(0, 144, 48):
                query = conv_rows(rows, weights, masks, member, chunk, 48).astype(F32)
                cot = cots[tile, pl.ds(first + chunk, 48), :].astype(F32)
                head_ref[pl.ds(TAIL + chunk, 48), lanes] = (cot * query).astype(BF16)
            for stream in (1, 2):
                rows[pl.ds(8 + 112, 144), :] = feat[tile, stream, pl.ds(first + 112, 144), :].astype(F32)
                weights = taps_ref[stream, :, lanes]
                for chunk in range(0, 128, 64):
                    part = conv_rows(rows, weights, masks, member, 128 + chunk, 64)
                    place = pl.ds(chunk, 64)
                    if stream == 2:
                        part = (tail_ref[place, lanes].astype(F32) * part.astype(F32)).astype(BF16)
                    tail_ref[place, lanes] = part
            for stream in range(3):
                tail_ref[pl.ds(128 + stream * EDGE, EDGE), lanes] = feat[
                    tile, stream, pl.ds(first + STRETCH - EDGE, EDGE), :
                ]
                head_ref[pl.ds(TAIL + 144 + stream * EDGE, EDGE), lanes] = feat[
                    tile, stream, pl.ds(first, EDGE), :
                ]
            head_ref[pl.ds(TAIL + 144 + 3 * EDGE, EDGE), lanes] = cots[tile, pl.ds(first, EDGE), :]


def own_kernel(members, lengths_ref, feat_ref, cot_ref, taps_ref, kvg_ref, masks, rows):
    @pl.when(pl.program_id(0) == 0)
    def _():
        own_masks(members, lengths_ref, masks)

    rows[pl.ds(0, 8), :] = jnp.zeros((8, TILE), F32)
    for member in range(2):
        first = member * STRETCH
        for stream in range(3):
            rows[pl.ds(8, STRETCH), :] = feat_ref[stream, pl.ds(first, STRETCH), :].astype(F32)
            weights = taps_ref[stream]
            for chunk in range(0, STRETCH, 64):
                rounded = conv_rows(rows, weights, masks, member, chunk, 64)
                if stream == 0:
                    cot = cot_ref[pl.ds(first + chunk, 64), :].astype(F32)
                    rounded = (cot * rounded.astype(F32)).astype(BF16)
                    kvg_ref[2, pl.ds(first + chunk, 64), :] = rounded
                else:
                    kvg_ref[stream - 1, pl.ds(first + chunk, 64), :] = rounded


def tables_kernel(
    members, lengths_ref, medium_ref,
    forward_ref, backward_ref, keep_f_ref, keep_b_ref, keep_r_ref, shifted_ref, edge_ref,
    forward_rows, backward_rows, offsets,
):
    device = lax.axis_index("ctx")

    @pl.when(pl.program_id(0) == 0)
    def _():
        lag = lax.broadcasted_iota(jnp.int32, (LAGS, 256), 0)
        lane = lax.broadcasted_iota(jnp.int32, (LAGS, 256), 1)
        taps = medium_ref[...].astype(BF16)
        dims = (((0,), (0,)), ((), ()))
        place_f = jnp.where(lane == LAGS - lag, 1.0, 0.0).astype(BF16)
        place_b = jnp.where(lane == lag, 1.0, 0.0).astype(BF16)
        forward_rows[...] = lax.dot_general(taps, place_f, dims, preferred_element_type=F32)
        backward_rows[...] = lax.dot_general(taps, place_b, dims, preferred_element_type=F32)
        wide = lax.broadcasted_iota(jnp.int32, (128, 256), 1)
        tall = lax.broadcasted_iota(jnp.int32, (128, 256), 0)
        narrow = lax.broadcasted_iota(jnp.int32, (128, 128), 1)
        for member in range(2):
            base = base_of(device, members, member)
            starts = lane_starts(lengths_ref, base, 512)
            for block in range(3):
                begin = row_starts(starts, block)
                begin = jnp.concatenate([begin, begin], axis=1)
                source = (base + (block - 1) * 128 + wide).astype(F32)
                keep_f_ref[member, block] = jnp.where(source >= begin, 1.0, 0.0).astype(BF16)
                if block < 2:
                    turned = jnp.where(
                        narrow + tall[:, :128] >= 127,
                        base + block * 128 + 127 - narrow, base + (block - 1) * 128 + 127 - narrow,
                    ).astype(F32)
                    keep_r_ref[member, block] = jnp.where(turned >= begin[:, :128], 1.0, 0.0)
                own = (base + block * 128 + tall).astype(F32)
                target = jnp.broadcast_to(starts[0:1, block * 128 : block * 128 + 256], (128, 256))
                keep_b_ref[member, block] = jnp.where(own >= target, 1.0, 0.0).astype(BF16)
                offsets[pl.ds(block * 128, 128), :] = row_positions(base, block) - begin[:, :128]
            for lag in range(1, TAPS):
                shifted_ref[member, lag - 1] = jnp.where(
                    offsets[pl.ds(lag, STRETCH), :] >= lag, 1.0, 0.0
                )
                for side in range(2):
                    edge_ref[member, side, lag - 1] = jnp.where(
                        offsets[pl.ds(side * STRETCH, EDGE), :] >= lag, 1.0, 0.0
                    )

    first = pl.multiple_of(lax.axis_index("tp") * 32 + pl.program_id(0) * PER_TILE, PER_TILE)
    rows_f = forward_rows[pl.ds(first, PER_TILE), :]
    rows_b = backward_rows[pl.ds(first, PER_TILE), :]
    for group in range(PER_TILE):
        for rows, out_ref in ((rows_f, forward_ref), (rows_b, backward_ref)):
            spread = jnp.broadcast_to(rows[group : group + 1, :], (128, 256))
            out_ref[group] = pltpu.roll(spread, 0, 1, stride=1, stride_axis=0).astype(BF16)


def edge_conv(rows, weights, edge_ref, side):
    total = rows[pl.ds(EDGE, EDGE), :] * weights[0:1, :]
    for lag in range(1, TAPS):
        moved = rows[pl.ds(EDGE - lag, EDGE), :] * weights[lag : lag + 1, :]
        total = total + moved * edge_ref[side, lag - 1]
    return total.astype(BF16).astype(F32)


def pair_kernel(
    members, feat_ref, kvg_ref, cot_ref, own_up_ref, up_ref, down_ref, taps_ref, keep_r_ref, edge_ref,
    mixed_ref, grads_ref, kv_ref, sums_ref,
    left, right, rows,
):
    member = pl.program_id(1)
    tile = pl.program_id(0)
    lanes = pl.ds(pl.multiple_of(tile * TILE, TILE), TILE)
    base = member * STRETCH

    def own(first, count):
        return pl.ds(pl.multiple_of(base + first, EDGE), count)

    is_last = lax.axis_index("ctx") == members - 1

    @pl.when(member == 0)
    def _():
        left[...] = up_ref[pl.ds(0, TAIL), lanes]

    @pl.when((member == 1) & is_last)
    def _():
        left[...] = own_up_ref[pl.ds(0, TAIL), lanes]

    @pl.when((member == 1) & jnp.logical_not(is_last))
    def _():
        left[...] = down_ref[pl.ds(0, TAIL), lanes]

    @pl.when(member == 1)
    def _():
        right[...] = up_ref[pl.ds(TAIL, HEAD), lanes]

    @pl.when((member == 0) & is_last)
    def _():
        right[...] = own_up_ref[pl.ds(TAIL, HEAD), lanes]

    @pl.when((member == 0) & jnp.logical_not(is_last))
    def _():
        right[...] = down_ref[pl.ds(TAIL, HEAD), lanes]

    inner = pl.ds(EDGE, STRETCH - EDGE)
    for side in range(2):
        place = pl.ds(side * STRETCH, EDGE)
        if side == 0:
            cot = cot_ref[own(0, EDGE), lanes]
        else:
            cot = right[pl.ds(144 + 3 * EDGE, EDGE), :]
        fixed = []
        for stream in range(3):
            if side == 0:
                before = left[pl.ds(128 + stream * EDGE, EDGE), :]
                after = feat_ref[stream, own(0, EDGE), lanes]
            else:
                before = feat_ref[stream, own(STRETCH - EDGE, EDGE), lanes]
                after = right[pl.ds(144 + stream * EDGE, EDGE), :]
            rows[pl.ds(0, EDGE), :] = before.astype(F32)
            rows[pl.ds(EDGE, EDGE), :] = after.astype(F32)
            fixed.append(edge_conv(rows, taps_ref[stream, :, lanes], edge_ref.at[member], side))
        grads_ref[member, place, lanes] = (cot.astype(F32) * fixed[0]).astype(BF16)
        kv_ref[member, 0, place, lanes] = fixed[1].astype(BF16)
        kv_ref[member, 1, place, lanes] = fixed[2].astype(BF16)
        mixed_ref[member, pl.ds(128 + side * STRETCH, EDGE), lanes] = (fixed[1] * fixed[2]).astype(BF16)
    keys = kvg_ref[0, own(EDGE, STRETCH - EDGE), lanes]
    values = kvg_ref[1, own(EDGE, STRETCH - EDGE), lanes]
    kv_ref[member, 0, inner, lanes] = keys
    kv_ref[member, 1, inner, lanes] = values
    mixed_ref[member, pl.ds(0, 128), lanes] = left[pl.ds(0, 128), :]
    mixed_ref[member, pl.ds(128 + EDGE, STRETCH - EDGE), lanes] = (keys.astype(F32) * values.astype(F32)).astype(BF16)
    mixed_ref[member, pl.ds(400, 112), lanes] = jnp.zeros((112, TILE), BF16)
    grads_ref[member, inner, lanes] = kvg_ref[2, own(EDGE, STRETCH - EDGE), lanes]
    grads_ref[member, pl.ds(STRETCH + EDGE, 128), lanes] = right[pl.ds(EDGE, 128), :]
    grads_ref[member, pl.ds(400, 112), lanes] = jnp.zeros((112, TILE), BF16)

    @pl.when(member == 1)
    def _():
        pair_sums(mixed_ref, grads_ref, keep_r_ref, sums_ref, tile, lanes)


def pair_sums(mixed_ref, grads_ref, keep_r_ref, sums_ref, tile, lanes):
    lane = lax.broadcasted_iota(jnp.int32, (128, TILE), 1)
    row = lax.broadcasted_iota(jnp.int32, (128, TILE), 0)
    lane_group = lane // GROUP
    near = lane + row >= 127
    turn = jnp.where(lane + row == 127, 1.0, 0.0).astype(BF16)
    sources = []
    for member in range(2):
        turned = [
            lax.dot_general(
                mixed_ref[member, pl.ds(piece * 128, 128), lanes], turn, (((0,), (0,)), ((), ())),
                preferred_element_type=F32,
            ).astype(BF16)
            for piece in range(3)
        ]
        for block in range(2):
            sources.append(jnp.concatenate([turned[block + 1], turned[block]], axis=1))
    for group in range(PER_TILE):
        choose = jnp.where(lane_group == group, 1.0, 0.0).astype(BF16)
        total = jnp.zeros((128, TILE), F32)
        for member in range(2):
            for block in range(2):
                chosen = grads_ref[member, pl.ds(block * 128, 128), lanes] * choose
                pair = jnp.dot(chosen, sources[member * 2 + block], preferred_element_type=F32)
                pair = jnp.where(near, pair[:, :128], pair[:, 128:])
                total = total + pair * keep_r_ref[member, block]
        lined_up = pltpu.roll(total, 1, 1, stride=1, stride_axis=0)
        sums_ref[pl.ds(tile * PER_TILE + group, 1), :] = jnp.sum(lined_up, axis=0, keepdims=True)


def conv_kernel(
    members, first_tile, feat_ref, mixed_ref, grads_ref, kv_ref, cot_ref, own_up_ref, up_ref, down_ref,
    taps_ref, skip_ref, forward_ref, backward_ref, keep_f_ref, keep_b_ref, shifted_ref,
    previous_ref, out_ref, sums_ref,
    cots, stack,
):
    del previous_ref
    member = pl.program_id(1)
    tile = first_tile + pl.program_id(0)
    lanes = pl.ds(pl.multiple_of(tile * TILE, TILE), TILE)
    base = member * STRETCH

    def own(first, count):
        return pl.ds(pl.multiple_of(base + first, EDGE), count)

    is_last = lax.axis_index("ctx") == members - 1
    first_group = tile * PER_TILE
    lane_group = lax.broadcasted_iota(jnp.int32, (128, TILE), 1) // GROUP
    skip = skip_ref[:, lanes]
    after = pl.ds(TAIL + 144 + 3 * EDGE, EDGE)
    beyond = pl.ds(STRETCH, EDGE)
    cots[pl.ds(0, STRETCH), :] = cot_ref[own(0, STRETCH), lanes].astype(F32)

    @pl.when(member == 1)
    def _():
        cots[beyond, :] = up_ref[after, lanes].astype(F32)

    @pl.when((member == 0) & is_last)
    def _():
        cots[beyond, :] = own_up_ref[after, lanes].astype(F32)

    @pl.when((member == 0) & jnp.logical_not(is_last))
    def _():
        cots[beyond, :] = down_ref[after, lanes].astype(F32)

    def convolved(table_ref, keep_ref, window, block):
        height = 128 if block < 2 else EDGE
        keep = keep_ref[member, block, pl.ds(0, height), :]
        result = jnp.zeros((height, TILE), F32)
        for group in range(PER_TILE):
            matrix = table_ref[first_group + group, pl.ds(0, height), :] * keep
            product = jnp.dot(matrix, window, preferred_element_type=F32)
            result = jnp.where(lane_group[:height] == group, product, result)
        return result

    for block in range(3):
        height = 128 if block < 2 else EDGE
        place = pl.ds(block * 128, height)
        medium = convolved(forward_ref, keep_f_ref, mixed_ref[member, pl.ds(block * 128, 256), lanes], block)
        medium = medium + skip * mixed_ref[member, pl.ds(block * 128 + 128, height), lanes].astype(F32)
        grad_conv = convolved(backward_ref, keep_b_ref, grads_ref[member, pl.ds(block * 128, 256), lanes], block)
        grad_conv = grad_conv + skip * grads_ref[member, place, lanes].astype(F32)
        for stream in range(3):
            if stream == 0:
                product = cots[place, :] * medium
            else:
                product = grad_conv * kv_ref[member, 2 - stream, place, lanes].astype(F32)
            stack[stream, place, :] = product.astype(BF16).astype(F32)

    @pl.when(member == 0)
    def _():
        sums_ref[...] = jnp.zeros(sums_ref.shape, F32)

    for stream in range(3):
        weights = taps_ref[stream, :, lanes]
        partial = [jnp.zeros((8, TILE), F32) for _ in range(TAPS)]
        for chunk in range(0, STRETCH, 64):
            source = feat_ref[stream, own(chunk, 64), lanes].astype(F32)
            total = jnp.zeros((64, TILE), F32)
            for lag in range(TAPS):
                later = stack[stream, pl.ds(chunk + lag, 64), :]
                if lag > 0:
                    later = later * shifted_ref[member, lag - 1, pl.ds(chunk, 64), :]
                total = total + later * weights[lag : lag + 1, :]
                partial[lag] = partial[lag] + jnp.sum((later * source).reshape(8, 8, TILE), axis=0)
            out_ref[stream, pl.ds(chunk, 64), :] = total.astype(BF16)
        for lag in range(TAPS):
            row = pl.ds(stream * 8 + lag, 1)
            sums_ref[row, :] += jnp.sum(partial[lag], axis=0, keepdims=True)
    bias = jnp.sum(
        grads_ref[member, pl.ds(0, STRETCH), lanes].astype(F32) * mixed_ref[member, pl.ds(128, STRETCH), lanes].astype(F32),
        axis=0, keepdims=True,
    )
    sums_ref[pl.ds(7, 1), :] += bias


def turn_kernel(scale, gathered_ref, out_ref):
    out_ref[...] = gathered_ref[...].T * scale


def along(block, axis, route):
    return lax.ppermute(block, axis, route)


def routes_z():
    return [
        [(i, i // 8 * 8 + 7 - i % 8) for i in range(32)],
        [(i, i ^ 1) for i in range(32)],
        [(i, i ^ 2) for i in range(32)],
    ]


def routes_x():
    return [[(i, (3 - i // 8) * 8 + i % 8) for i in range(32)], [(i, i ^ 8) for i in range(32)]]


def shards(features, short_filter, medium_filter, skip_bias, cotangent, doc_lengths):
    members = lax.axis_size("ctx")
    tp = lax.axis_index("tp")
    channels = features.shape[2]
    tiles = channels // TILE
    scale = 1.0 / math.sqrt(2 * STRETCH * members)
    streams = jnp.transpose(features, (1, 0, 2))
    weights = jnp.transpose(short_filter, (1, 0, 2))
    smem = pl.BlockSpec(memory_space=pltpu.SMEM)
    shape = jax.ShapeDtypeStruct
    params = pltpu.CompilerParams(vmem_limit_bytes=40 * 1024 * 1024)

    whole = pl.BlockSpec(memory_space=pltpu.VMEM)
    anywhere = pl.BlockSpec(memory_space=pl.ANY)
    pay_up, pay_down = pl.pallas_call(
        functools.partial(payload_kernel, members),
        in_specs=[smem, anywhere, anywhere, whole],
        out_specs=[whole, whole],
        out_shape=[shape((TAIL + HEAD, channels), BF16), shape((TAIL + HEAD, channels), BF16)],
        scratch_shapes=[
            pltpu.VMEM((tiles, 3, 2 * STRETCH, TILE), BF16),
            pltpu.VMEM((tiles, 2 * STRETCH, TILE), BF16),
            pltpu.VMEM((2, TAPS - 1, STRETCH, TILE), F32),
            pltpu.VMEM((STRETCH + 8, TILE), F32),
            pltpu.SemaphoreType.DMA((tiles,)),
            pltpu.SemaphoreType.DMA((tiles,)),
        ],
        compiler_params=pltpu.CompilerParams(vmem_limit_bytes=56 * 1024 * 1024),
        cost_estimate=pl.CostEstimate(flops=20_000_000, bytes_accessed=2_800_000, transcendentals=0),
        name="payload_rows",
    )(doc_lengths, streams, cotangent, weights)

    got_up = lax.ppermute(pay_up, "ctx", [(i, i + 1) for i in range(members - 1)])
    got_down = lax.ppermute(pay_down, "ctx", [(i + 1, i) for i in range(members - 1)])

    kvg = pl.pallas_call(
        functools.partial(own_kernel, members),
        grid=(tiles,),
        in_specs=[
            smem,
            pl.BlockSpec((3, 2 * STRETCH, TILE), lambda l: (0, 0, l)),
            pl.BlockSpec((2 * STRETCH, TILE), lambda l: (0, l)),
            pl.BlockSpec((3, TAPS, TILE), lambda l: (0, 0, l)),
        ],
        out_specs=pl.BlockSpec((3, 2 * STRETCH, TILE), lambda l: (0, 0, l)),
        out_shape=shape((3, 2 * STRETCH, channels), BF16),
        scratch_shapes=[
            pltpu.VMEM((2, TAPS - 1, STRETCH, TILE), F32),
            pltpu.VMEM((STRETCH + 8, TILE), F32),
        ],
        compiler_params=params,
        cost_estimate=pl.CostEstimate(flops=40_000_000, bytes_accessed=4_500_000, transcendentals=0),
        name="own_rows",
    )(doc_lengths, streams, cotangent, weights)

    groups = channels // GROUP
    tables = pl.pallas_call(
        functools.partial(tables_kernel, members),
        grid=(tiles,),
        in_specs=[smem, pl.BlockSpec(medium_filter.shape, lambda l: (0, 0))],
        out_specs=[
            pl.BlockSpec((PER_TILE, 128, 256), lambda l: (l, 0, 0)),
            pl.BlockSpec((PER_TILE, 128, 256), lambda l: (l, 0, 0)),
            pl.BlockSpec((2, 3, 128, 256), lambda l: (0, 0, 0, 0)),
            pl.BlockSpec((2, 3, 128, 256), lambda l: (0, 0, 0, 0)),
            pl.BlockSpec((2, 2, 128, 128), lambda l: (0, 0, 0, 0)),
            pl.BlockSpec((2, TAPS - 1, STRETCH, TILE), lambda l: (0, 0, 0, 0)),
            pl.BlockSpec((2, 2, TAPS - 1, EDGE, TILE), lambda l: (0, 0, 0, 0, 0)),
        ],
        out_shape=[
            shape((groups, 128, 256), BF16),
            shape((groups, 128, 256), BF16),
            shape((2, 3, 128, 256), BF16),
            shape((2, 3, 128, 256), BF16),
            shape((2, 2, 128, 128), F32),
            shape((2, TAPS - 1, STRETCH, TILE), F32),
            shape((2, 2, TAPS - 1, EDGE, TILE), F32),
        ],
        scratch_shapes=[
            pltpu.VMEM((256, 256), F32),
            pltpu.VMEM((256, 256), F32),
            pltpu.VMEM((384, TILE), F32),
        ],
        compiler_params=params,
        cost_estimate=pl.CostEstimate(flops=20_000_000, bytes_accessed=7_000_000, transcendentals=0),
        name="tables",
    )(doc_lengths, medium_filter)

    forward, backward, keep_f, keep_b, keep_r, shifted, edge = tables
    mixed, grads, kv, taps = pl.pallas_call(
        functools.partial(pair_kernel, members),
        grid=(tiles, 2),
        in_specs=[whole] * 9,
        out_specs=[whole] * 4,
        out_shape=[
            shape((2, 512, channels), BF16),
            shape((2, 512, channels), BF16),
            shape((2, 2, STRETCH + EDGE, channels), BF16),
            shape((groups, LAGS), F32),
        ],
        scratch_shapes=[
            pltpu.VMEM((TAIL, TILE), BF16),
            pltpu.VMEM((HEAD, TILE), BF16),
            pltpu.VMEM((2 * EDGE, TILE), F32),
        ],
        compiler_params=params,
        cost_estimate=pl.CostEstimate(flops=500_000_000, bytes_accessed=10_000_000, transcendentals=0),
        name="pair_rows",
    )(streams, kvg, cotangent, pay_up, got_up, got_down, weights, keep_r, edge)

    def convolve(first, count, mixed, grads, previous):
        return pl.pallas_call(
            functools.partial(conv_kernel, members, first),
            grid=(count, 2),
            in_specs=[whole] * 15 + [anywhere],
            out_specs=[
                pl.BlockSpec((3, STRETCH, TILE), lambda l, m: (0, m, first + l)),
                pl.BlockSpec((24, TILE), lambda l, m: (0, l)),
            ],
            out_shape=[
                shape((3, 2 * STRETCH, channels), BF16),
                shape((24, count * TILE), F32),
            ],
            input_output_aliases={15: 0} if first > 0 else {},
            scratch_shapes=[
                pltpu.VMEM((STRETCH + EDGE, TILE), F32),
                pltpu.VMEM((3, STRETCH + EDGE, TILE), F32),
            ],
            compiler_params=params,
            cost_estimate=pl.CostEstimate(flops=count * 100_000_000, bytes_accessed=count * 2_500_000, transcendentals=0),
            name=f"conv_rows_{first}",
        )(
            streams, mixed, grads, kv, cotangent, pay_up, got_up, got_down,
            weights, skip_bias.reshape(1, channels), forward, backward, keep_f, keep_b, shifted, previous,
        )

    parts = []
    grad_streams = kvg
    for route, (first, count) in zip(routes_x() + routes_z()[:1], ((0, 1), (1, 1), (2, 2))):
        other = along(taps, "ctx", route)
        grad_streams, part = convolve(first, count, mixed, grads, grad_streams)
        taps, mixed, grads, part = lax.optimization_barrier((taps + other, mixed, grads, part))
        parts.append(part)

    sums = jnp.concatenate(parts, axis=1)
    routes = routes_z()[1:] + routes_z()[:1] + routes_x()
    flip = 1
    for step, route in enumerate(routes):
        if step < 2:
            both = jnp.concatenate([sums, taps.reshape(8, channels)], axis=0)
            other = along(both, "ctx", route)
            both = both + other
            sums, taps = both[:24], both[24:].reshape(groups, LAGS)
        else:
            other = along(sums, "ctx", route)
            next_taps = along(taps, "tp", [(i, i ^ flip) for i in range(lax.axis_size("tp"))])
            upper = (tp // flip) % 2 == 1
            taps = jnp.concatenate(
                [jnp.where(upper, next_taps, taps), jnp.where(upper, taps, next_taps)], axis=0
            )
            sums = sums + other
            flip *= 2
        sums, taps = lax.optimization_barrier((sums, taps))
    grad_medium = pl.pallas_call(
        functools.partial(turn_kernel, scale),
        out_shape=shape(medium_filter.shape, F32),
        name="turn",
    )(taps)
    short = jnp.transpose(sums.reshape(3, 8, channels)[:, :TAPS], (1, 0, 2)) * scale
    return (jnp.transpose(grad_streams, (1, 0, 2)), short, grad_medium, sums[7] * scale)


def solution(mesh):
    in_specs = (P("ctx", None, "tp"), P(None, None, "tp"), P(), P("tp"), P("ctx", "tp"), P())
    out_specs = (P("ctx", None, "tp"), P(None, None, "tp"), P(), P("tp"))
    return jax.shard_map(shards, mesh=mesh, in_specs=in_specs, out_specs=out_specs, check_vma=False)
```

time: 103 us -> 85.6 us (0.83)
  waiting for transfers between devices: 33 us -> 22.7 us
  Pallas kernels: 41.4 us -> 33.1 us
  starting transfers between devices: 20.6 us -> 23.4 us
  local copies, waits for them, and re-layouts: 4.82 us -> 2.31 us
    pallas_call x1 -> x5, Pallas kernels: 33.1 us -> 24.9 us  [the longest x3 15 us: convolve(): pl.pallas_call(functools.partial(conv_kernel, members, first), grid=(coun...]
    ppermute x8 -> x11, waiting for transfers between devices: 24.7 us -> 19.4 us  [along(): return lax.ppermute(block, axis, route)]
    ppermute x1, waiting for transfers between devices: 3.34 us -> 0.01 us  [shards(): lax.ppermute(pay_up, 'ctx', [(i, i + 1) for i in range(members - 1)])]
    ppermute x8 -> x11, starting transfers between devices: 14.8 us -> 17.5 us  [along(): return lax.ppermute(block, axis, route)]
    unnamed x16 -> x19, local copies, waits for them, and re-layouts: 4.81 us -> 2.28 us
    ppermute x1, waiting for transfers between devices: 4.95 us -> 3.24 us  [shards(): lax.ppermute(pay_down, 'ctx', [(i + 1, i) for i in range(members - 1)])]
  transfers between devices with their start and end apart: 10 -> 13, of which waited for: 10 -> 7; matrix products, arithmetic and copies ran while one was open for 1% -> 0% of each run, Pallas kernels for 3% -> 25%
where the time goes in v1:
time: 85.6 us; the launch traced here: 84.3 us
  Pallas kernels  33.1 us (39%)
  starting transfers between devices  23.4 us (27%)
  waiting for transfers between devices  22.7 us (27%)
  local copies, waits for them, and re-layouts  2.31 us (3%)
  other arithmetic  1.97 us (2%)
  between operations  0.93 us (1%)
    ppermute x11, waiting for transfers between devices, along(): return lax.ppermute(block, axis, route)  19.4 us
    ppermute x11, starting transfers between devices, along(): return lax.ppermute(block, axis, route)  17.5 us
    pallas_call x3, Pallas kernels, convolve(): pl.pallas_call(functools.partial(conv_kernel, members, first), grid=(coun...  15 us
    pallas_call x1, Pallas kernels, shards(): pl.pallas_call(functools.partial(pair_kernel, members), grid=(tiles, 2),...  5.48 us
    pallas_call x1, Pallas kernels, shards(): pl.pallas_call(functools.partial(payload_kernel, members), in_specs=[smem...  4.43 us
    pallas_call x1, Pallas kernels, shards(): pl.pallas_call(functools.partial(own_kernel, members), grid=(tiles,), in_...  3.83 us
    ppermute x1, starting transfers between devices, shards(): lax.ppermute(pay_up, 'ctx', [(i, i + 1) for i in range(members - 1)])  3.83 us
    ppermute x1, waiting for transfers between devices, shards(): lax.ppermute(pay_down, 'ctx', [(i + 1, i) for i in range(members - 1)])  3.24 us
  transfers between devices with their start and end apart: 13, of which 7 were waited for; matrix products, arithmetic and copies ran while one was open for 0% of the time, Pallas kernels for 25%

profile of v1, /device:TPU:64, one launch (start us, length us, event | category | flops | bytes accessed | tf_op | source)
XLA Modules:
  0.0 84.3 jit_solution(9100309674600202497)
XLA Ops:
  0.6 0.0 copy-start
  0.6 0.0 copy-start.5
  0.7 0.0 copy-start.3
  0.7 0.0 copy-start.8
  0.7 4.4 %payload_rows.1 = (bf16[384,512]{1,0:T(8,128)(2,1)}, bf16[384,512]{1,0:T(8,128)(2,1)}) custom-call(s32[64]{0:T(128)} %lengths_ref.5, bf16[3,512,512]{2,1,0:T(8,128)(2,1)} %bitcast.8, bf16[512,512]{1,0:T(8,128)(2,1)} %cot_ref.9, f32[3,7,512]{2,1,0:T(8,128)} %bitcast.14), custom_call_target="tpu_custom_call" | custom-call | flops 20000000 | bytes 2800000 | tf_op jit(solution)/shard_map/payload_rows/pallas_call | solution.py:431
  5.1 3.8 %collective-permute-start = (bf16[384,512]{1,0:T(8,128)(2,1)}, bf16[384,512]{1,0:T(8,128)(2,1)S(1)}, u32[]{:S(2)}, u32[]{:S(2)}) collective-permute-start(bf16[384,512]{1,0:T(8,128)(2,1)} %get-tuple-element.43.own_up_ref), channel_id=1, source_target_pairs={{0,8},{8,16},{16,24},{24,32},{32,40},{40,48},{48,56},{56,64},{64,7... | collective-permute-start | bytes 1179656 | tf_op jit(solution)/shard_map/ppermute | solution.py:449
  8.9 2.0 %collective-permute-start.1 = (bf16[384,512]{1,0:T(8,128)(2,1)}, bf16[384,512]{1,0:T(8,128)(2,1)S(1)}, u32[]{:S(2)}, u32[]{:S(2)}) collective-permute-start(bf16[384,512]{1,0:T(8,128)(2,1)} %get-tuple-element.44), channel_id=1, source_target_pairs={{8,0},{16,8},{24,16},{32,24},{40,32},{48,40},{56,48},{64,56},{72,6... | collective-permute-start | bytes 1179656 | tf_op jit(solution)/shard_map/ppermute | solution.py:450
  11.0 0.0 copy-done.8
  11.0 0.0 copy-start.6
  11.0 0.9 %copy-done.6 = f32[128,256]{1,0:T(8,128)S(1)} copy-done((f32[128,256]{1,0:T(8,128)S(1)}, f32[128,256]{1,0:T(8,128)}, u32[]{:S(2)}) %copy-start.6) | copy-done | bytes 131096
  11.9 2.7 %tables.1 = (bf16[32,128,256]{2,1,0:T(8,128)(2,1)S(1)}, bf16[32,128,256]{2,1,0:T(8,128)(2,1)S(1)}, bf16[2,3,128,256]{3,2,1,0:T(8,128)(2,1)S(1)}, bf16[2,3,128,25...) custom-call(s32[64]{0:T(128)S(1)} %copy-done.8, ...), custom_call_target="tpu_custom_call" | custom-call | flops 20000000 | bytes 7000000 | tf_op jit(solution)/shard_map/tables/pallas_call | solution.py:473
  14.6 0.0 copy-start.1
  14.6 1.3 %copy-done.1 = bf16[32,128,256]{2,1,0:T(8,128)(2,1)} copy-done((bf16[32,128,256]{2,1,0:T(8,128)(2,1)}, bf16[32,128,256]{2,1,0:T(8,128)(2,1)S(1)}, u32[]{:S(2)}) %copy-start.1) | copy-done | bytes 2097176
  15.9 0.0 copy-done
  15.9 0.0 copy-done.5
  15.9 0.0 copy-done.3
  15.9 0.0 copy-start.4
  15.9 3.8 %own_rows.1.kvg_ref.previous_ref = bf16[3,512,512]{2,1,0:T(8,128)(2,1)S(1)} custom-call(s32[64]{0:T(128)S(1)} %copy-done.8, bf16[3,512,512]{2,1,0:T(8,128)(2,1)S(1)} %bitcast.9, bf16[512,512]{1,0:T(8,128)(2,1)S(1)} %copy-done.3, f32[3,7,512]{2,1,0:T(8,128)S(1)} %bitcast.15), custom_call_target="tpu_custom_call" | custom-call | flops 40000000 | bytes 4500000 | tf_op jit(solution)/shard_map/own_rows/pallas_call | solution.py:452
  19.8 0.0 collective-permute-done.up_ref
  19.8 3.2 %collective-permute-done.1.down_ref = bf16[384,512]{1,0:T(8,128)(2,1)S(1)} collective-permute-done((bf16[384,512]{1,0:T(8,128)(2,1)}, bf16[384,512]{1,0:T(8,128)(2,1)S(1)}, u32[]{:S(2)}, u32[]{:S(2)}) %collective-permute-start.1) | collective-permute-done | bytes 393248 | tf_op jit(solution)/shard_map/ppermute | solution.py:450
  23.0 0.0 copy-done.4
  23.0 0.0 copy-start.7
  23.0 5.5 %pair_rows.1 = (bf16[2,512,512]{2,1,0:T(8,128)(2,1)S(1)}, bf16[2,512,512]{2,1,0:T(8,128)(2,1)S(1)}, bf16[2,2,272,512]{3,2,1,0:T(8,128)(2,1)S(1)}, f32[32,128]{1,0:T(8,128)S(1)}) custom-call(bf16[3,512,512]{2,1,0:T(8,128)(2,1)S(1)} %bitcast.10, bf16[3,512,512]{2,1,0:T(8,128)(2,1)S(1)} %own_rows.1.kvg_ref.previous_ref, bf16[512,512]{1,0:T(8,128)(2,1)S(1)} %copy-done.3, ...), custom_call_target="tpu_custom_call" | custom-call | flops 500000000 | bytes 10000000 | tf_op jit(solution)/shard_map/pair_rows/pallas_call | solution.py:506
  28.5 2.8 %collective-permute-start.2 = (f32[32,128]{1,0:T(8,128)S(1)}, f32[32,128]{1,0:T(8,128)S(1)}, u32[]{:S(2)}, u32[]{:S(2)}) collective-permute-start(f32[32,128]{1,0:T(8,128)S(1)} %get-tuple-element.47), channel_id=1, source_target_pairs={{0,192},{8,200},{16,208},{24,216},{32,224},{40,232},{48,240},{56,2... | collective-permute-start | bytes 49160 | tf_op jit(solution)/shard_map/ppermute | solution.py:402
  31.4 0.0 copy-done.7
  31.4 0.0 copy-start.2
  31.4 5.2 %conv_rows_0.1 = (bf16[3,512,512]{2,1,0:T(8,128)(2,1)}, f32[24,128]{1,0:T(8,128)S(1)}) custom-call(bf16[3,512,512]{2,1,0:T(8,128)(2,1)S(1)} %bitcast.11, bf16[2,512,512]{2,1,0:T(8,128)(2,1)S(1)} %get-tuple-element.62.mixed_ref, bf16[2,512,512]{2,1,0:T(8,128)(2,1)S(1)} %get-tuple-element.63.grads_ref, bf16[2,2,272,512]{3,2,1,0:T(8,128)(2,1)S(1)} %get-tuple-element.50.kv_ref, ...), custom_call_target="tpu_custom_call" | custom-call | flops 100000000 | bytes 2500000 | tf_op jit(solution)/shard_map/conv_rows_0/pallas_call | solution.py:528
  36.5 0.0 collective-permute-done.2
  36.6 0.3 collective-permute-start.3
  36.9 0.0 copy-done.2
  36.9 3.5 %conv_rows_1.1 = (bf16[3,512,512]{2,1,0:T(8,128)(2,1)}, f32[24,128]{1,0:T(8,128)S(1)}) custom-call(bf16[3,512,512]{2,1,0:T(8,128)(2,1)S(1)} %bitcast.12, bf16[2,512,512]{2,1,0:T(8,128)(2,1)S(1)} %get-tuple-element.62.mixed_ref, bf16[2,512,512]{2,1,0:T(8,128)(2,1)S(1)} %get-tuple-element.63.grads_ref, ...), custom_call_target="tpu_custom_call", output_to_operand_aliasing={{0}: (15, {})} | custom-call | flops 100000000 | bytes 2500000 | tf_op jit(solution)/shard_map/conv_rows_1/pallas_call | solution.py:528
  40.3 0.0 collective-permute-done.3
  40.4 2.7 %collective-permute-start.4 = (f32[32,128]{1,0:T(8,128)S(1)}, f32[32,128]{1,0:T(8,128)S(1)}, u32[]{:S(2)}, u32[]{:S(2)}) collective-permute-start(f32[32,128]{1,0:T(8,128)S(1)} %add.38), channel_id=1, source_target_pairs={{0,56},{8,48},{16,40},{24,32},{32,24},{40,16},{48,8},{56,0},{64,12... | collective-permute-start | bytes 49160 | tf_op jit(solution)/shard_map/ppermute | solution.py:402
  43.1 6.3 %conv_rows_2.1 = (bf16[3,512,512]{2,1,0:T(8,128)(2,1)}, f32[24,256]{1,0:T(8,128)S(1)}) custom-call(bf16[3,512,512]{2,1,0:T(8,128)(2,1)S(1)} %bitcast.13, bf16[2,512,512]{2,1,0:T(8,128)(2,1)S(1)} %get-tuple-element.62.mixed_ref, bf16[2,512,512]{2,1,0:T(8,128)(2,1)S(1)} %get-tuple-element.63.grads_ref, ...), custom_call_target="tpu_custom_call", output_to_operand_aliasing={{0}: (15, {})} | custom-call | flops 200000000 | bytes 5000000 | tf_op jit(solution)/shard_map/conv_rows_2/pallas_call | solution.py:528
  49.4 0.0 collective-permute-done.4
  49.5 0.5 collective-permute-start.5
  50.0 3.8 %collective-permute-done.5 = f32[32,512]{1,0:T(8,128)S(1)} collective-permute-done((f32[32,512]{1,0:T(8,128)S(1)}, f32[32,512]{1,0:T(8,128)S(1)}, u32[]{:S(2)}, u32[]{:S(2)}) %collective-permute-start.5) | collective-permute-done | bytes 65568 | tf_op jit(solution)/shard_map/ppermute | solution.py:402
  53.9 2.2 %collective-permute-start.6 = (f32[32,512]{1,0:T(8,128)S(1)}, f32[32,512]{1,0:T(8,128)S(1)}, u32[]{:S(2)}, u32[]{:S(2)}) collective-permute-start(f32[32,512]{1,0:T(8,128)S(1)} %constant_dynamic-update-slice_fusion), channel_id=1, source_target_pairs={{0,16},{8,24},{16,0},{24,8},{32,48},{40,56},{48,32},{56,40},{64,80... | collective-permute-start | bytes 196616 | tf_op jit(solution)/shard_map/ppermute | solution.py:402
  56.1 3.2 %collective-permute-done.6 = f32[32,512]{1,0:T(8,128)S(1)} collective-permute-done((f32[32,512]{1,0:T(8,128)S(1)}, f32[32,512]{1,0:T(8,128)S(1)}, u32[]{:S(2)}, u32[]{:S(2)}) %collective-permute-start.6) | collective-permute-done | bytes 65568 | tf_op jit(solution)/shard_map/ppermute | solution.py:402
  59.4 0.1 collective-permute-start.8
  59.5 2.5 %collective-permute-start.7 = (f32[24,512]{1,0:T(8,128)S(1)}, f32[24,512]{1,0:T(8,128)S(1)}, u32[]{:S(2)}, u32[]{:S(2)}) collective-permute-start(f32[24,512]{1,0:T(8,128)S(1)} %slice.26), channel_id=1, source_target_pairs={{0,56},{8,48},{16,40},{24,32},{32,24},{40,16},{48,8},{56,0},{64,12... | collective-permute-start | bytes 147464 | tf_op jit(solution)/shard_map/ppermute | solution.py:402
  62.0 0.0 collective-permute-done.8
  62.0 4.7 %collective-permute-done.7 = f32[24,512]{1,0:T(8,128)S(1)} collective-permute-done((f32[24,512]{1,0:T(8,128)S(1)}, f32[24,512]{1,0:T(8,128)S(1)}, u32[]{:S(2)}, u32[]{:S(2)}) %collective-permute-start.7) | collective-permute-done | bytes 49184 | tf_op jit(solution)/shard_map/ppermute | solution.py:402
  66.7 1.7 %collective-permute-start.10 = (f32[64,128]{1,0:T(8,128)S(1)}, f32[64,128]{1,0:T(8,128)S(1)}, u32[]{:S(2)}, u32[]{:S(2)}) collective-permute-start(f32[64,128]{1,0:T(8,128)S(1)} %pad_maximum_fusion.3), channel_id=1, source_target_pairs={{0,2},{1,3},{2,0},{3,1},{4,6},{5,7},{6,4},{7,5},{8,10},{9,11},{10,... | collective-permute-start | bytes 98312 | tf_op jit(solution)/shard_map/ppermute | solution.py:402
  68.4 1.1 %collective-permute-start.9 = (f32[24,512]{1,0:T(8,128)S(1)}, f32[24,512]{1,0:T(8,128)S(1)}, u32[]{:S(2)}, u32[]{:S(2)}) collective-permute-start(f32[24,512]{1,0:T(8,128)S(1)} %add.42), channel_id=1, source_target_pairs={{0,192},{8,200},{16,208},{24,216},{32,224},{40,232},{48,240},{56,2... | collective-permute-start | bytes 147464 | tf_op jit(solution)/shard_map/ppermute | solution.py:402
  69.5 1.2 %collective-permute-done.10 = f32[64,128]{1,0:T(8,128)S(1)} collective-permute-done((f32[64,128]{1,0:T(8,128)S(1)}, f32[64,128]{1,0:T(8,128)S(1)}, u32[]{:S(2)}, u32[]{:S(2)}) %collective-permute-start.10) | collective-permute-done | bytes 32800 | tf_op jit(solution)/shard_map/ppermute | solution.py:402
  70.7 2.9 %collective-permute-done.9 = f32[24,512]{1,0:T(8,128)S(1)} collective-permute-done((f32[24,512]{1,0:T(8,128)S(1)}, f32[24,512]{1,0:T(8,128)S(1)}, u32[]{:S(2)}, u32[]{:S(2)}) %collective-permute-start.9) | collective-permute-done | bytes 49184 | tf_op jit(solution)/shard_map/ppermute | solution.py:402
  73.7 3.0 %collective-permute-start.12 = (f32[128,128]{1,0:T(8,128)S(1)}, f32[128,128]{1,0:T(8,128)S(1)}, u32[]{:S(2)}, u32[]{:S(2)}) collective-permute-start(f32[128,128]{1,0:T(8,128)S(1)} %pad_maximum_fusion.2), channel_id=1, source_target_pairs={{0,4},{1,5},{2,6},{3,7},{4,0},{5,1},{6,2},{7,3},{8,12},{9,13},{10,... | collective-permute-start | bytes 196616 | tf_op jit(solution)/shard_map/ppermute | solution.py:402
  76.7 0.6 collective-permute-start.11
  77.3 3.5 %collective-permute-done.11 = f32[24,512]{1,0:T(8,128)S(1)} collective-permute-done((f32[24,512]{1,0:T(8,128)S(1)}, f32[24,512]{1,0:T(8,128)S(1)}, u32[]{:S(2)}, u32[]{:S(2)}) %collective-permute-start.11) | collective-permute-done | bytes 49184 | tf_op jit(solution)/shard_map/ppermute | solution.py:402
  80.8 0.0 collective-permute-done.12
  80.8 0.7 pad_maximum_fusion.gathered_ref
  81.5 1.7 %turn.1 = f32[128,256]{1,0:T(8,128)} custom-call(f32[256,128]{1,0:T(8,128)} %pad_maximum_fusion.gathered_ref), custom_call_target="tpu_custom_call" | custom-call | tf_op jit(solution)/shard_map/turn/pallas_call | solution.py:580
  83.1 0.6 slice_multiply_fusion.1
  83.7 0.6 fusion
  (24 shorter events, 0.1 us)
Async XLA Ops:
  0.6 15.3 %copy-start = (bf16[512,3,512]{2,0,1:T(8,128)(2,1)S(1)}, bf16[512,3,512]{2,0,1:T(8,128)(2,1)}, u32[]{:S(2)}) copy-start(bf16[512,3,512]{2,0,1:T(8,128)(2,1)} %param.6) | copy-start | bytes 4718596
  0.6 15.3 %copy-start.5 = (f32[7,3,512]{2,0,1:T(8,128)S(1)}, f32[7,3,512]{2,0,1:T(8,128)}, u32[]{:S(2)}) copy-start(f32[7,3,512]{2,0,1:T(8,128)} %param.7) | copy-start | bytes 129028
  0.7 15.3 %copy-start.3 = (bf16[512,512]{1,0:T(8,128)(2,1)S(1)}, bf16[512,512]{1,0:T(8,128)(2,1)}, u32[]{:S(2)}) copy-start(bf16[512,512]{1,0:T(8,128)(2,1)} %cot_ref.9) | copy-start | bytes 1572868
  0.7 10.3 %copy-start.8 = (s32[64]{0:T(128)S(1)}, s32[64]{0:T(128)}, u32[]{:S(2)}) copy-start(s32[64]{0:T(128)} %lengths_ref.5) | copy-start | bytes 772
  5.1 14.7 %collective-permute-start = (bf16[384,512]{1,0:T(8,128)(2,1)}, bf16[384,512]{1,0:T(8,128)(2,1)S(1)}, u32[]{:S(2)}, u32[]{:S(2)}) collective-permute-start(bf16[384,512]{1,0:T(8,128)(2,1)} %get-tuple-element.43.own_up_ref), channel_id=1, source_target_pairs={{0,8},{8,16},{16,24},{24,32},{32,40},{40,48},{48,56},{56,64},{64,7... | collective-permute-start | bytes 1179656 | tf_op jit(solution)/shard_map/ppermute | solution.py:449
  8.9 14.1 %collective-permute-start.1 = (bf16[384,512]{1,0:T(8,128)(2,1)}, bf16[384,512]{1,0:T(8,128)(2,1)S(1)}, u32[]{:S(2)}, u32[]{:S(2)}) collective-permute-start(bf16[384,512]{1,0:T(8,128)(2,1)} %get-tuple-element.44), channel_id=1, source_target_pairs={{8,0},{16,8},{24,16},{32,24},{40,32},{48,40},{56,48},{64,56},{72,6... | collective-permute-start | bytes 1179656 | tf_op jit(solution)/shard_map/ppermute | solution.py:450
  11.0 0.9 %copy-start.6 = (f32[128,256]{1,0:T(8,128)S(1)}, f32[128,256]{1,0:T(8,128)}, u32[]{:S(2)}) copy-start(f32[128,256]{1,0:T(8,128)} %medium_ref.1) | copy-start | bytes 393220
  14.6 1.4 %copy-start.1 = (bf16[32,128,256]{2,1,0:T(8,128)(2,1)}, bf16[32,128,256]{2,1,0:T(8,128)(2,1)S(1)}, u32[]{:S(2)}) copy-start(bf16[32,128,256]{2,1,0:T(8,128)(2,1)S(1)} %get-tuple-element.52.backward_ref) | copy-start | bytes 6291460
  15.9 7.1 %copy-start.4 = (bf16[384,512]{1,0:T(8,128)(2,1)S(1)}, bf16[384,512]{1,0:T(8,128)(2,1)}, u32[]{:S(2)}) copy-start(bf16[384,512]{1,0:T(8,128)(2,1)} %get-tuple-element.43.own_up_ref) | copy-start | bytes 1179652
  23.0 8.3 %copy-start.7 = (f32[512]{0:T(512)S(1)}, f32[512]{0:T(512)}, u32[]{:S(2)}) copy-start(f32[512]{0:T(512)} %param.9) | copy-start | bytes 6148
  28.5 8.0 %collective-permute-start.2 = (f32[32,128]{1,0:T(8,128)S(1)}, f32[32,128]{1,0:T(8,128)S(1)}, u32[]{:S(2)}, u32[]{:S(2)}) collective-permute-start(f32[32,128]{1,0:T(8,128)S(1)} %get-tuple-element.47), channel_id=1, source_target_pairs={{0,192},{8,200},{16,208},{24,216},{32,224},{40,232},{48,240},{56,2... | collective-permute-start | bytes 49160 | tf_op jit(solution)/shard_map/ppermute | solution.py:402
  31.4 5.5 %copy-start.2 = (bf16[32,128,256]{2,1,0:T(8,128)(2,1)S(1)}, bf16[32,128,256]{2,1,0:T(8,128)(2,1)}, u32[]{:S(2)}) copy-start(bf16[32,128,256]{2,1,0:T(8,128)(2,1)} %copy-done.1) | copy-start | bytes 6291460
  36.6 3.8 %collective-permute-start.3 = (f32[32,128]{1,0:T(8,128)S(1)}, f32[32,128]{1,0:T(8,128)S(1)}, u32[]{:S(2)}, u32[]{:S(2)}) collective-permute-start(f32[32,128]{1,0:T(8,128)S(1)} %add.37), channel_id=1, source_target_pairs={{0,64},{8,72},{16,80},{24,88},{32,96},{40,104},{48,112},{56,120},{... | collective-permute-start | bytes 49160 | tf_op jit(solution)/shard_map/ppermute | solution.py:402
  40.4 9.1 %collective-permute-start.4 = (f32[32,128]{1,0:T(8,128)S(1)}, f32[32,128]{1,0:T(8,128)S(1)}, u32[]{:S(2)}, u32[]{:S(2)}) collective-permute-start(f32[32,128]{1,0:T(8,128)S(1)} %add.38), channel_id=1, source_target_pairs={{0,56},{8,48},{16,40},{24,32},{32,24},{40,16},{48,8},{56,0},{64,12... | collective-permute-start | bytes 49160 | tf_op jit(solution)/shard_map/ppermute | solution.py:402
  49.5 4.4 %collective-permute-start.5 = (f32[32,512]{1,0:T(8,128)S(1)}, f32[32,512]{1,0:T(8,128)S(1)}, u32[]{:S(2)}, u32[]{:S(2)}) collective-permute-start(f32[32,512]{1,0:T(8,128)S(1)} %pad_maximum_fusion.1), channel_id=1, source_target_pairs={{0,8},{8,0},{16,24},{24,16},{32,40},{40,32},{48,56},{56,48},{64,72... | collective-permute-start | bytes 196616 | tf_op jit(solution)/shard_map/ppermute | solution.py:402
  53.9 5.4 %collective-permute-start.6 = (f32[32,512]{1,0:T(8,128)S(1)}, f32[32,512]{1,0:T(8,128)S(1)}, u32[]{:S(2)}, u32[]{:S(2)}) collective-permute-start(f32[32,512]{1,0:T(8,128)S(1)} %constant_dynamic-update-slice_fusion), channel_id=1, source_target_pairs={{0,16},{8,24},{16,0},{24,8},{32,48},{40,56},{48,32},{56,40},{64,80... | collective-permute-start | bytes 196616 | tf_op jit(solution)/shard_map/ppermute | solution.py:402
  59.4 2.6 %collective-permute-start.8 = (f32[32,128]{1,0:T(8,128)S(1)}, f32[32,128]{1,0:T(8,128)S(1)}, u32[]{:S(2)}, u32[]{:S(2)}) collective-permute-start(f32[32,128]{1,0:T(8,128)S(1)} %reshape.34), channel_id=1, source_target_pairs={{0,1},{1,0},{2,3},{3,2},{4,5},{5,4},{6,7},{7,6},{8,9},{9,8},{10,11... | collective-permute-start | bytes 49160 | tf_op jit(solution)/shard_map/ppermute | solution.py:402
  59.5 7.2 %collective-permute-start.7 = (f32[24,512]{1,0:T(8,128)S(1)}, f32[24,512]{1,0:T(8,128)S(1)}, u32[]{:S(2)}, u32[]{:S(2)}) collective-permute-start(f32[24,512]{1,0:T(8,128)S(1)} %slice.26), channel_id=1, source_target_pairs={{0,56},{8,48},{16,40},{24,32},{32,24},{40,16},{48,8},{56,0},{64,12... | collective-permute-start | bytes 147464 | tf_op jit(solution)/shard_map/ppermute | solution.py:402
  66.7 4.0 %collective-permute-start.10 = (f32[64,128]{1,0:T(8,128)S(1)}, f32[64,128]{1,0:T(8,128)S(1)}, u32[]{:S(2)}, u32[]{:S(2)}) collective-permute-start(f32[64,128]{1,0:T(8,128)S(1)} %pad_maximum_fusion.3), channel_id=1, source_target_pairs={{0,2},{1,3},{2,0},{3,1},{4,6},{5,7},{6,4},{7,5},{8,10},{9,11},{10,... | collective-permute-start | bytes 98312 | tf_op jit(solution)/shard_map/ppermute | solution.py:402
  68.4 5.3 %collective-permute-start.9 = (f32[24,512]{1,0:T(8,128)S(1)}, f32[24,512]{1,0:T(8,128)S(1)}, u32[]{:S(2)}, u32[]{:S(2)}) collective-permute-start(f32[24,512]{1,0:T(8,128)S(1)} %add.42), channel_id=1, source_target_pairs={{0,192},{8,200},{16,208},{24,216},{32,224},{40,232},{48,240},{56,2... | collective-permute-start | bytes 147464 | tf_op jit(solution)/shard_map/ppermute | solution.py:402
  73.7 7.1 %collective-permute-start.12 = (f32[128,128]{1,0:T(8,128)S(1)}, f32[128,128]{1,0:T(8,128)S(1)}, u32[]{:S(2)}, u32[]{:S(2)}) collective-permute-start(f32[128,128]{1,0:T(8,128)S(1)} %pad_maximum_fusion.2), channel_id=1, source_target_pairs={{0,4},{1,5},{2,6},{3,7},{4,0},{5,1},{6,2},{7,3},{8,12},{9,13},{10,... | collective-permute-start | bytes 196616 | tf_op jit(solution)/shard_map/ppermute | solution.py:402
  76.7 4.1 %collective-permute-start.11 = (f32[24,512]{1,0:T(8,128)S(1)}, f32[24,512]{1,0:T(8,128)S(1)}, u32[]{:S(2)}, u32[]{:S(2)}) collective-permute-start(f32[24,512]{1,0:T(8,128)S(1)} %add.44), channel_id=1, source_target_pairs={{0,64},{8,72},{16,80},{24,88},{32,96},{40,104},{48,112},{56,120},{... | collective-permute-start | bytes 147464 | tf_op jit(solution)/shard_map/ppermute | solution.py:402

commit v2 on v1

--- a/solution.py
+++ b/solution.py
@@ -140,15 +140,18 @@
 def tables_kernel(
     members, lengths_ref, medium_ref,
     forward_ref, backward_ref, keep_f_ref, keep_b_ref, keep_r_ref, shifted_ref, edge_ref,
-    forward_rows, backward_rows, offsets,
+    forward_rows, backward_rows, offsets, medium, medium_sem,
 ):
     device = lax.axis_index("ctx")
 
     @pl.when(pl.program_id(0) == 0)
     def _():
+        copy = pltpu.make_async_copy(medium_ref, medium, medium_sem)
+        copy.start()
         lag = lax.broadcasted_iota(jnp.int32, (LAGS, 256), 0)
         lane = lax.broadcasted_iota(jnp.int32, (LAGS, 256), 1)
-        taps = medium_ref[...].astype(BF16)
+        copy.wait()
+        taps = medium[...].astype(BF16)
         dims = (((0,), (0,)), ((), ()))
         place_f = jnp.where(lane == LAGS - lag, 1.0, 0.0).astype(BF16)
         place_b = jnp.where(lane == lag, 1.0, 0.0).astype(BF16)
@@ -394,8 +397,24 @@
     sums_ref[pl.ds(7, 1), :] += bias
 
 
-def turn_kernel(scale, gathered_ref, out_ref):
-    out_ref[...] = gathered_ref[...].T * scale
+def final_kernel(scale, flip, taps_ref, next_taps_ref, sums_ref, other_ref, medium_ref, short_ref, bias_ref):
+    half = taps_ref.shape[0]
+    upper = (lax.axis_index("tp") // flip) % 2 == 1
+
+    @pl.when(upper)
+    def _():
+        medium_ref[:, pl.ds(half, half)] = taps_ref[...].T * scale
+        medium_ref[:, pl.ds(0, half)] = next_taps_ref[...].T * scale
+
+    @pl.when(jnp.logical_not(upper))
+    def _():
+        medium_ref[:, pl.ds(0, half)] = taps_ref[...].T * scale
+        medium_ref[:, pl.ds(half, half)] = next_taps_ref[...].T * scale
+
+    total = (sums_ref[...] + other_ref[...]) * scale
+    for stream in range(3):
+        short_ref[stream] = total[stream * 8 : stream * 8 + TAPS]
+    bias_ref[...] = total[TAPS : TAPS + 1]
 
 
 def along(block, axis, route):
@@ -424,7 +443,7 @@
     weights = jnp.transpose(short_filter, (1, 0, 2))
     smem = pl.BlockSpec(memory_space=pltpu.SMEM)
     shape = jax.ShapeDtypeStruct
-    params = pltpu.CompilerParams(vmem_limit_bytes=40 * 1024 * 1024)
+    params = pltpu.CompilerParams(vmem_limit_bytes=16 * 1024 * 1024)
 
     whole = pl.BlockSpec(memory_space=pltpu.VMEM)
     anywhere = pl.BlockSpec(memory_space=pl.ANY)
@@ -473,7 +492,7 @@
     tables = pl.pallas_call(
         functools.partial(tables_kernel, members),
         grid=(tiles,),
-        in_specs=[smem, pl.BlockSpec(medium_filter.shape, lambda l: (0, 0))],
+        in_specs=[smem, anywhere],
         out_specs=[
             pl.BlockSpec((PER_TILE, 128, 256), lambda l: (l, 0, 0)),
             pl.BlockSpec((PER_TILE, 128, 256), lambda l: (l, 0, 0)),
@@ -496,6 +515,8 @@
             pltpu.VMEM((256, 256), F32),
             pltpu.VMEM((256, 256), F32),
             pltpu.VMEM((384, TILE), F32),
+            pltpu.VMEM(medium_filter.shape, F32),
+            pltpu.SemaphoreType.DMA,
         ],
         compiler_params=params,
         cost_estimate=pl.CostEstimate(flops=20_000_000, bytes_accessed=7_000_000, transcendentals=0),
@@ -552,14 +573,14 @@
 
     parts = []
     grad_streams = kvg
-    for route, (first, count) in zip(routes_x() + routes_z()[:1], ((0, 1), (1, 1), (2, 2))):
+    for route, (first, count) in zip(routes_x() + routes_z()[1:2], ((0, 1), (1, 1), (2, 2))):
         other = along(taps, "ctx", route)
         grad_streams, part = convolve(first, count, mixed, grads, grad_streams)
         taps, mixed, grads, part = lax.optimization_barrier((taps + other, mixed, grads, part))
         parts.append(part)
 
     sums = jnp.concatenate(parts, axis=1)
-    routes = routes_z()[1:] + routes_z()[:1] + routes_x()
+    routes = routes_z()[2:] + routes_z()[:2] + routes_x()
     flip = 1
     for step, route in enumerate(routes):
         if step < 2:
@@ -570,20 +591,27 @@
         else:
             other = along(sums, "ctx", route)
             next_taps = along(taps, "tp", [(i, i ^ flip) for i in range(lax.axis_size("tp"))])
-            upper = (tp // flip) % 2 == 1
-            taps = jnp.concatenate(
-                [jnp.where(upper, next_taps, taps), jnp.where(upper, taps, next_taps)], axis=0
-            )
-            sums = sums + other
-            flip *= 2
+            if step < len(routes) - 1:
+                upper = (tp // flip) % 2 == 1
+                taps = jnp.concatenate(
+                    [jnp.where(upper, next_taps, taps), jnp.where(upper, taps, next_taps)], axis=0
+                )
+                sums = sums + other
+                flip *= 2
         sums, taps = lax.optimization_barrier((sums, taps))
-    grad_medium = pl.pallas_call(
-        functools.partial(turn_kernel, scale),
-        out_shape=shape(medium_filter.shape, F32),
-        name="turn",
-    )(taps)
-    short = jnp.transpose(sums.reshape(3, 8, channels)[:, :TAPS], (1, 0, 2)) * scale
-    return (jnp.transpose(grad_streams, (1, 0, 2)), short, grad_medium, sums[7] * scale)
+    grad_medium, short, bias = pl.pallas_call(
+        functools.partial(final_kernel, scale, flip),
+        in_specs=[whole] * 4,
+        out_shape=[
+            shape(medium_filter.shape, F32), shape((3, TAPS, channels), F32), shape((1, channels), F32),
+        ],
+        compiler_params=params,
+        name="final",
+    )(taps, next_taps, sums, other)
+    return (
+        jnp.transpose(grad_streams, (1, 0, 2)), jnp.transpose(short, (1, 0, 2)), grad_medium,
+        bias.reshape(channels),
+    )
 
 
 def solution(mesh):

time: 85.6 us -> 80.7 us (0.943); the launches traced: 84.3 us -> 80.5 us
  waiting for transfers between devices: 22.7 us -> 27.6 us
  starting transfers between devices: 23.4 us -> 19.8 us
  Pallas kernels: 33.1 us -> 31.1 us
  other arithmetic: 1.97 us -> 0.09 us
  local copies, waits for them, and re-layouts: 2.31 us -> 0.97 us
    ppermute x11, waiting for transfers between devices: 19.4 us -> 23.3 us  [along(): return lax.ppermute(block, axis, route)]
    ppermute x11, starting transfers between devices: 17.5 us -> 13.9 us  [along(): return lax.ppermute(block, axis, route)]
    unnamed x19 -> x15, local copies, waits for them, and re-layouts: 2.28 us -> 0.93 us
    pallas_call x3, Pallas kernels: 15 us -> 13.7 us  [convolve(): pl.pallas_call(functools.partial(conv_kernel, members, first), grid=(coun...]
    mul x2 -> x0, other arithmetic: 1.21 us -> none  [the longest x1 0.62 us: shards(): jnp.transpose(sums.reshape(3, 8, channels)[:, :TAPS], (1, 0, 2)) * scale]
    ppermute x1, waiting for transfers between devices: 3.24 us -> 4.32 us  [shards(): lax.ppermute(pay_down, 'ctx', [(i + 1, i) for i in range(members - 1)])]
    pallas_call x1, Pallas kernels: 1.66 us -> 0.77 us  [shards(): pl.pallas_call(functools.partial(final_kernel, scale, flip), in_specs=[wh...]
  transfers between devices with their start and end apart: 13 -> 13, of which waited for: 7 -> 8; matrix products, arithmetic and copies ran while one was open for 0% -> 0% of each run, Pallas kernels for 25% -> 25%
where the time goes in v2:
time: 80.7 us; the launch traced here: 80.5 us
  Pallas kernels  31.1 us (39%)
  waiting for transfers between devices  27.6 us (34%)
  starting transfers between devices  19.8 us (25%)
  local copies, waits for them, and re-layouts  0.97 us (1%)
  between operations  0.94 us (1%)
    ppermute x11, waiting for transfers between devices, along(): return lax.ppermute(block, axis, route)  23.3 us
    ppermute x11, starting transfers between devices, along(): return lax.ppermute(block, axis, route)  13.9 us
    pallas_call x3, Pallas kernels, convolve(): pl.pallas_call(functools.partial(conv_kernel, members, first), grid=(coun...  13.7 us
    pallas_call x1, Pallas kernels, shards(): pl.pallas_call(functools.partial(pair_kernel, members), grid=(tiles, 2),...  5.42 us
    pallas_call x1, Pallas kernels, shards(): pl.pallas_call(functools.partial(payload_kernel, members), in_specs=[smem...  4.44 us
    ppermute x1, waiting for transfers between devices, shards(): lax.ppermute(pay_down, 'ctx', [(i + 1, i) for i in range(members - 1)])  4.32 us
    pallas_call x1, Pallas kernels, shards(): pl.pallas_call(functools.partial(own_kernel, members), grid=(tiles,), in_...  3.83 us
    ppermute x1, starting transfers between devices, shards(): lax.ppermute(pay_up, 'ctx', [(i, i + 1) for i in range(members - 1)])  3.83 us
  transfers between devices with their start and end apart: 13, of which 8 were waited for; matrix products, arithmetic and copies ran while one was open for 0% of the time, Pallas kernels for 25%

profile of v2, /device:TPU:64, one launch (start us, length us, event | category | flops | bytes accessed | tf_op | source)
XLA Modules:
  0.0 80.5 jit_solution(16608427419336767837)
XLA Ops:
  0.6 0.0 copy-start
  0.6 0.0 copy-start.3
  0.7 0.0 copy-start.1
  0.7 0.0 copy-start.6
  0.7 4.4 %payload_rows.1 = (bf16[384,512]{1,0:T(8,128)(2,1)}, bf16[384,512]{1,0:T(8,128)(2,1)}) custom-call(s32[64]{0:T(128)} %lengths_ref.5, bf16[3,512,512]{2,1,0:T(8,128)(2,1)} %bitcast.6, bf16[512,512]{1,0:T(8,128)(2,1)} %cot_ref.9, f32[3,7,512]{2,1,0:T(8,128)} %bitcast.12), custom_call_target="tpu_custom_call" | custom-call | flops 20000000 | bytes 2800000 | tf_op jit(solution)/shard_map/payload_rows/pallas_call | solution.py:450
  5.1 3.8 %collective-permute-start = (bf16[384,512]{1,0:T(8,128)(2,1)}, bf16[384,512]{1,0:T(8,128)(2,1)S(1)}, u32[]{:S(2)}, u32[]{:S(2)}) collective-permute-start(bf16[384,512]{1,0:T(8,128)(2,1)} %get-tuple-element.46.own_up_ref), channel_id=1, source_target_pairs={{0,8},{8,16},{16,24},{24,32},{32,40},{40,48},{48,56},{56,64},{64,7... | collective-permute-start | bytes 1179656 | tf_op jit(solution)/shard_map/ppermute | solution.py:468
  9.0 2.0 %collective-permute-start.1 = (bf16[384,512]{1,0:T(8,128)(2,1)}, bf16[384,512]{1,0:T(8,128)(2,1)S(1)}, u32[]{:S(2)}, u32[]{:S(2)}) collective-permute-start(bf16[384,512]{1,0:T(8,128)(2,1)} %get-tuple-element.47), channel_id=1, source_target_pairs={{8,0},{16,8},{24,16},{32,24},{40,32},{48,40},{56,48},{64,56},{72,6... | collective-permute-start | bytes 1179656 | tf_op jit(solution)/shard_map/ppermute | solution.py:469
  11.0 0.0 copy-done.6
  11.0 0.0 copy-start.4
  11.0 0.9 %copy-done.4 = f32[128,256]{1,0:T(8,128)S(1)} copy-done((f32[128,256]{1,0:T(8,128)S(1)}, f32[128,256]{1,0:T(8,128)}, u32[]{:S(2)}) %copy-start.4) | copy-done | bytes 131096
  11.9 2.9 %tables.1 = (bf16[32,128,256]{2,1,0:T(8,128)(2,1)S(1)}, bf16[32,128,256]{2,1,0:T(8,128)(2,1)S(1)}, bf16[2,3,128,256]{3,2,1,0:T(8,128)(2,1)S(1)}, bf16[2,3,128,25...) custom-call(s32[64]{0:T(128)S(1)} %copy-done.6, ...), custom_call_target="tpu_custom_call" | custom-call | flops 20000000 | bytes 7000000 | tf_op jit(solution)/shard_map/tables/pallas_call | solution.py:492
  14.8 0.0 copy-done
  14.8 0.0 copy-done.3
  14.8 0.0 copy-done.1
  14.8 0.0 copy-start.2
  14.9 3.8 %own_rows.1.kvg_ref.previous_ref = bf16[3,512,512]{2,1,0:T(8,128)(2,1)S(1)} custom-call(s32[64]{0:T(128)S(1)} %copy-done.6, bf16[3,512,512]{2,1,0:T(8,128)(2,1)S(1)} %bitcast.7, bf16[512,512]{1,0:T(8,128)(2,1)S(1)} %copy-done.1, f32[3,7,512]{2,1,0:T(8,128)S(1)} %bitcast.13), custom_call_target="tpu_custom_call" | custom-call | flops 40000000 | bytes 4500000 | tf_op jit(solution)/shard_map/own_rows/pallas_call | solution.py:471
  18.7 0.0 collective-permute-done.up_ref
  18.7 4.3 %collective-permute-done.1.down_ref = bf16[384,512]{1,0:T(8,128)(2,1)S(1)} collective-permute-done((bf16[384,512]{1,0:T(8,128)(2,1)}, bf16[384,512]{1,0:T(8,128)(2,1)S(1)}, u32[]{:S(2)}, u32[]{:S(2)}) %collective-permute-start.1) | collective-permute-done | bytes 393248 | tf_op jit(solution)/shard_map/ppermute | solution.py:469
  23.0 0.0 copy-done.2
  23.0 0.0 copy-start.5
  23.0 5.4 %pair_rows.1 = (bf16[2,512,512]{2,1,0:T(8,128)(2,1)S(1)}, bf16[2,512,512]{2,1,0:T(8,128)(2,1)S(1)}, bf16[2,2,272,512]{3,2,1,0:T(8,128)(2,1)S(1)}, f32[32,128]{1,0:T(8,128)S(1)}) custom-call(bf16[3,512,512]{2,1,0:T(8,128)(2,1)S(1)} %bitcast.8, bf16[3,512,512]{2,1,0:T(8,128)(2,1)S(1)} %own_rows.1.kvg_ref.previous_ref, bf16[512,512]{1,0:T(8,128)(2,1)S(1)} %copy-done.1, ...), custom_call_target="tpu_custom_call" | custom-call | flops 500000000 | bytes 10000000 | tf_op jit(solution)/shard_map/pair_rows/pallas_call | solution.py:527
  28.5 2.8 %collective-permute-start.2 = (f32[32,128]{1,0:T(8,128)S(1)}, f32[32,128]{1,0:T(8,128)S(1)}, u32[]{:S(2)}, u32[]{:S(2)}) collective-permute-start(f32[32,128]{1,0:T(8,128)S(1)} %get-tuple-element.50), channel_id=1, source_target_pairs={{0,192},{8,200},{16,208},{24,216},{32,224},{40,232},{48,240},{56,2... | collective-permute-start | bytes 49160 | tf_op jit(solution)/shard_map/ppermute | solution.py:421
  31.3 0.0 copy-done.5
  31.3 3.6 %conv_rows_0.1 = (bf16[3,512,512]{2,1,0:T(8,128)(2,1)}, f32[24,128]{1,0:T(8,128)S(1)}) custom-call(bf16[3,512,512]{2,1,0:T(8,128)(2,1)S(1)} %bitcast.9, bf16[2,512,512]{2,1,0:T(8,128)(2,1)S(1)} %get-tuple-element.65.mixed_ref, bf16[2,512,512]{2,1,0:T(8,128)(2,1)S(1)} %get-tuple-element.66.grads_ref, bf16[2,2,272,512]{3,2,1,0:T(8,128)(2,1)S(1)} %get-tuple-element.53.kv_ref, ...), custom_call_target="tpu_custom_call" | custom-call | flops 100000000 | bytes 2500000 | tf_op jit(solution)/shard_map/conv_rows_0/pallas_call | solution.py:549
  34.9 0.0 collective-permute-done.2
  34.9 0.3 collective-permute-start.3
  35.2 3.6 %conv_rows_1.1 = (bf16[3,512,512]{2,1,0:T(8,128)(2,1)}, f32[24,128]{1,0:T(8,128)S(1)}) custom-call(bf16[3,512,512]{2,1,0:T(8,128)(2,1)S(1)} %bitcast.10, bf16[2,512,512]{2,1,0:T(8,128)(2,1)S(1)} %get-tuple-element.65.mixed_ref, bf16[2,512,512]{2,1,0:T(8,128)(2,1)S(1)} %get-tuple-element.66.grads_ref, ...), custom_call_target="tpu_custom_call", output_to_operand_aliasing={{0}: (15, {})} | custom-call | flops 100000000 | bytes 2500000 | tf_op jit(solution)/shard_map/conv_rows_1/pallas_call | solution.py:549
  38.8 0.0 collective-permute-done.3
  38.8 3.0 %collective-permute-start.4 = (f32[32,128]{1,0:T(8,128)S(1)}, f32[32,128]{1,0:T(8,128)S(1)}, u32[]{:S(2)}, u32[]{:S(2)}) collective-permute-start(f32[32,128]{1,0:T(8,128)S(1)} %add.31), channel_id=1, source_target_pairs={{0,8},{8,0},{16,24},{24,16},{32,40},{40,32},{48,56},{56,48},{64,72... | collective-permute-start | bytes 49160 | tf_op jit(solution)/shard_map/ppermute | solution.py:421
  41.8 6.6 %conv_rows_2.1 = (bf16[3,512,512]{2,1,0:T(8,128)(2,1)}, f32[24,256]{1,0:T(8,128)S(1)}) custom-call(bf16[3,512,512]{2,1,0:T(8,128)(2,1)S(1)} %bitcast.11, bf16[2,512,512]{2,1,0:T(8,128)(2,1)S(1)} %get-tuple-element.65.mixed_ref, bf16[2,512,512]{2,1,0:T(8,128)(2,1)S(1)} %get-tuple-element.66.grads_ref, ...), custom_call_target="tpu_custom_call", output_to_operand_aliasing={{0}: (15, {})} | custom-call | flops 200000000 | bytes 5000000 | tf_op jit(solution)/shard_map/conv_rows_2/pallas_call | solution.py:549
  48.4 0.0 collective-permute-done.4
  48.4 0.1 collective-permute-start.5
  48.5 5.2 %collective-permute-done.5 = f32[32,512]{1,0:T(8,128)S(1)} collective-permute-done((f32[32,512]{1,0:T(8,128)S(1)}, f32[32,512]{1,0:T(8,128)S(1)}, u32[]{:S(2)}, u32[]{:S(2)}) %collective-permute-start.5) | collective-permute-done | bytes 65568 | tf_op jit(solution)/shard_map/ppermute | solution.py:421
  53.8 0.9 %collective-permute-start.6 = (f32[32,512]{1,0:T(8,128)S(1)}, f32[32,512]{1,0:T(8,128)S(1)}, u32[]{:S(2)}, u32[]{:S(2)}) collective-permute-start(f32[32,512]{1,0:T(8,128)S(1)} %constant_dynamic-update-slice_fusion), channel_id=1, source_target_pairs={{0,56},{8,48},{16,40},{24,32},{32,24},{40,16},{48,8},{56,0},{64,12... | collective-permute-start | bytes 196616 | tf_op jit(solution)/shard_map/ppermute | solution.py:421
  54.6 6.5 %collective-permute-done.6 = f32[32,512]{1,0:T(8,128)S(1)} collective-permute-done((f32[32,512]{1,0:T(8,128)S(1)}, f32[32,512]{1,0:T(8,128)S(1)}, u32[]{:S(2)}, u32[]{:S(2)}) %collective-permute-start.6) | collective-permute-done | bytes 65568 | tf_op jit(solution)/shard_map/ppermute | solution.py:421
  61.2 0.3 collective-permute-start.8
  61.5 0.1 collective-permute-start.7
  61.6 1.1 %collective-permute-done.8 = f32[32,128]{1,0:T(8,128)S(1)} collective-permute-done((f32[32,128]{1,0:T(8,128)S(1)}, f32[32,128]{1,0:T(8,128)S(1)}, u32[]{:S(2)}, u32[]{:S(2)}) %collective-permute-start.8) | collective-permute-done | bytes 16416 | tf_op jit(solution)/shard_map/ppermute | solution.py:421
  62.6 3.0 %collective-permute-done.7 = f32[24,512]{1,0:T(8,128)S(1)} collective-permute-done((f32[24,512]{1,0:T(8,128)S(1)}, f32[24,512]{1,0:T(8,128)S(1)}, u32[]{:S(2)}, u32[]{:S(2)}) %collective-permute-start.7) | collective-permute-done | bytes 49184 | tf_op jit(solution)/shard_map/ppermute | solution.py:421
  65.6 1.7 %collective-permute-start.10 = (f32[64,128]{1,0:T(8,128)S(1)}, f32[64,128]{1,0:T(8,128)S(1)}, u32[]{:S(2)}, u32[]{:S(2)}) collective-permute-start(f32[64,128]{1,0:T(8,128)S(1)} %pad_maximum_fusion.2), channel_id=1, source_target_pairs={{0,2},{1,3},{2,0},{3,1},{4,6},{5,7},{6,4},{7,5},{8,10},{9,11},{10,... | collective-permute-start | bytes 98312 | tf_op jit(solution)/shard_map/ppermute | solution.py:421
  67.3 1.2 %collective-permute-start.9 = (f32[24,512]{1,0:T(8,128)S(1)}, f32[24,512]{1,0:T(8,128)S(1)}, u32[]{:S(2)}, u32[]{:S(2)}) collective-permute-start(f32[24,512]{1,0:T(8,128)S(1)} %add.35), channel_id=1, source_target_pairs={{0,192},{8,200},{16,208},{24,216},{32,224},{40,232},{48,240},{56,2... | collective-permute-start | bytes 147464 | tf_op jit(solution)/shard_map/ppermute | solution.py:421
  68.5 1.2 %collective-permute-done.10 = f32[64,128]{1,0:T(8,128)S(1)} collective-permute-done((f32[64,128]{1,0:T(8,128)S(1)}, f32[64,128]{1,0:T(8,128)S(1)}, u32[]{:S(2)}, u32[]{:S(2)}) %collective-permute-start.10) | collective-permute-done | bytes 32800 | tf_op jit(solution)/shard_map/ppermute | solution.py:421
  69.7 2.9 %collective-permute-done.9 = f32[24,512]{1,0:T(8,128)S(1)} collective-permute-done((f32[24,512]{1,0:T(8,128)S(1)}, f32[24,512]{1,0:T(8,128)S(1)}, u32[]{:S(2)}, u32[]{:S(2)}) %collective-permute-start.9) | collective-permute-done | bytes 49184 | tf_op jit(solution)/shard_map/ppermute | solution.py:421
  72.6 3.0 %collective-permute-start.11 = (f32[128,128]{1,0:T(8,128)S(1)}, f32[128,128]{1,0:T(8,128)S(1)}, u32[]{:S(2)}, u32[]{:S(2)}) collective-permute-start(f32[128,128]{1,0:T(8,128)S(1)} %pad_maximum_fusion.1.taps_ref), channel_id=1, source_target_pairs={{0,4},{1,5},{2,6},{3,7},{4,0},{5,1},{6,2},{7,3},{8,12},{9,13},{10,... | collective-permute-start | bytes 196616 | tf_op jit(solution)/shard_map/ppermute | solution.py:421
  75.6 0.6 collective-permute-start.12
  76.2 3.5 %collective-permute-done.12.other_ref = f32[24,512]{1,0:T(8,128)S(1)} collective-permute-done((f32[24,512]{1,0:T(8,128)S(1)}, f32[24,512]{1,0:T(8,128)S(1)}, u32[]{:S(2)}, u32[]{:S(2)}) %collective-permute-start.12) | collective-permute-done | bytes 49184 | tf_op jit(solution)/shard_map/ppermute | solution.py:421
  79.7 0.0 collective-permute-done.11.next_taps_ref
  79.7 0.8 final.1
  (22 shorter events, 0.1 us)
Async XLA Ops:
  0.6 14.2 %copy-start = (bf16[512,3,512]{2,0,1:T(8,128)(2,1)S(1)}, bf16[512,3,512]{2,0,1:T(8,128)(2,1)}, u32[]{:S(2)}) copy-start(bf16[512,3,512]{2,0,1:T(8,128)(2,1)} %param.6) | copy-start | bytes 4718596
  0.6 14.2 %copy-start.3 = (f32[7,3,512]{2,0,1:T(8,128)S(1)}, f32[7,3,512]{2,0,1:T(8,128)}, u32[]{:S(2)}) copy-start(f32[7,3,512]{2,0,1:T(8,128)} %param.7) | copy-start | bytes 129028
  0.7 14.2 %copy-start.1 = (bf16[512,512]{1,0:T(8,128)(2,1)S(1)}, bf16[512,512]{1,0:T(8,128)(2,1)}, u32[]{:S(2)}) copy-start(bf16[512,512]{1,0:T(8,128)(2,1)} %cot_ref.9) | copy-start | bytes 1572868
  0.7 10.3 %copy-start.6 = (s32[64]{0:T(128)S(1)}, s32[64]{0:T(128)}, u32[]{:S(2)}) copy-start(s32[64]{0:T(128)} %lengths_ref.5) | copy-start | bytes 772
  5.1 13.6 %collective-permute-start = (bf16[384,512]{1,0:T(8,128)(2,1)}, bf16[384,512]{1,0:T(8,128)(2,1)S(1)}, u32[]{:S(2)}, u32[]{:S(2)}) collective-permute-start(bf16[384,512]{1,0:T(8,128)(2,1)} %get-tuple-element.46.own_up_ref), channel_id=1, source_target_pairs={{0,8},{8,16},{16,24},{24,32},{32,40},{40,48},{48,56},{56,64},{64,7... | collective-permute-start | bytes 1179656 | tf_op jit(solution)/shard_map/ppermute | solution.py:468
  9.0 14.1 %collective-permute-start.1 = (bf16[384,512]{1,0:T(8,128)(2,1)}, bf16[384,512]{1,0:T(8,128)(2,1)S(1)}, u32[]{:S(2)}, u32[]{:S(2)}) collective-permute-start(bf16[384,512]{1,0:T(8,128)(2,1)} %get-tuple-element.47), channel_id=1, source_target_pairs={{8,0},{16,8},{24,16},{32,24},{40,32},{48,40},{56,48},{64,56},{72,6... | collective-permute-start | bytes 1179656 | tf_op jit(solution)/shard_map/ppermute | solution.py:469
  11.0 0.9 %copy-start.4 = (f32[128,256]{1,0:T(8,128)S(1)}, f32[128,256]{1,0:T(8,128)}, u32[]{:S(2)}) copy-start(f32[128,256]{1,0:T(8,128)} %medium_ref.1) | copy-start | bytes 393220
  14.8 8.2 %copy-start.2 = (bf16[384,512]{1,0:T(8,128)(2,1)S(1)}, bf16[384,512]{1,0:T(8,128)(2,1)}, u32[]{:S(2)}) copy-start(bf16[384,512]{1,0:T(8,128)(2,1)} %get-tuple-element.46.own_up_ref) | copy-start | bytes 1179652
  23.0 8.3 %copy-start.5 = (f32[512]{0:T(512)S(1)}, f32[512]{0:T(512)}, u32[]{:S(2)}) copy-start(f32[512]{0:T(512)} %param.9) | copy-start | bytes 6148
  28.5 6.4 %collective-permute-start.2 = (f32[32,128]{1,0:T(8,128)S(1)}, f32[32,128]{1,0:T(8,128)S(1)}, u32[]{:S(2)}, u32[]{:S(2)}) collective-permute-start(f32[32,128]{1,0:T(8,128)S(1)} %get-tuple-element.50), channel_id=1, source_target_pairs={{0,192},{8,200},{16,208},{24,216},{32,224},{40,232},{48,240},{56,2... | collective-permute-start | bytes 49160 | tf_op jit(solution)/shard_map/ppermute | solution.py:421
  34.9 3.9 %collective-permute-start.3 = (f32[32,128]{1,0:T(8,128)S(1)}, f32[32,128]{1,0:T(8,128)S(1)}, u32[]{:S(2)}, u32[]{:S(2)}) collective-permute-start(f32[32,128]{1,0:T(8,128)S(1)} %add.30), channel_id=1, source_target_pairs={{0,64},{8,72},{16,80},{24,88},{32,96},{40,104},{48,112},{56,120},{... | collective-permute-start | bytes 49160 | tf_op jit(solution)/shard_map/ppermute | solution.py:421
  38.8 9.6 %collective-permute-start.4 = (f32[32,128]{1,0:T(8,128)S(1)}, f32[32,128]{1,0:T(8,128)S(1)}, u32[]{:S(2)}, u32[]{:S(2)}) collective-permute-start(f32[32,128]{1,0:T(8,128)S(1)} %add.31), channel_id=1, source_target_pairs={{0,8},{8,0},{16,24},{24,16},{32,40},{40,32},{48,56},{56,48},{64,72... | collective-permute-start | bytes 49160 | tf_op jit(solution)/shard_map/ppermute | solution.py:421
  48.4 5.3 %collective-permute-start.5 = (f32[32,512]{1,0:T(8,128)S(1)}, f32[32,512]{1,0:T(8,128)S(1)}, u32[]{:S(2)}, u32[]{:S(2)}) collective-permute-start(f32[32,512]{1,0:T(8,128)S(1)} %pad_maximum_fusion), channel_id=1, source_target_pairs={{0,16},{8,24},{16,0},{24,8},{32,48},{40,56},{48,32},{56,40},{64,80... | collective-permute-start | bytes 196616 | tf_op jit(solution)/shard_map/ppermute | solution.py:421
  53.8 7.4 %collective-permute-start.6 = (f32[32,512]{1,0:T(8,128)S(1)}, f32[32,512]{1,0:T(8,128)S(1)}, u32[]{:S(2)}, u32[]{:S(2)}) collective-permute-start(f32[32,512]{1,0:T(8,128)S(1)} %constant_dynamic-update-slice_fusion), channel_id=1, source_target_pairs={{0,56},{8,48},{16,40},{24,32},{32,24},{40,16},{48,8},{56,0},{64,12... | collective-permute-start | bytes 196616 | tf_op jit(solution)/shard_map/ppermute | solution.py:421
  61.2 1.5 %collective-permute-start.8 = (f32[32,128]{1,0:T(8,128)S(1)}, f32[32,128]{1,0:T(8,128)S(1)}, u32[]{:S(2)}, u32[]{:S(2)}) collective-permute-start(f32[32,128]{1,0:T(8,128)S(1)} %reshape.32), channel_id=1, source_target_pairs={{0,1},{1,0},{2,3},{3,2},{4,5},{5,4},{6,7},{7,6},{8,9},{9,8},{10,11... | collective-permute-start | bytes 49160 | tf_op jit(solution)/shard_map/ppermute | solution.py:421
  61.5 4.2 %collective-permute-start.7 = (f32[24,512]{1,0:T(8,128)S(1)}, f32[24,512]{1,0:T(8,128)S(1)}, u32[]{:S(2)}, u32[]{:S(2)}) collective-permute-start(f32[24,512]{1,0:T(8,128)S(1)} %slice.18), channel_id=1, source_target_pairs={{0,8},{8,0},{16,24},{24,16},{32,40},{40,32},{48,56},{56,48},{64,72... | collective-permute-start | bytes 147464 | tf_op jit(solution)/shard_map/ppermute | solution.py:421
  65.6 4.0 %collective-permute-start.10 = (f32[64,128]{1,0:T(8,128)S(1)}, f32[64,128]{1,0:T(8,128)S(1)}, u32[]{:S(2)}, u32[]{:S(2)}) collective-permute-start(f32[64,128]{1,0:T(8,128)S(1)} %pad_maximum_fusion.2), channel_id=1, source_target_pairs={{0,2},{1,3},{2,0},{3,1},{4,6},{5,7},{6,4},{7,5},{8,10},{9,11},{10,... | collective-permute-start | bytes 98312 | tf_op jit(solution)/shard_map/ppermute | solution.py:421
  67.3 5.3 %collective-permute-start.9 = (f32[24,512]{1,0:T(8,128)S(1)}, f32[24,512]{1,0:T(8,128)S(1)}, u32[]{:S(2)}, u32[]{:S(2)}) collective-permute-start(f32[24,512]{1,0:T(8,128)S(1)} %add.35), channel_id=1, source_target_pairs={{0,192},{8,200},{16,208},{24,216},{32,224},{40,232},{48,240},{56,2... | collective-permute-start | bytes 147464 | tf_op jit(solution)/shard_map/ppermute | solution.py:421
  72.6 7.1 %collective-permute-start.11 = (f32[128,128]{1,0:T(8,128)S(1)}, f32[128,128]{1,0:T(8,128)S(1)}, u32[]{:S(2)}, u32[]{:S(2)}) collective-permute-start(f32[128,128]{1,0:T(8,128)S(1)} %pad_maximum_fusion.1.taps_ref), channel_id=1, source_target_pairs={{0,4},{1,5},{2,6},{3,7},{4,0},{5,1},{6,2},{7,3},{8,12},{9,13},{10,... | collective-permute-start | bytes 196616 | tf_op jit(solution)/shard_map/ppermute | solution.py:421
  75.6 4.1 %collective-permute-start.12 = (f32[24,512]{1,0:T(8,128)S(1)}, f32[24,512]{1,0:T(8,128)S(1)}, u32[]{:S(2)}, u32[]{:S(2)}) collective-permute-start(f32[24,512]{1,0:T(8,128)S(1)} %add.37.sums_ref), channel_id=1, source_target_pairs={{0,64},{8,72},{16,80},{24,88},{32,96},{40,104},{48,112},{56,120},{... | collective-permute-start | bytes 147464 | tf_op jit(solution)/shard_map/ppermute | solution.py:421

commit v3 on v2

--- a/solution.py
+++ b/solution.py
@@ -15,8 +15,10 @@
 LAGS = 128
 TAPS = 7
 EDGE = 16
-TAIL = 128 + 3 * EDGE
-HEAD = 144 + 4 * EDGE
+TAIL = 128 + 2 * EDGE
+HEAD = 128 + 2 * EDGE
+REACH = TAPS - 1
+NEAR = 8
 DOCS = 64
 F32 = jnp.float32
 BF16 = jnp.bfloat16
@@ -31,14 +33,13 @@
 
 
 def lane_starts(lengths_ref, base, count):
-    position = (base + lax.broadcasted_iota(jnp.int32, (8, count), 1)).astype(F32)
-    found = jnp.zeros((8, count), F32)
+    position = base + lax.broadcasted_iota(jnp.int32, (8, count), 1)
+    found = jnp.zeros((8, count), jnp.int32)
     running = jnp.int32(0)
     for doc in range(DOCS):
-        here = running.astype(F32)
-        found = jnp.where(position >= here, here, found)
+        found = jnp.where(position >= running, running, found)
         running = running + lengths_ref[doc]
-    return found
+    return found.astype(F32)
 
 
 def row_starts(starts, block):
@@ -69,36 +70,66 @@
 
 
 def payload_kernel(
-    members, lengths_ref, feat_hbm, cot_hbm, taps_ref, up_ref, down_ref, feat, cots, masks, rows, feat_sem, cot_sem,
+    members, lengths_hbm, feat_hbm, cot_hbm, taps_hbm, up_hbm, down_hbm,
+    lengths_ref, taps_ref, up_ref, down_ref, feat, cots, masks, rows, grads, sems,
 ):
-    tiles = feat.shape[0]
     copies = []
-    for tile in range(tiles):
-        lanes = pl.ds(tile * TILE, TILE)
-        copies.append((
-            pltpu.make_async_copy(feat_hbm.at[:, :, lanes], feat.at[tile], feat_sem.at[tile]),
-            pltpu.make_async_copy(cot_hbm.at[:, lanes], cots.at[tile], cot_sem.at[tile]),
-        ))
-        copies[-1][0].start()
-        copies[-1][1].start()
+
+    def fetch(source, target):
+        copies.append(pltpu.make_async_copy(source, target, sems.at[len(copies)]))
+        copies[-1].start()
+        return copies[-1]
+
+    def fetch_rows(stream, first, count):
+        place = pl.ds(first, count)
+        return fetch(feat_hbm.at[stream, place, :], feat.at[stream, place, :])
+
+    fetch(lengths_hbm, lengths_ref)
+    fetch(taps_hbm, taps_ref)
+    needed = {}
+    for member in range(2):
+        first = member * STRETCH
+        head = pl.ds(first, 144)
+        needed[member, "head"] = [fetch_rows(0, first, 144), fetch(cot_hbm.at[head, :], cots.at[head, :])]
+    for member in range(2):
+        first = member * STRETCH
+        needed[member, "tail"] = [fetch_rows(stream, first + 112, 144) for stream in (1, 2)]
+    edges = []
+    for member in range(2):
+        first = member * STRETCH
+        edges.append(fetch_rows(0, first + STRETCH - EDGE, EDGE))
+        edges += [fetch_rows(stream, first, EDGE) for stream in (1, 2)]
+
+    copies[0].wait()
     own_masks(members, lengths_ref, masks)
+    copies[1].wait()
     rows[pl.ds(0, 8), :] = jnp.zeros((8, TILE), F32)
-    for tile in range(tiles):
-        lanes = pl.ds(tile * TILE, TILE)
-        copies[tile][0].wait()
-        copies[tile][1].wait()
-        for member in range(2):
-            first = member * STRETCH
-            tail_ref = up_ref if member == 0 else down_ref
-            head_ref = down_ref if member == 0 else up_ref
-            rows[pl.ds(8, 144), :] = feat[tile, 0, pl.ds(first, 144), :].astype(F32)
+    tiles = [pl.ds(tile * TILE, TILE) for tile in range(up_ref.shape[1] // TILE)]
+    for member in range(2):
+        head_ref = down_ref if member == 0 else up_ref
+        first = member * STRETCH
+        for copy in needed[member, "head"]:
+            copy.wait()
+        for lanes in tiles:
+            rows[pl.ds(8, 144), :] = feat[0, pl.ds(first, 144), lanes].astype(F32)
             weights = taps_ref[0, :, lanes]
             for chunk in range(0, 144, 48):
                 query = conv_rows(rows, weights, masks, member, chunk, 48).astype(F32)
-                cot = cots[tile, pl.ds(first + chunk, 48), :].astype(F32)
-                head_ref[pl.ds(TAIL + chunk, 48), lanes] = (cot * query).astype(BF16)
+                cot = cots[pl.ds(first + chunk, 48), lanes].astype(F32)
+                grads[pl.ds(chunk, 48), :] = cot * query
+            head_ref[pl.ds(TAIL, 128), lanes] = grads[pl.ds(REACH, 128), :].astype(BF16)
+    sent = []
+    big = pl.ds(TAIL, 128)
+    for source, target in ((up_ref, up_hbm), (down_ref, down_hbm)):
+        sent.append(fetch(source.at[big, :], target.at[big, :]))
+    for member in range(2):
+        tail_ref = up_ref if member == 0 else down_ref
+        first = member * STRETCH
+        for copy in needed[member, "tail"]:
+            copy.wait()
+        for lanes in tiles:
             for stream in (1, 2):
-                rows[pl.ds(8 + 112, 144), :] = feat[tile, stream, pl.ds(first + 112, 144), :].astype(F32)
+                rows[pl.ds(8 + 112, 144), :] = feat[stream, pl.ds(first + 112, 144), lanes].astype(F32)
                 weights = taps_ref[stream, :, lanes]
                 for chunk in range(0, 128, 64):
                     part = conv_rows(rows, weights, masks, member, 128 + chunk, 64)
@@ -106,14 +137,26 @@
                     if stream == 2:
                         part = (tail_ref[place, lanes].astype(F32) * part.astype(F32)).astype(BF16)
                     tail_ref[place, lanes] = part
-            for stream in range(3):
-                tail_ref[pl.ds(128 + stream * EDGE, EDGE), lanes] = feat[
-                    tile, stream, pl.ds(first + STRETCH - EDGE, EDGE), :
-                ]
-                head_ref[pl.ds(TAIL + 144 + stream * EDGE, EDGE), lanes] = feat[
-                    tile, stream, pl.ds(first, EDGE), :
-                ]
-            head_ref[pl.ds(TAIL + 144 + 3 * EDGE, EDGE), lanes] = cots[tile, pl.ds(first, EDGE), :]
+    for copy in edges:
+        copy.wait()
+    for member in range(2):
+        tail_ref = up_ref if member == 0 else down_ref
+        head_ref = down_ref if member == 0 else up_ref
+        first = member * STRETCH
+        last = [feat[stream, pl.ds(first + STRETCH - EDGE, EDGE), :].astype(F32)[NEAR:] for stream in range(3)]
+        ahead = [feat[stream, pl.ds(first, EDGE), :].astype(F32)[:NEAR] for stream in range(3)]
+        ahead.append(cots[pl.ds(first, EDGE), :].astype(F32)[:NEAR])
+        for pair in range(2):
+            place = 128 + pair * EDGE
+            two = jnp.concatenate([last[2 * pair], last[min(2 * pair + 1, 2)]], axis=0)
+            tail_ref[pl.ds(place, EDGE), :] = two.astype(BF16)
+            two = jnp.concatenate([ahead[2 * pair], ahead[2 * pair + 1]], axis=0)
+            head_ref[pl.ds(TAIL + place, EDGE), :] = two.astype(BF16)
+    for source, target in ((up_ref, up_hbm), (down_ref, down_hbm)):
+        for part in (pl.ds(0, TAIL), pl.ds(TAIL + 128, 2 * EDGE)):
+            sent.append(fetch(source.at[part, :], target.at[part, :]))
+    for copy in sent:
+        copy.wait()
 
 
 def own_kernel(members, lengths_ref, feat_ref, cot_ref, taps_ref, kvg_ref, masks, rows):
@@ -197,9 +240,9 @@
 
 
 def edge_conv(rows, weights, edge_ref, side):
-    total = rows[pl.ds(EDGE, EDGE), :] * weights[0:1, :]
+    total = rows[pl.ds(NEAR, EDGE), :] * weights[0:1, :]
     for lag in range(1, TAPS):
-        moved = rows[pl.ds(EDGE - lag, EDGE), :] * weights[lag : lag + 1, :]
+        moved = rows[pl.ds(NEAR - lag, EDGE), :] * weights[lag : lag + 1, :]
         total = total + moved * edge_ref[side, lag - 1]
     return total.astype(BF16).astype(F32)
 
@@ -207,7 +250,7 @@
 def pair_kernel(
     members, feat_ref, kvg_ref, cot_ref, own_up_ref, up_ref, down_ref, taps_ref, keep_r_ref, edge_ref,
     mixed_ref, grads_ref, kv_ref, sums_ref,
-    left, right, rows,
+    left, right, rows, beyond,
 ):
     member = pl.program_id(1)
     tile = pl.program_id(0)
@@ -247,21 +290,27 @@
     for side in range(2):
         place = pl.ds(side * STRETCH, EDGE)
         if side == 0:
-            cot = cot_ref[own(0, EDGE), lanes]
+            cot = cot_ref[own(0, EDGE), lanes].astype(F32)
         else:
-            cot = right[pl.ds(144 + 3 * EDGE, EDGE), :]
+            cot = right[pl.ds(144, EDGE), :].astype(F32)[NEAR:]
         fixed = []
         for stream in range(3):
+            place_two, half = pl.ds(128 + stream // 2 * EDGE, EDGE), stream % 2 * NEAR
             if side == 0:
-                before = left[pl.ds(128 + stream * EDGE, EDGE), :]
-                after = feat_ref[stream, own(0, EDGE), lanes]
+                rows[pl.ds(0, NEAR), :] = left[place_two, :].astype(F32)[half : half + NEAR]
+                rows[pl.ds(NEAR, EDGE), :] = feat_ref[stream, own(0, EDGE), lanes].astype(F32)
             else:
-                before = feat_ref[stream, own(STRETCH - EDGE, EDGE), lanes]
-                after = right[pl.ds(144 + stream * EDGE, EDGE), :]
-            rows[pl.ds(0, EDGE), :] = before.astype(F32)
-            rows[pl.ds(EDGE, EDGE), :] = after.astype(F32)
+                rows[pl.ds(0, NEAR), :] = feat_ref[stream, own(STRETCH - EDGE, EDGE), lanes].astype(F32)[NEAR:]
+                rows[pl.ds(NEAR, NEAR), :] = right[place_two, :].astype(F32)[half : half + NEAR]
+                rows[pl.ds(EDGE, NEAR), :] = jnp.zeros((NEAR, TILE), F32)
             fixed.append(edge_conv(rows, taps_ref[stream, :, lanes], edge_ref.at[member], side))
-        grads_ref[member, place, lanes] = (cot.astype(F32) * fixed[0]).astype(BF16)
+        if side == 0:
+            grads_ref[member, place, lanes] = (cot * fixed[0]).astype(BF16)
+        else:
+            beyond[pl.ds(0, NEAR), :] = cot * fixed[0][:NEAR]
+            beyond[pl.ds(REACH, 128), :] = right[pl.ds(0, 128), :].astype(F32)
+            beyond[pl.ds(REACH + 128, 144 - REACH - 128), :] = jnp.zeros((144 - REACH - 128, TILE), F32)
+            grads_ref[member, pl.ds(STRETCH, 144), lanes] = beyond[...].astype(BF16)
         kv_ref[member, 0, place, lanes] = fixed[1].astype(BF16)
         kv_ref[member, 1, place, lanes] = fixed[2].astype(BF16)
         mixed_ref[member, pl.ds(128 + side * STRETCH, EDGE), lanes] = (fixed[1] * fixed[2]).astype(BF16)
@@ -273,7 +322,6 @@
     mixed_ref[member, pl.ds(128 + EDGE, STRETCH - EDGE), lanes] = (keys.astype(F32) * values.astype(F32)).astype(BF16)
     mixed_ref[member, pl.ds(400, 112), lanes] = jnp.zeros((112, TILE), BF16)
     grads_ref[member, inner, lanes] = kvg_ref[2, own(EDGE, STRETCH - EDGE), lanes]
-    grads_ref[member, pl.ds(STRETCH + EDGE, 128), lanes] = right[pl.ds(EDGE, 128), :]
     grads_ref[member, pl.ds(400, 112), lanes] = jnp.zeros((112, TILE), BF16)
 
     @pl.when(member == 1)
@@ -330,30 +378,31 @@
     first_group = tile * PER_TILE
     lane_group = lax.broadcasted_iota(jnp.int32, (128, TILE), 1) // GROUP
     skip = skip_ref[:, lanes]
-    after = pl.ds(TAIL + 144 + 3 * EDGE, EDGE)
-    beyond = pl.ds(STRETCH, EDGE)
+    after = pl.ds(TAIL + 144, EDGE)
+    beyond = pl.ds(STRETCH, NEAR)
+    cots[pl.ds(STRETCH + NEAR, NEAR), :] = jnp.zeros((NEAR, TILE), F32)
     cots[pl.ds(0, STRETCH), :] = cot_ref[own(0, STRETCH), lanes].astype(F32)
 
     @pl.when(member == 1)
     def _():
-        cots[beyond, :] = up_ref[after, lanes].astype(F32)
+        cots[beyond, :] = up_ref[after, lanes].astype(F32)[NEAR:]
 
     @pl.when((member == 0) & is_last)
     def _():
-        cots[beyond, :] = own_up_ref[after, lanes].astype(F32)
+        cots[beyond, :] = own_up_ref[after, lanes].astype(F32)[NEAR:]
 
     @pl.when((member == 0) & jnp.logical_not(is_last))
     def _():
-        cots[beyond, :] = down_ref[after, lanes].astype(F32)
+        cots[beyond, :] = down_ref[after, lanes].astype(F32)[NEAR:]
 
     def convolved(table_ref, keep_ref, window, block):
         height = 128 if block < 2 else EDGE
         keep = keep_ref[member, block, pl.ds(0, height), :]
-        result = jnp.zeros((height, TILE), F32)
-        for group in range(PER_TILE):
-            matrix = table_ref[first_group + group, pl.ds(0, height), :] * keep
-            product = jnp.dot(matrix, window, preferred_element_type=F32)
-            result = jnp.where(lane_group[:height] == group, product, result)
+        matrix = table_ref[pl.ds(first_group, PER_TILE), pl.ds(0, height), :] * keep[None]
+        product = jnp.dot(matrix.reshape(PER_TILE * height, 256), window, preferred_element_type=F32)
+        result = product[:height]
+        for group in range(1, PER_TILE):
+            result = jnp.where(lane_group[:height] == group, product[group * height : (group + 1) * height], result)
         return result
 
     for block in range(3):
@@ -449,16 +498,20 @@
     anywhere = pl.BlockSpec(memory_space=pl.ANY)
     pay_up, pay_down = pl.pallas_call(
         functools.partial(payload_kernel, members),
-        in_specs=[smem, anywhere, anywhere, whole],
-        out_specs=[whole, whole],
+        in_specs=[anywhere] * 4,
+        out_specs=[anywhere] * 2,
         out_shape=[shape((TAIL + HEAD, channels), BF16), shape((TAIL + HEAD, channels), BF16)],
         scratch_shapes=[
-            pltpu.VMEM((tiles, 3, 2 * STRETCH, TILE), BF16),
-            pltpu.VMEM((tiles, 2 * STRETCH, TILE), BF16),
+            pltpu.SMEM((DOCS,), jnp.int32),
+            pltpu.VMEM((3, TAPS, channels), F32),
+            pltpu.VMEM((TAIL + HEAD, channels), BF16),
+            pltpu.VMEM((TAIL + HEAD, channels), BF16),
+            pltpu.VMEM((3, 2 * STRETCH, channels), BF16),
+            pltpu.VMEM((2 * STRETCH, channels), BF16),
             pltpu.VMEM((2, TAPS - 1, STRETCH, TILE), F32),
             pltpu.VMEM((STRETCH + 8, TILE), F32),
-            pltpu.SemaphoreType.DMA((tiles,)),
-            pltpu.SemaphoreType.DMA((tiles,)),
+            pltpu.VMEM((144, TILE), F32),
+            pltpu.SemaphoreType.DMA((22,)),
         ],
         compiler_params=pltpu.CompilerParams(vmem_limit_bytes=56 * 1024 * 1024),
         cost_estimate=pl.CostEstimate(flops=20_000_000, bytes_accessed=2_800_000, transcendentals=0),
@@ -538,7 +591,8 @@
         scratch_shapes=[
             pltpu.VMEM((TAIL, TILE), BF16),
             pltpu.VMEM((HEAD, TILE), BF16),
-            pltpu.VMEM((2 * EDGE, TILE), F32),
+            pltpu.VMEM((NEAR + EDGE, TILE), F32),
+            pltpu.VMEM((144, TILE), F32),
         ],
         compiler_params=params,
         cost_estimate=pl.CostEstimate(flops=500_000_000, bytes_accessed=10_000_000, transcendentals=0),

time: 80.7 us -> 77.9 us (0.965)
  waiting for transfers between devices: 27.6 us -> 25.3 us
  Pallas kernels: 31.1 us -> 29.9 us
    ppermute x1, waiting for transfers between devices: 4.32 us -> 2.83 us  [shards(): lax.ppermute(pay_down, 'ctx', [(i + 1, i) for i in range(members - 1)])]
    ppermute x11, starting transfers between devices: 13.9 us -> 14.8 us  [along(): return lax.ppermute(block, axis, route)]
    ppermute x11, waiting for transfers between devices: 23.3 us -> 22.5 us  [along(): return lax.ppermute(block, axis, route)]
  transfers between devices with their start and end apart: 13 -> 13, of which waited for: 8 -> 9; matrix products, arithmetic and copies ran while one was open for 0% -> 0% of each run, Pallas kernels for 25% -> 26%
where the time goes in v3:
time: 77.9 us; the launch traced here: 77.8 us
  Pallas kernels  29.9 us (38%)
  waiting for transfers between devices  25.3 us (32%)
  starting transfers between devices  20.6 us (26%)
  local copies, waits for them, and re-layouts  0.97 us (1%)
  between operations  0.93 us (1%)
    ppermute x11, waiting for transfers between devices, along(): return lax.ppermute(block, axis, route)  22.5 us
    ppermute x11, starting transfers between devices, along(): return lax.ppermute(block, axis, route)  14.8 us
    pallas_call x3, Pallas kernels, convolve(): pl.pallas_call(functools.partial(conv_kernel, members, first), grid=(coun...  13.1 us
    pallas_call x1, Pallas kernels, shards(): pl.pallas_call(functools.partial(pair_kernel, members), grid=(tiles, 2),...  5.45 us
    pallas_call x1, Pallas kernels, shards(): pl.pallas_call(functools.partial(own_kernel, members), grid=(tiles,), in_...  3.91 us
    ppermute x1, starting transfers between devices, shards(): lax.ppermute(pay_up, 'ctx', [(i, i + 1) for i in range(members - 1)])  3.83 us
    pallas_call x1, Pallas kernels, shards(): pl.pallas_call(functools.partial(payload_kernel, members), in_specs=[anyw...  3.72 us
    pallas_call x1, Pallas kernels, shards(): pl.pallas_call(functools.partial(tables_kernel, members), grid=(tiles,),...  2.91 us
  transfers between devices with their start and end apart: 13, of which 9 were waited for; matrix products, arithmetic and copies ran while one was open for 0% of the time, Pallas kernels for 26%

profile of v3, /device:TPU:64, one launch (start us, length us, event | category | flops | bytes accessed | tf_op | source)
XLA Modules:
  0.0 77.8 jit_solution(8912463786385356618)
XLA Ops:
  0.6 0.0 copy-start
  0.6 0.0 copy-start.3
  0.7 0.0 copy-start.1
  0.7 0.0 copy-start.6
  0.7 3.7 %payload_rows.1 = (bf16[320,512]{1,0:T(8,128)(2,1)}, bf16[320,512]{1,0:T(8,128)(2,1)}) custom-call(s32[64]{0:T(128)} %lengths_ref.3, bf16[3,512,512]{2,1,0:T(8,128)(2,1)} %bitcast.6, bf16[512,512]{1,0:T(8,128)(2,1)} %cot_ref.9, f32[3,7,512]{2,1,0:T(8,128)} %bitcast.12), custom_call_target="tpu_custom_call" | custom-call | flops 20000000 | bytes 2800000 | tf_op jit(solution)/shard_map/payload_rows/pallas_call | solution.py:499
  4.4 3.8 %collective-permute-start = (bf16[320,512]{1,0:T(8,128)(2,1)}, bf16[320,512]{1,0:T(8,128)(2,1)S(1)}, u32[]{:S(2)}, u32[]{:S(2)}) collective-permute-start(bf16[320,512]{1,0:T(8,128)(2,1)} %get-tuple-element.46.own_up_ref), channel_id=1, source_target_pairs={{0,8},{8,16},{16,24},{24,32},{32,40},{40,48},{48,56},{56,64},{64,7... | collective-permute-start | bytes 983048 | tf_op jit(solution)/shard_map/ppermute | solution.py:521
  8.2 2.0 %collective-permute-start.1 = (bf16[320,512]{1,0:T(8,128)(2,1)}, bf16[320,512]{1,0:T(8,128)(2,1)S(1)}, u32[]{:S(2)}, u32[]{:S(2)}) collective-permute-start(bf16[320,512]{1,0:T(8,128)(2,1)} %get-tuple-element.47), channel_id=1, source_target_pairs={{8,0},{16,8},{24,16},{32,24},{40,32},{48,40},{56,48},{64,56},{72,6... | collective-permute-start | bytes 983048 | tf_op jit(solution)/shard_map/ppermute | solution.py:522
  10.3 0.0 copy-done.6
  10.3 0.0 copy-start.4
  10.3 0.9 %copy-done.4 = f32[128,256]{1,0:T(8,128)S(1)} copy-done((f32[128,256]{1,0:T(8,128)S(1)}, f32[128,256]{1,0:T(8,128)}, u32[]{:S(2)}) %copy-start.4) | copy-done | bytes 131096
  11.2 2.9 %tables.1 = (bf16[32,128,256]{2,1,0:T(8,128)(2,1)S(1)}, bf16[32,128,256]{2,1,0:T(8,128)(2,1)S(1)}, bf16[2,3,128,256]{3,2,1,0:T(8,128)(2,1)S(1)}, bf16[2,3,128,25...) custom-call(s32[64]{0:T(128)S(1)} %copy-done.6, ...), custom_call_target="tpu_custom_call" | custom-call | flops 20000000 | bytes 7000000 | tf_op jit(solution)/shard_map/tables/pallas_call | solution.py:545
  14.1 0.0 copy-done
  14.1 0.0 copy-done.3
  14.1 0.0 copy-done.1
  14.1 0.0 copy-start.2
  14.1 3.9 %own_rows.1.kvg_ref.previous_ref = bf16[3,512,512]{2,1,0:T(8,128)(2,1)S(1)} custom-call(s32[64]{0:T(128)S(1)} %copy-done.6, bf16[3,512,512]{2,1,0:T(8,128)(2,1)S(1)} %bitcast.7, bf16[512,512]{1,0:T(8,128)(2,1)S(1)} %copy-done.1, f32[3,7,512]{2,1,0:T(8,128)S(1)} %bitcast.13), custom_call_target="tpu_custom_call" | custom-call | flops 40000000 | bytes 4500000 | tf_op jit(solution)/shard_map/own_rows/pallas_call | solution.py:524
  18.1 0.0 collective-permute-done.up_ref
  18.1 2.8 %collective-permute-done.1.down_ref = bf16[320,512]{1,0:T(8,128)(2,1)S(1)} collective-permute-done((bf16[320,512]{1,0:T(8,128)(2,1)}, bf16[320,512]{1,0:T(8,128)(2,1)S(1)}, u32[]{:S(2)}, u32[]{:S(2)}) %collective-permute-start.1) | collective-permute-done | bytes 327712 | tf_op jit(solution)/shard_map/ppermute | solution.py:522
  20.9 0.0 copy-done.2
  20.9 0.0 copy-start.5
  20.9 5.5 %pair_rows.1 = (bf16[2,512,512]{2,1,0:T(8,128)(2,1)S(1)}, bf16[2,512,512]{2,1,0:T(8,128)(2,1)S(1)}, bf16[2,2,272,512]{3,2,1,0:T(8,128)(2,1)S(1)}, f32[32,128]{1,0:T(8,128)S(1)}) custom-call(bf16[3,512,512]{2,1,0:T(8,128)(2,1)S(1)} %bitcast.8, bf16[3,512,512]{2,1,0:T(8,128)(2,1)S(1)} %own_rows.1.kvg_ref.previous_ref, bf16[512,512]{1,0:T(8,128)(2,1)S(1)} %copy-done.1, ...), custom_call_target="tpu_custom_call" | custom-call | flops 500000000 | bytes 10000000 | tf_op jit(solution)/shard_map/pair_rows/pallas_call | solution.py:580
  26.4 2.8 %collective-permute-start.2 = (f32[32,128]{1,0:T(8,128)S(1)}, f32[32,128]{1,0:T(8,128)S(1)}, u32[]{:S(2)}, u32[]{:S(2)}) collective-permute-start(f32[32,128]{1,0:T(8,128)S(1)} %get-tuple-element.50), channel_id=1, source_target_pairs={{0,192},{8,200},{16,208},{24,216},{32,224},{40,232},{48,240},{56,2... | collective-permute-start | bytes 49160 | tf_op jit(solution)/shard_map/ppermute | solution.py:470
  29.2 0.0 copy-done.5
  29.2 3.4 %conv_rows_0.1 = (bf16[3,512,512]{2,1,0:T(8,128)(2,1)}, f32[24,128]{1,0:T(8,128)S(1)}) custom-call(bf16[3,512,512]{2,1,0:T(8,128)(2,1)S(1)} %bitcast.9, bf16[2,512,512]{2,1,0:T(8,128)(2,1)S(1)} %get-tuple-element.65.mixed_ref, bf16[2,512,512]{2,1,0:T(8,128)(2,1)S(1)} %get-tuple-element.66.grads_ref, bf16[2,2,272,512]{3,2,1,0:T(8,128)(2,1)S(1)} %get-tuple-element.53.kv_ref, ...), custom_call_target="tpu_custom_call" | custom-call | flops 100000000 | bytes 2500000 | tf_op jit(solution)/shard_map/conv_rows_0/pallas_call | solution.py:603
  32.6 0.0 collective-permute-done.2
  32.6 0.3 collective-permute-start.3
  33.0 3.4 %conv_rows_1.1 = (bf16[3,512,512]{2,1,0:T(8,128)(2,1)}, f32[24,128]{1,0:T(8,128)S(1)}) custom-call(bf16[3,512,512]{2,1,0:T(8,128)(2,1)S(1)} %bitcast.10, bf16[2,512,512]{2,1,0:T(8,128)(2,1)S(1)} %get-tuple-element.65.mixed_ref, bf16[2,512,512]{2,1,0:T(8,128)(2,1)S(1)} %get-tuple-element.66.grads_ref, ...), custom_call_target="tpu_custom_call", output_to_operand_aliasing={{0}: (15, {})} | custom-call | flops 100000000 | bytes 2500000 | tf_op jit(solution)/shard_map/conv_rows_1/pallas_call | solution.py:603
  36.4 0.1 collective-permute-done.3
  36.5 2.9 %collective-permute-start.4 = (f32[32,128]{1,0:T(8,128)S(1)}, f32[32,128]{1,0:T(8,128)S(1)}, u32[]{:S(2)}, u32[]{:S(2)}) collective-permute-start(f32[32,128]{1,0:T(8,128)S(1)} %add.31), channel_id=1, source_target_pairs={{0,8},{8,0},{16,24},{24,16},{32,40},{40,32},{48,56},{56,48},{64,72... | collective-permute-start | bytes 49160 | tf_op jit(solution)/shard_map/ppermute | solution.py:470
  39.4 6.3 %conv_rows_2.1 = (bf16[3,512,512]{2,1,0:T(8,128)(2,1)}, f32[24,256]{1,0:T(8,128)S(1)}) custom-call(bf16[3,512,512]{2,1,0:T(8,128)(2,1)S(1)} %bitcast.11, bf16[2,512,512]{2,1,0:T(8,128)(2,1)S(1)} %get-tuple-element.65.mixed_ref, bf16[2,512,512]{2,1,0:T(8,128)(2,1)S(1)} %get-tuple-element.66.grads_ref, ...), custom_call_target="tpu_custom_call", output_to_operand_aliasing={{0}: (15, {})} | custom-call | flops 200000000 | bytes 5000000 | tf_op jit(solution)/shard_map/conv_rows_2/pallas_call | solution.py:603
  45.7 0.0 collective-permute-done.4
  45.7 0.1 collective-permute-start.5
  45.8 5.2 %collective-permute-done.5 = f32[32,512]{1,0:T(8,128)S(1)} collective-permute-done((f32[32,512]{1,0:T(8,128)S(1)}, f32[32,512]{1,0:T(8,128)S(1)}, u32[]{:S(2)}, u32[]{:S(2)}) %collective-permute-start.5) | collective-permute-done | bytes 65568 | tf_op jit(solution)/shard_map/ppermute | solution.py:470
  51.1 1.7 %collective-permute-start.6 = (f32[32,512]{1,0:T(8,128)S(1)}, f32[32,512]{1,0:T(8,128)S(1)}, u32[]{:S(2)}, u32[]{:S(2)}) collective-permute-start(f32[32,512]{1,0:T(8,128)S(1)} %constant_dynamic-update-slice_fusion), channel_id=1, source_target_pairs={{0,56},{8,48},{16,40},{24,32},{32,24},{40,16},{48,8},{56,0},{64,12... | collective-permute-start | bytes 196616 | tf_op jit(solution)/shard_map/ppermute | solution.py:470
  52.8 5.8 %collective-permute-done.6 = f32[32,512]{1,0:T(8,128)S(1)} collective-permute-done((f32[32,512]{1,0:T(8,128)S(1)}, f32[32,512]{1,0:T(8,128)S(1)}, u32[]{:S(2)}, u32[]{:S(2)}) %collective-permute-start.6) | collective-permute-done | bytes 65568 | tf_op jit(solution)/shard_map/ppermute | solution.py:470
  58.7 0.1 collective-permute-start.8
  58.8 0.1 collective-permute-start.7
  58.9 1.1 %collective-permute-done.8 = f32[32,128]{1,0:T(8,128)S(1)} collective-permute-done((f32[32,128]{1,0:T(8,128)S(1)}, f32[32,128]{1,0:T(8,128)S(1)}, u32[]{:S(2)}, u32[]{:S(2)}) %collective-permute-start.8) | collective-permute-done | bytes 16416 | tf_op jit(solution)/shard_map/ppermute | solution.py:470
  59.9 3.0 %collective-permute-done.7 = f32[24,512]{1,0:T(8,128)S(1)} collective-permute-done((f32[24,512]{1,0:T(8,128)S(1)}, f32[24,512]{1,0:T(8,128)S(1)}, u32[]{:S(2)}, u32[]{:S(2)}) %collective-permute-start.7) | collective-permute-done | bytes 49184 | tf_op jit(solution)/shard_map/ppermute | solution.py:470
  63.0 1.7 %collective-permute-start.10 = (f32[64,128]{1,0:T(8,128)S(1)}, f32[64,128]{1,0:T(8,128)S(1)}, u32[]{:S(2)}, u32[]{:S(2)}) collective-permute-start(f32[64,128]{1,0:T(8,128)S(1)} %pad_maximum_fusion.2), channel_id=1, source_target_pairs={{0,2},{1,3},{2,0},{3,1},{4,6},{5,7},{6,4},{7,5},{8,10},{9,11},{10,... | collective-permute-start | bytes 98312 | tf_op jit(solution)/shard_map/ppermute | solution.py:470
  64.6 1.4 %collective-permute-start.9 = (f32[24,512]{1,0:T(8,128)S(1)}, f32[24,512]{1,0:T(8,128)S(1)}, u32[]{:S(2)}, u32[]{:S(2)}) collective-permute-start(f32[24,512]{1,0:T(8,128)S(1)} %add.35), channel_id=1, source_target_pairs={{0,192},{8,200},{16,208},{24,216},{32,224},{40,232},{48,240},{56,2... | collective-permute-start | bytes 147464 | tf_op jit(solution)/shard_map/ppermute | solution.py:470
  66.1 0.9 %collective-permute-done.10 = f32[64,128]{1,0:T(8,128)S(1)} collective-permute-done((f32[64,128]{1,0:T(8,128)S(1)}, f32[64,128]{1,0:T(8,128)S(1)}, u32[]{:S(2)}, u32[]{:S(2)}) %collective-permute-start.10) | collective-permute-done | bytes 32800 | tf_op jit(solution)/shard_map/ppermute | solution.py:470
  67.0 2.9 %collective-permute-done.9 = f32[24,512]{1,0:T(8,128)S(1)} collective-permute-done((f32[24,512]{1,0:T(8,128)S(1)}, f32[24,512]{1,0:T(8,128)S(1)}, u32[]{:S(2)}, u32[]{:S(2)}) %collective-permute-start.9) | collective-permute-done | bytes 49184 | tf_op jit(solution)/shard_map/ppermute | solution.py:470
  69.9 3.0 %collective-permute-start.11 = (f32[128,128]{1,0:T(8,128)S(1)}, f32[128,128]{1,0:T(8,128)S(1)}, u32[]{:S(2)}, u32[]{:S(2)}) collective-permute-start(f32[128,128]{1,0:T(8,128)S(1)} %pad_maximum_fusion.1.taps_ref), channel_id=1, source_target_pairs={{0,4},{1,5},{2,6},{3,7},{4,0},{5,1},{6,2},{7,3},{8,12},{9,13},{10,... | collective-permute-start | bytes 196616 | tf_op jit(solution)/shard_map/ppermute | solution.py:470
  72.9 0.6 collective-permute-start.12
  73.5 3.5 %collective-permute-done.12.other_ref = f32[24,512]{1,0:T(8,128)S(1)} collective-permute-done((f32[24,512]{1,0:T(8,128)S(1)}, f32[24,512]{1,0:T(8,128)S(1)}, u32[]{:S(2)}, u32[]{:S(2)}) %collective-permute-start.12) | collective-permute-done | bytes 49184 | tf_op jit(solution)/shard_map/ppermute | solution.py:470
  77.0 0.0 collective-permute-done.11.next_taps_ref
  77.0 0.8 final.1
  (22 shorter events, 0.1 us)
Async XLA Ops:
  0.6 13.5 %copy-start = (bf16[512,3,512]{2,0,1:T(8,128)(2,1)S(1)}, bf16[512,3,512]{2,0,1:T(8,128)(2,1)}, u32[]{:S(2)}) copy-start(bf16[512,3,512]{2,0,1:T(8,128)(2,1)} %param.6) | copy-start | bytes 4718596
  0.6 13.5 %copy-start.3 = (f32[7,3,512]{2,0,1:T(8,128)S(1)}, f32[7,3,512]{2,0,1:T(8,128)}, u32[]{:S(2)}) copy-start(f32[7,3,512]{2,0,1:T(8,128)} %param.7) | copy-start | bytes 129028
  0.7 13.5 %copy-start.1 = (bf16[512,512]{1,0:T(8,128)(2,1)S(1)}, bf16[512,512]{1,0:T(8,128)(2,1)}, u32[]{:S(2)}) copy-start(bf16[512,512]{1,0:T(8,128)(2,1)} %cot_ref.9) | copy-start | bytes 1572868
  0.7 9.6 %copy-start.6 = (s32[64]{0:T(128)S(1)}, s32[64]{0:T(128)}, u32[]{:S(2)}) copy-start(s32[64]{0:T(128)} %lengths_ref.3) | copy-start | bytes 772
  4.4 13.7 %collective-permute-start = (bf16[320,512]{1,0:T(8,128)(2,1)}, bf16[320,512]{1,0:T(8,128)(2,1)S(1)}, u32[]{:S(2)}, u32[]{:S(2)}) collective-permute-start(bf16[320,512]{1,0:T(8,128)(2,1)} %get-tuple-element.46.own_up_ref), channel_id=1, source_target_pairs={{0,8},{8,16},{16,24},{24,32},{32,40},{40,48},{48,56},{56,64},{64,7... | collective-permute-start | bytes 983048 | tf_op jit(solution)/shard_map/ppermute | solution.py:521
  8.2 12.7 %collective-permute-start.1 = (bf16[320,512]{1,0:T(8,128)(2,1)}, bf16[320,512]{1,0:T(8,128)(2,1)S(1)}, u32[]{:S(2)}, u32[]{:S(2)}) collective-permute-start(bf16[320,512]{1,0:T(8,128)(2,1)} %get-tuple-element.47), channel_id=1, source_target_pairs={{8,0},{16,8},{24,16},{32,24},{40,32},{48,40},{56,48},{64,56},{72,6... | collective-permute-start | bytes 983048 | tf_op jit(solution)/shard_map/ppermute | solution.py:522
  10.3 0.9 %copy-start.4 = (f32[128,256]{1,0:T(8,128)S(1)}, f32[128,256]{1,0:T(8,128)}, u32[]{:S(2)}) copy-start(f32[128,256]{1,0:T(8,128)} %medium_ref.1) | copy-start | bytes 393220
  14.1 6.8 %copy-start.2 = (bf16[320,512]{1,0:T(8,128)(2,1)S(1)}, bf16[320,512]{1,0:T(8,128)(2,1)}, u32[]{:S(2)}) copy-start(bf16[320,512]{1,0:T(8,128)(2,1)} %get-tuple-element.46.own_up_ref) | copy-start | bytes 983044
  20.9 8.3 %copy-start.5 = (f32[512]{0:T(512)S(1)}, f32[512]{0:T(512)}, u32[]{:S(2)}) copy-start(f32[512]{0:T(512)} %param.9) | copy-start | bytes 6148
  26.4 6.3 %collective-permute-start.2 = (f32[32,128]{1,0:T(8,128)S(1)}, f32[32,128]{1,0:T(8,128)S(1)}, u32[]{:S(2)}, u32[]{:S(2)}) collective-permute-start(f32[32,128]{1,0:T(8,128)S(1)} %get-tuple-element.50), channel_id=1, source_target_pairs={{0,192},{8,200},{16,208},{24,216},{32,224},{40,232},{48,240},{56,2... | collective-permute-start | bytes 49160 | tf_op jit(solution)/shard_map/ppermute | solution.py:470
  32.6 3.8 %collective-permute-start.3 = (f32[32,128]{1,0:T(8,128)S(1)}, f32[32,128]{1,0:T(8,128)S(1)}, u32[]{:S(2)}, u32[]{:S(2)}) collective-permute-start(f32[32,128]{1,0:T(8,128)S(1)} %add.30), channel_id=1, source_target_pairs={{0,64},{8,72},{16,80},{24,88},{32,96},{40,104},{48,112},{56,120},{... | collective-permute-start | bytes 49160 | tf_op jit(solution)/shard_map/ppermute | solution.py:470
  36.5 9.2 %collective-permute-start.4 = (f32[32,128]{1,0:T(8,128)S(1)}, f32[32,128]{1,0:T(8,128)S(1)}, u32[]{:S(2)}, u32[]{:S(2)}) collective-permute-start(f32[32,128]{1,0:T(8,128)S(1)} %add.31), channel_id=1, source_target_pairs={{0,8},{8,0},{16,24},{24,16},{32,40},{40,32},{48,56},{56,48},{64,72... | collective-permute-start | bytes 49160 | tf_op jit(solution)/shard_map/ppermute | solution.py:470
  45.7 5.3 %collective-permute-start.5 = (f32[32,512]{1,0:T(8,128)S(1)}, f32[32,512]{1,0:T(8,128)S(1)}, u32[]{:S(2)}, u32[]{:S(2)}) collective-permute-start(f32[32,512]{1,0:T(8,128)S(1)} %pad_maximum_fusion), channel_id=1, source_target_pairs={{0,16},{8,24},{16,0},{24,8},{32,48},{40,56},{48,32},{56,40},{64,80... | collective-permute-start | bytes 196616 | tf_op jit(solution)/shard_map/ppermute | solution.py:470
  51.1 7.5 %collective-permute-start.6 = (f32[32,512]{1,0:T(8,128)S(1)}, f32[32,512]{1,0:T(8,128)S(1)}, u32[]{:S(2)}, u32[]{:S(2)}) collective-permute-start(f32[32,512]{1,0:T(8,128)S(1)} %constant_dynamic-update-slice_fusion), channel_id=1, source_target_pairs={{0,56},{8,48},{16,40},{24,32},{32,24},{40,16},{48,8},{56,0},{64,12... | collective-permute-start | bytes 196616 | tf_op jit(solution)/shard_map/ppermute | solution.py:470
  58.7 1.3 %collective-permute-start.8 = (f32[32,128]{1,0:T(8,128)S(1)}, f32[32,128]{1,0:T(8,128)S(1)}, u32[]{:S(2)}, u32[]{:S(2)}) collective-permute-start(f32[32,128]{1,0:T(8,128)S(1)} %reshape.32), channel_id=1, source_target_pairs={{0,1},{1,0},{2,3},{3,2},{4,5},{5,4},{6,7},{7,6},{8,9},{9,8},{10,11... | collective-permute-start | bytes 49160 | tf_op jit(solution)/shard_map/ppermute | solution.py:470
  58.8 4.2 %collective-permute-start.7 = (f32[24,512]{1,0:T(8,128)S(1)}, f32[24,512]{1,0:T(8,128)S(1)}, u32[]{:S(2)}, u32[]{:S(2)}) collective-permute-start(f32[24,512]{1,0:T(8,128)S(1)} %slice.18), channel_id=1, source_target_pairs={{0,8},{8,0},{16,24},{24,16},{32,40},{40,32},{48,56},{56,48},{64,72... | collective-permute-start | bytes 147464 | tf_op jit(solution)/shard_map/ppermute | solution.py:470
  63.0 4.0 %collective-permute-start.10 = (f32[64,128]{1,0:T(8,128)S(1)}, f32[64,128]{1,0:T(8,128)S(1)}, u32[]{:S(2)}, u32[]{:S(2)}) collective-permute-start(f32[64,128]{1,0:T(8,128)S(1)} %pad_maximum_fusion.2), channel_id=1, source_target_pairs={{0,2},{1,3},{2,0},{3,1},{4,6},{5,7},{6,4},{7,5},{8,10},{9,11},{10,... | collective-permute-start | bytes 98312 | tf_op jit(solution)/shard_map/ppermute | solution.py:470
  64.6 5.3 %collective-permute-start.9 = (f32[24,512]{1,0:T(8,128)S(1)}, f32[24,512]{1,0:T(8,128)S(1)}, u32[]{:S(2)}, u32[]{:S(2)}) collective-permute-start(f32[24,512]{1,0:T(8,128)S(1)} %add.35), channel_id=1, source_target_pairs={{0,192},{8,200},{16,208},{24,216},{32,224},{40,232},{48,240},{56,2... | collective-permute-start | bytes 147464 | tf_op jit(solution)/shard_map/ppermute | solution.py:470
  69.9 7.1 %collective-permute-start.11 = (f32[128,128]{1,0:T(8,128)S(1)}, f32[128,128]{1,0:T(8,128)S(1)}, u32[]{:S(2)}, u32[]{:S(2)}) collective-permute-start(f32[128,128]{1,0:T(8,128)S(1)} %pad_maximum_fusion.1.taps_ref), channel_id=1, source_target_pairs={{0,4},{1,5},{2,6},{3,7},{4,0},{5,1},{6,2},{7,3},{8,12},{9,13},{10,... | collective-permute-start | bytes 196616 | tf_op jit(solution)/shard_map/ppermute | solution.py:470
  72.9 4.1 %collective-permute-start.12 = (f32[24,512]{1,0:T(8,128)S(1)}, f32[24,512]{1,0:T(8,128)S(1)}, u32[]{:S(2)}, u32[]{:S(2)}) collective-permute-start(f32[24,512]{1,0:T(8,128)S(1)} %add.37.sums_ref), channel_id=1, source_target_pairs={{0,64},{8,72},{16,80},{24,88},{32,96},{40,104},{48,112},{56,120},{... | collective-permute-start | bytes 147464 | tf_op jit(solution)/shard_map/ppermute | solution.py:470

commit v4 on v3

--- a/solution.py
+++ b/solution.py
@@ -362,10 +362,9 @@
 def conv_kernel(
     members, first_tile, feat_ref, mixed_ref, grads_ref, kv_ref, cot_ref, own_up_ref, up_ref, down_ref,
     taps_ref, skip_ref, forward_ref, backward_ref, keep_f_ref, keep_b_ref, shifted_ref,
-    previous_ref, out_ref, sums_ref,
+    stack_ref, sums_ref,
     cots, stack,
 ):
-    del previous_ref
     member = pl.program_id(1)
     tile = first_tile + pl.program_id(0)
     lanes = pl.ds(pl.multiple_of(tile * TILE, TILE), TILE)
@@ -417,25 +416,23 @@
                 product = cots[place, :] * medium
             else:
                 product = grad_conv * kv_ref[member, 2 - stream, place, lanes].astype(F32)
-            stack[stream, place, :] = product.astype(BF16).astype(F32)
+            product = product.astype(BF16)
+            stack[stream, place, :] = product.astype(F32)
+            stack_ref[member, stream, place, pl.ds(pl.multiple_of(pl.program_id(0) * TILE, TILE), TILE)] = product
 
     @pl.when(member == 0)
     def _():
         sums_ref[...] = jnp.zeros(sums_ref.shape, F32)
 
     for stream in range(3):
-        weights = taps_ref[stream, :, lanes]
         partial = [jnp.zeros((8, TILE), F32) for _ in range(TAPS)]
         for chunk in range(0, STRETCH, 64):
             source = feat_ref[stream, own(chunk, 64), lanes].astype(F32)
-            total = jnp.zeros((64, TILE), F32)
             for lag in range(TAPS):
-                later = stack[stream, pl.ds(chunk + lag, 64), :]
+                later = stack[stream, pl.ds(chunk + lag, 64), :] * source
                 if lag > 0:
                     later = later * shifted_ref[member, lag - 1, pl.ds(chunk, 64), :]
-                total = total + later * weights[lag : lag + 1, :]
-                partial[lag] = partial[lag] + jnp.sum((later * source).reshape(8, 8, TILE), axis=0)
-            out_ref[stream, pl.ds(chunk, 64), :] = total.astype(BF16)
+                partial[lag] = partial[lag] + jnp.sum(later.reshape(8, 8, TILE), axis=0)
         for lag in range(TAPS):
             row = pl.ds(stream * 8 + lag, 1)
             sums_ref[row, :] += jnp.sum(partial[lag], axis=0, keepdims=True)
@@ -444,6 +441,26 @@
         axis=0, keepdims=True,
     )
     sums_ref[pl.ds(7, 1), :] += bias
+
+
+def adjoint_kernel(pieces, *refs):
+    stack_refs, (taps_ref, shifted_ref, previous_ref, out_ref, stack) = refs[:pieces], refs[pieces:]
+    del previous_ref
+    tile, member = pl.program_id(0), pl.program_id(1)
+    if pieces == 1:
+        stack[...] = stack_refs[0][member, :, :, pl.ds(pl.multiple_of(tile * TILE, TILE), TILE)].astype(F32)
+    for piece in range(pieces if pieces > 1 else 0):
+        @pl.when(tile == piece)
+        def _():
+            stack[...] = stack_refs[piece][member].astype(F32)
+    for stream in range(3):
+        weights = taps_ref[stream]
+        for chunk in range(0, STRETCH, 64):
+            total = stack[stream, pl.ds(chunk, 64), :] * weights[0:1, :]
+            for lag in range(1, TAPS):
+                later = stack[stream, pl.ds(chunk + lag, 64), :] * shifted_ref[member, lag - 1, pl.ds(chunk, 64), :]
+                total = total + later * weights[lag : lag + 1, :]
+            out_ref[stream, pl.ds(chunk, 64), :] = total.astype(BF16)
 
 
 def final_kernel(scale, flip, taps_ref, next_taps_ref, sums_ref, other_ref, medium_ref, short_ref, bias_ref):
@@ -599,20 +616,19 @@
         name="pair_rows",
     )(streams, kvg, cotangent, pay_up, got_up, got_down, weights, keep_r, edge)
 
-    def convolve(first, count, mixed, grads, previous):
+    def convolve(first, count, mixed, grads):
         return pl.pallas_call(
             functools.partial(conv_kernel, members, first),
             grid=(count, 2),
-            in_specs=[whole] * 15 + [anywhere],
+            in_specs=[whole] * 15,
             out_specs=[
-                pl.BlockSpec((3, STRETCH, TILE), lambda l, m: (0, m, first + l)),
+                whole,
                 pl.BlockSpec((24, TILE), lambda l, m: (0, l)),
             ],
             out_shape=[
-                shape((3, 2 * STRETCH, channels), BF16),
+                shape((2, 3, STRETCH + EDGE, count * TILE), BF16),
                 shape((24, count * TILE), F32),
             ],
-            input_output_aliases={15: 0} if first > 0 else {},
             scratch_shapes=[
                 pltpu.VMEM((STRETCH + EDGE, TILE), F32),
                 pltpu.VMEM((3, STRETCH + EDGE, TILE), F32),
@@ -622,18 +638,35 @@
             name=f"conv_rows_{first}",
         )(
             streams, mixed, grads, kv, cotangent, pay_up, got_up, got_down,
-            weights, skip_bias.reshape(1, channels), forward, backward, keep_f, keep_b, shifted, previous,
+            weights, skip_bias.reshape(1, channels), forward, backward, keep_f, keep_b, shifted,
         )
 
-    parts = []
-    grad_streams = kvg
+    parts, stacks = [], []
     for route, (first, count) in zip(routes_x() + routes_z()[1:2], ((0, 1), (1, 1), (2, 2))):
         other = along(taps, "ctx", route)
-        grad_streams, part = convolve(first, count, mixed, grads, grad_streams)
+        stack, part = convolve(first, count, mixed, grads)
+        stacks.append(stack)
         taps, mixed, grads, part = lax.optimization_barrier((taps + other, mixed, grads, part))
         parts.append(part)
 
+    def adjoint(first, pieces, previous):
+        return pl.pallas_call(
+            functools.partial(adjoint_kernel, len(pieces)),
+            grid=(2, 2),
+            in_specs=[whole] * len(pieces) + [
+                pl.BlockSpec((3, TAPS, TILE), lambda l, m: (0, 0, first + l)), whole, anywhere,
+            ],
+            out_specs=pl.BlockSpec((3, STRETCH, TILE), lambda l, m: (0, m, first + l)),
+            out_shape=shape((3, 2 * STRETCH, channels), BF16),
+            input_output_aliases={len(pieces) + 2: 0} if first > 0 else {},
+            scratch_shapes=[pltpu.VMEM((3, STRETCH + EDGE, TILE), F32)],
+            compiler_params=params,
+            cost_estimate=pl.CostEstimate(flops=20_000_000, bytes_accessed=4_000_000, transcendentals=0),
+            name=f"adjoint_rows_{first}",
+        )(*pieces, weights, shifted, previous)
+
     sums = jnp.concatenate(parts, axis=1)
+    grad_streams = kvg
     routes = routes_z()[2:] + routes_z()[:2] + routes_x()
     flip = 1
     for step, route in enumerate(routes):
@@ -652,7 +685,9 @@
                 )
                 sums = sums + other
                 flip *= 2
-        sums, taps = lax.optimization_barrier((sums, taps))
+        if step < 2:
+            grad_streams = adjoint(2 * step, stacks[2 * step : 2 * step + 2], grad_streams)
+        sums, taps, grad_streams = lax.optimization_barrier((sums, taps, grad_streams))
     grad_medium, short, bias = pl.pallas_call(
         functools.partial(final_kernel, scale, flip),
         in_specs=[whole] * 4,

time: 77.9 us -> 77.7 us (level); the launches traced: 77.8 us -> 76.8 us
  waiting for transfers between devices: 25.3 us -> 18 us
  local copies, waits for them, and re-layouts: 0.97 us -> 6.54 us
    ppermute x11, waiting for transfers between devices: 22.5 us -> 15.2 us  [along(): return lax.ppermute(block, axis, route)]
    unnamed x15 -> x27, local copies, waits for them, and re-layouts: 0.93 us -> 6.5 us
    pallas_call x0 -> x2, Pallas kernels: none -> 4.46 us  [adjoint(): pl.pallas_call(functools.partial(adjoint_kernel, len(pieces)), grid=(2, 2...]
    pallas_call x3, Pallas kernels: 13.1 us -> 9.28 us  [convolve(): pl.pallas_call(functools.partial(conv_kernel, members, first), grid=(coun...]
  transfers between devices with their start and end apart: 13 -> 13, of which waited for: 9 -> 9; matrix products, arithmetic and copies ran while one was open for 0% -> 0% of each run, Pallas kernels for 26% -> 27%
where the time goes in v4:
time: 77.7 us; the launch traced here: 76.8 us
  Pallas kernels  30.5 us (39%)
  starting transfers between devices  20.6 us (27%)
  waiting for transfers between devices  18 us (23%)
  local copies, waits for them, and re-layouts  6.54 us (8%)
  between operations  0.98 us (1%)
    ppermute x11, waiting for transfers between devices, along(): return lax.ppermute(block, axis, route)  15.2 us
    ppermute x11, starting transfers between devices, along(): return lax.ppermute(block, axis, route)  14.8 us
    pallas_call x3, Pallas kernels, convolve(): pl.pallas_call(functools.partial(conv_kernel, members, first), grid=(coun...  9.28 us
    unnamed x27, local copies, waits for them, and re-layouts  6.5 us
    pallas_call x1, Pallas kernels, shards(): pl.pallas_call(functools.partial(pair_kernel, members), grid=(tiles, 2),...  5.49 us
    pallas_call x2, Pallas kernels, adjoint(): pl.pallas_call(functools.partial(adjoint_kernel, len(pieces)), grid=(2, 2...  4.46 us
    pallas_call x1, Pallas kernels, shards(): pl.pallas_call(functools.partial(own_kernel, members), grid=(tiles,), in_...  3.91 us
    ppermute x1, starting transfers between devices, shards(): lax.ppermute(pay_up, 'ctx', [(i, i + 1) for i in range(members - 1)])  3.83 us
  transfers between devices with their start and end apart: 13, of which 9 were waited for; matrix products, arithmetic and copies ran while one was open for 0% of the time, Pallas kernels for 27%

profile of v4, /device:TPU:64, one launch (start us, length us, event | category | flops | bytes accessed | tf_op | source)
XLA Modules:
  0.0 76.8 jit_solution(16401809082278428323)
XLA Ops:
  0.6 0.0 copy-start
  0.6 0.0 copy-start.12
  0.7 0.0 copy-start.1
  0.7 0.0 copy-start.3
  0.7 3.7 %payload_rows.1 = (bf16[320,512]{1,0:T(8,128)(2,1)}, bf16[320,512]{1,0:T(8,128)(2,1)}) custom-call(s32[64]{0:T(128)} %lengths_ref.3, bf16[3,512,512]{2,1,0:T(8,128)(2,1)} %bitcast.6, bf16[512,512]{1,0:T(8,128)(2,1)} %cot_ref.9, f32[3,7,512]{2,1,0:T(8,128)} %bitcast.12), custom_call_target="tpu_custom_call" | custom-call | flops 20000000 | bytes 2800000 | tf_op jit(solution)/shard_map/payload_rows/pallas_call | solution.py:516
  4.4 3.8 %collective-permute-start = (bf16[320,512]{1,0:T(8,128)(2,1)}, bf16[320,512]{1,0:T(8,128)(2,1)S(1)}, u32[]{:S(2)}, u32[]{:S(2)}) collective-permute-start(bf16[320,512]{1,0:T(8,128)(2,1)} %get-tuple-element.50.own_up_ref), channel_id=1, source_target_pairs={{0,8},{8,16},{16,24},{24,32},{32,40},{40,48},{48,56},{56,64},{64,7... | collective-permute-start | bytes 983048 | tf_op jit(solution)/shard_map/ppermute | solution.py:538
  8.2 2.0 %collective-permute-start.1 = (bf16[320,512]{1,0:T(8,128)(2,1)}, bf16[320,512]{1,0:T(8,128)(2,1)S(1)}, u32[]{:S(2)}, u32[]{:S(2)}) collective-permute-start(bf16[320,512]{1,0:T(8,128)(2,1)} %get-tuple-element.51), channel_id=1, source_target_pairs={{8,0},{16,8},{24,16},{32,24},{40,32},{48,40},{56,48},{64,56},{72,6... | collective-permute-start | bytes 983048 | tf_op jit(solution)/shard_map/ppermute | solution.py:539
  10.2 0.0 copy-done.12
  10.3 0.0 copy-start.10
  10.3 0.9 %copy-done.10 = f32[128,256]{1,0:T(8,128)S(1)} copy-done((f32[128,256]{1,0:T(8,128)S(1)}, f32[128,256]{1,0:T(8,128)}, u32[]{:S(2)}) %copy-start.10) | copy-done | bytes 131096
  11.2 2.9 %tables.1 = (bf16[32,128,256]{2,1,0:T(8,128)(2,1)S(1)}, bf16[32,128,256]{2,1,0:T(8,128)(2,1)S(1)}, bf16[2,3,128,256]{3,2,1,0:T(8,128)(2,1)S(1)}, bf16[2,3,128,25...) custom-call(s32[64]{0:T(128)S(1)} %copy-done.12, ...), custom_call_target="tpu_custom_call" | custom-call | flops 20000000 | bytes 7000000 | tf_op jit(solution)/shard_map/tables/pallas_call | solution.py:562
  14.1 0.0 copy-done
  14.1 0.0 copy-done.1
  14.1 0.0 copy-done.3
  14.1 0.0 copy-start.2
  14.1 3.9 %own_rows.1.kvg_ref.refs_4_ = bf16[3,512,512]{2,1,0:T(8,128)(2,1)S(1)} custom-call(s32[64]{0:T(128)S(1)} %copy-done.12, bf16[3,512,512]{2,1,0:T(8,128)(2,1)S(1)} %bitcast.7, bf16[512,512]{1,0:T(8,128)(2,1)S(1)} %copy-done.1, f32[3,7,512]{2,1,0:T(8,128)S(1)} %bitcast.13), custom_call_target="tpu_custom_call" | custom-call | flops 40000000 | bytes 4500000 | tf_op jit(solution)/shard_map/own_rows/pallas_call | solution.py:541
  18.0 0.0 collective-permute-done.up_ref
  18.1 2.8 %collective-permute-done.1.down_ref = bf16[320,512]{1,0:T(8,128)(2,1)S(1)} collective-permute-done((bf16[320,512]{1,0:T(8,128)(2,1)}, bf16[320,512]{1,0:T(8,128)(2,1)S(1)}, u32[]{:S(2)}, u32[]{:S(2)}) %collective-permute-start.1) | collective-permute-done | bytes 327712 | tf_op jit(solution)/shard_map/ppermute | solution.py:539
  20.9 0.0 copy-done.2
  20.9 0.0 copy-start.11
  20.9 5.5 %pair_rows.1 = (bf16[2,512,512]{2,1,0:T(8,128)(2,1)S(1)}, bf16[2,512,512]{2,1,0:T(8,128)(2,1)S(1)}, bf16[2,2,272,512]{3,2,1,0:T(8,128)(2,1)S(1)}, f32[32,128]{1,0:T(8,128)S(1)}) custom-call(bf16[3,512,512]{2,1,0:T(8,128)(2,1)S(1)} %bitcast.8, bf16[3,512,512]{2,1,0:T(8,128)(2,1)S(1)} %own_rows.1.kvg_ref.refs_4_, bf16[512,512]{1,0:T(8,128)(2,1)S(1)} %copy-done.1, ...), custom_call_target="tpu_custom_call" | custom-call | flops 500000000 | bytes 10000000 | tf_op jit(solution)/shard_map/pair_rows/pallas_call | solution.py:597
  26.4 2.8 %collective-permute-start.2 = (f32[32,128]{1,0:T(8,128)S(1)}, f32[32,128]{1,0:T(8,128)S(1)}, u32[]{:S(2)}, u32[]{:S(2)}) collective-permute-start(f32[32,128]{1,0:T(8,128)S(1)} %get-tuple-element.54), channel_id=1, source_target_pairs={{0,192},{8,200},{16,208},{24,216},{32,224},{40,232},{48,240},{56,2... | collective-permute-start | bytes 49160 | tf_op jit(solution)/shard_map/ppermute | solution.py:487
  29.2 0.0 copy-done.11
  29.2 2.3 %conv_rows_0.1 = (bf16[2,3,272,128]{3,2,1,0:T(8,128)(2,1)S(1)}, f32[24,128]{1,0:T(8,128)S(1)}) custom-call(bf16[3,512,512]{2,1,0:T(8,128)(2,1)S(1)} %bitcast.9, bf16[2,512,512]{2,1,0:T(8,128)(2,1)S(1)} %get-tuple-element.71.mixed_ref, bf16[2,512,512]{2,1,0:T(8,128)(2,1)S(1)} %get-tuple-element.72.grads_ref, ...), custom_call_target="tpu_custom_call" | custom-call | flops 100000000 | bytes 2500000 | tf_op jit(solution)/shard_map/conv_rows_0/pallas_call | solution.py:620
  31.5 0.0 copy-start.6
  31.5 0.7 copy-done.6
  32.3 0.0 collective-permute-done.2
  32.3 0.3 collective-permute-start.3
  32.6 2.3 %conv_rows_1.1 = (bf16[2,3,272,128]{3,2,1,0:T(8,128)(2,1)S(1)}, f32[24,128]{1,0:T(8,128)S(1)}) custom-call(bf16[3,512,512]{2,1,0:T(8,128)(2,1)S(1)} %bitcast.10, bf16[2,512,512]{2,1,0:T(8,128)(2,1)S(1)} %get-tuple-element.71.mixed_ref, bf16[2,512,512]{2,1,0:T(8,128)(2,1)S(1)} %get-tuple-element.72.grads_ref, ...), custom_call_target="tpu_custom_call" | custom-call | flops 100000000 | bytes 2500000 | tf_op jit(solution)/shard_map/conv_rows_1/pallas_call | solution.py:620
  34.9 0.0 copy-start.8
  34.9 0.8 %copy-done.8 = bf16[2,3,272,128]{3,2,1,0:T(8,128)(2,1)} copy-done((bf16[2,3,272,128]{3,2,1,0:T(8,128)(2,1)}, bf16[2,3,272,128]{3,2,1,0:T(8,128)(2,1)S(1)}, u32[]{:S(2)}) %copy-start.8) | copy-done | bytes 417816
  35.7 0.4 collective-permute-done.3
  36.1 2.9 %collective-permute-start.4 = (f32[32,128]{1,0:T(8,128)S(1)}, f32[32,128]{1,0:T(8,128)S(1)}, u32[]{:S(2)}, u32[]{:S(2)}) collective-permute-start(f32[32,128]{1,0:T(8,128)S(1)} %add.31), channel_id=1, source_target_pairs={{0,8},{8,0},{16,24},{24,16},{32,40},{40,32},{48,56},{56,48},{64,72... | collective-permute-start | bytes 49160 | tf_op jit(solution)/shard_map/ppermute | solution.py:487
  39.1 4.7 %conv_rows_2.1 = (bf16[2,3,272,256]{3,2,1,0:T(8,128)(2,1)S(1)}, f32[24,256]{1,0:T(8,128)S(1)}) custom-call(bf16[3,512,512]{2,1,0:T(8,128)(2,1)S(1)} %bitcast.11, bf16[2,512,512]{2,1,0:T(8,128)(2,1)S(1)} %get-tuple-element.71.mixed_ref, bf16[2,512,512]{2,1,0:T(8,128)(2,1)S(1)} %get-tuple-element.72.grads_ref, ...), custom_call_target="tpu_custom_call" | custom-call | flops 200000000 | bytes 5000000 | tf_op jit(solution)/shard_map/conv_rows_2/pallas_call | solution.py:620
  43.8 0.0 copy-start.4
  43.8 0.9 %copy-done.4 = bf16[2,3,272,256]{3,2,1,0:T(8,128)(2,1)} copy-done((bf16[2,3,272,256]{3,2,1,0:T(8,128)(2,1)}, bf16[2,3,272,256]{3,2,1,0:T(8,128)(2,1)S(1)}, u32[]{:S(2)}) %copy-start.4) | copy-done | bytes 835608
  44.7 0.0 collective-permute-done.4
  44.7 0.1 collective-permute-start.5
  44.8 0.0 copy-start.7
  44.8 1.0 %copy-done.7 = bf16[2,3,272,128]{3,2,1,0:T(8,128)(2,1)S(1)} copy-done((bf16[2,3,272,128]{3,2,1,0:T(8,128)(2,1)S(1)}, bf16[2,3,272,128]{3,2,1,0:T(8,128)(2,1)}, u32[]{:S(2)}) %copy-start.7) | copy-done | bytes 417816
  45.8 0.0 copy-start.9
  45.8 1.0 %copy-done.9 = bf16[2,3,272,128]{3,2,1,0:T(8,128)(2,1)S(1)} copy-done((bf16[2,3,272,128]{3,2,1,0:T(8,128)(2,1)S(1)}, bf16[2,3,272,128]{3,2,1,0:T(8,128)(2,1)}, u32[]{:S(2)}) %copy-start.9) | copy-done | bytes 417816
  46.8 2.2 %adjoint_rows_0.1.refs_3_ = bf16[3,512,512]{2,1,0:T(8,128)(2,1)} custom-call(bf16[2,3,272,128]{3,2,1,0:T(8,128)(2,1)S(1)} %copy-done.7, bf16[2,3,272,128]{3,2,1,0:T(8,128)(2,1)S(1)} %copy-done.9, f32[3,7,512]{2,1,0:T(8,128)S(1)} %bitcast.18, f32[2,6,256,128]{3,2,1,0:T(8,128)S(1)} %get-tuple-element.62.shifted_ref.refs_3_.refs_2_, ...), custom_call_target="tpu_custom_call" | custom-call | flops 20000000 | bytes 4000000 | tf_op jit(solution)/shard_map/adjoint_rows_0/pallas_call | solution.py:653
  49.1 0.9 %collective-permute-done.5 = f32[32,512]{1,0:T(8,128)S(1)} collective-permute-done((f32[32,512]{1,0:T(8,128)S(1)}, f32[32,512]{1,0:T(8,128)S(1)}, u32[]{:S(2)}, u32[]{:S(2)}) %collective-permute-start.5) | collective-permute-done | bytes 65568 | tf_op jit(solution)/shard_map/ppermute | solution.py:487
  50.1 1.7 %collective-permute-start.6 = (f32[32,512]{1,0:T(8,128)S(1)}, f32[32,512]{1,0:T(8,128)S(1)}, u32[]{:S(2)}, u32[]{:S(2)}) collective-permute-start(f32[32,512]{1,0:T(8,128)S(1)} %constant_dynamic-update-slice_fusion), channel_id=1, source_target_pairs={{0,56},{8,48},{16,40},{24,32},{32,24},{40,16},{48,8},{56,0},{64,12... | collective-permute-start | bytes 196616 | tf_op jit(solution)/shard_map/ppermute | solution.py:487
  51.8 0.0 copy-start.5
  51.8 1.1 %copy-done.5 = bf16[2,3,272,256]{3,2,1,0:T(8,128)(2,1)S(1)} copy-done((bf16[2,3,272,256]{3,2,1,0:T(8,128)(2,1)S(1)}, bf16[2,3,272,256]{3,2,1,0:T(8,128)(2,1)}, u32[]{:S(2)}) %copy-start.5) | copy-done | bytes 835608
  52.9 2.2 %adjoint_rows_2.1 = bf16[3,512,512]{2,1,0:T(8,128)(2,1)} custom-call(bf16[2,3,272,256]{3,2,1,0:T(8,128)(2,1)S(1)} %copy-done.5, f32[3,7,512]{2,1,0:T(8,128)S(1)} %bitcast.19, f32[2,6,256,128]{3,2,1,0:T(8,128)S(1)} %get-tuple-element.62.shifted_ref.refs_3_.refs_2_, bf16[3,512,512]{2,1,0:T(8,128)(2,1)} %adjoint_rows_0.1.refs_3_), custom_call_target="tpu_custom_call", output_to_operand_aliasing={{}: (3, {})} | custom-call | flops 20000000 | bytes 4000000 | tf_op jit(solution)/shard_map/adjoint_rows_2/pallas_call | solution.py:653
  55.1 2.5 %collective-permute-done.6 = f32[32,512]{1,0:T(8,128)S(1)} collective-permute-done((f32[32,512]{1,0:T(8,128)S(1)}, f32[32,512]{1,0:T(8,128)S(1)}, u32[]{:S(2)}, u32[]{:S(2)}) %collective-permute-start.6) | collective-permute-done | bytes 65568 | tf_op jit(solution)/shard_map/ppermute | solution.py:487
  57.7 0.1 collective-permute-start.8
  57.8 0.1 collective-permute-start.7
  57.9 1.1 %collective-permute-done.8 = f32[32,128]{1,0:T(8,128)S(1)} collective-permute-done((f32[32,128]{1,0:T(8,128)S(1)}, f32[32,128]{1,0:T(8,128)S(1)}, u32[]{:S(2)}, u32[]{:S(2)}) %collective-permute-start.8) | collective-permute-done | bytes 16416 | tf_op jit(solution)/shard_map/ppermute | solution.py:487
  58.9 3.0 %collective-permute-done.7 = f32[24,512]{1,0:T(8,128)S(1)} collective-permute-done((f32[24,512]{1,0:T(8,128)S(1)}, f32[24,512]{1,0:T(8,128)S(1)}, u32[]{:S(2)}, u32[]{:S(2)}) %collective-permute-start.7) | collective-permute-done | bytes 49184 | tf_op jit(solution)/shard_map/ppermute | solution.py:487
  62.0 1.7 %collective-permute-start.10 = (f32[64,128]{1,0:T(8,128)S(1)}, f32[64,128]{1,0:T(8,128)S(1)}, u32[]{:S(2)}, u32[]{:S(2)}) collective-permute-start(f32[64,128]{1,0:T(8,128)S(1)} %pad_maximum_fusion.2), channel_id=1, source_target_pairs={{0,2},{1,3},{2,0},{3,1},{4,6},{5,7},{6,4},{7,5},{8,10},{9,11},{10,... | collective-permute-start | bytes 98312 | tf_op jit(solution)/shard_map/ppermute | solution.py:487
  63.6 1.8 %collective-permute-start.9 = (f32[24,512]{1,0:T(8,128)S(1)}, f32[24,512]{1,0:T(8,128)S(1)}, u32[]{:S(2)}, u32[]{:S(2)}) collective-permute-start(f32[24,512]{1,0:T(8,128)S(1)} %add.35), channel_id=1, source_target_pairs={{0,192},{8,200},{16,208},{24,216},{32,224},{40,232},{48,240},{56,2... | collective-permute-start | bytes 147464 | tf_op jit(solution)/shard_map/ppermute | solution.py:487
  65.4 0.5 collective-permute-done.10
  66.0 2.9 %collective-permute-done.9 = f32[24,512]{1,0:T(8,128)S(1)} collective-permute-done((f32[24,512]{1,0:T(8,128)S(1)}, f32[24,512]{1,0:T(8,128)S(1)}, u32[]{:S(2)}, u32[]{:S(2)}) %collective-permute-start.9) | collective-permute-done | bytes 49184 | tf_op jit(solution)/shard_map/ppermute | solution.py:487
  68.9 3.0 %collective-permute-start.11 = (f32[128,128]{1,0:T(8,128)S(1)}, f32[128,128]{1,0:T(8,128)S(1)}, u32[]{:S(2)}, u32[]{:S(2)}) collective-permute-start(f32[128,128]{1,0:T(8,128)S(1)} %pad_maximum_fusion.1.taps_ref), channel_id=1, source_target_pairs={{0,4},{1,5},{2,6},{3,7},{4,0},{5,1},{6,2},{7,3},{8,12},{9,13},{10,... | collective-permute-start | bytes 196616 | tf_op jit(solution)/shard_map/ppermute | solution.py:487
  71.9 0.2 collective-permute-start.12
  72.2 3.9 %collective-permute-done.12.other_ref = f32[24,512]{1,0:T(8,128)S(1)} collective-permute-done((f32[24,512]{1,0:T(8,128)S(1)}, f32[24,512]{1,0:T(8,128)S(1)}, u32[]{:S(2)}, u32[]{:S(2)}) %collective-permute-start.12) | collective-permute-done | bytes 49184 | tf_op jit(solution)/shard_map/ppermute | solution.py:487
  76.0 0.0 collective-permute-done.11.next_taps_ref
  76.0 0.8 %final.1 = (f32[128,256]{1,0:T(8,128)}, f32[3,7,512]{2,1,0:T(8,128)}, f32[1,512]{1,0:T(1,128)}) custom-call(f32[128,128]{1,0:T(8,128)S(1)} %pad_maximum_fusion.1.taps_ref, f32[128,128]{1,0:T(8,128)S(1)} %collective-permute-done.11.next_taps_ref, f32[24,512]{1,0:T(8,128)S(1)} %add.37.sums_ref, f32[24,512]{1,0:T(8,128)S(1)} %collective-permute-done.12.other_ref), custom_call_target="tpu_custom_call" | custom-call | tf_op jit(solution)/shard_map/final/pallas_call | solution.py:691
  (22 shorter events, 0.1 us)
Async XLA Ops:
  0.6 13.5 %copy-start = (bf16[512,3,512]{2,0,1:T(8,128)(2,1)S(1)}, bf16[512,3,512]{2,0,1:T(8,128)(2,1)}, u32[]{:S(2)}) copy-start(bf16[512,3,512]{2,0,1:T(8,128)(2,1)} %param.6) | copy-start | bytes 4718596
  0.6 9.6 %copy-start.12 = (s32[64]{0:T(128)S(1)}, s32[64]{0:T(128)}, u32[]{:S(2)}) copy-start(s32[64]{0:T(128)} %lengths_ref.3) | copy-start | bytes 772
  0.7 13.4 %copy-start.1 = (bf16[512,512]{1,0:T(8,128)(2,1)S(1)}, bf16[512,512]{1,0:T(8,128)(2,1)}, u32[]{:S(2)}) copy-start(bf16[512,512]{1,0:T(8,128)(2,1)} %cot_ref.9) | copy-start | bytes 1572868
  0.7 13.4 %copy-start.3 = (f32[7,3,512]{2,0,1:T(8,128)S(1)}, f32[7,3,512]{2,0,1:T(8,128)}, u32[]{:S(2)}) copy-start(f32[7,3,512]{2,0,1:T(8,128)} %param.7) | copy-start | bytes 129028
  4.4 13.7 %collective-permute-start = (bf16[320,512]{1,0:T(8,128)(2,1)}, bf16[320,512]{1,0:T(8,128)(2,1)S(1)}, u32[]{:S(2)}, u32[]{:S(2)}) collective-permute-start(bf16[320,512]{1,0:T(8,128)(2,1)} %get-tuple-element.50.own_up_ref), channel_id=1, source_target_pairs={{0,8},{8,16},{16,24},{24,32},{32,40},{40,48},{48,56},{56,64},{64,7... | collective-permute-start | bytes 983048 | tf_op jit(solution)/shard_map/ppermute | solution.py:538
  8.2 12.7 %collective-permute-start.1 = (bf16[320,512]{1,0:T(8,128)(2,1)}, bf16[320,512]{1,0:T(8,128)(2,1)S(1)}, u32[]{:S(2)}, u32[]{:S(2)}) collective-permute-start(bf16[320,512]{1,0:T(8,128)(2,1)} %get-tuple-element.51), channel_id=1, source_target_pairs={{8,0},{16,8},{24,16},{32,24},{40,32},{48,40},{56,48},{64,56},{72,6... | collective-permute-start | bytes 983048 | tf_op jit(solution)/shard_map/ppermute | solution.py:539
  10.3 0.9 %copy-start.10 = (f32[128,256]{1,0:T(8,128)S(1)}, f32[128,256]{1,0:T(8,128)}, u32[]{:S(2)}) copy-start(f32[128,256]{1,0:T(8,128)} %medium_ref.1) | copy-start | bytes 393220
  14.1 6.8 %copy-start.2 = (bf16[320,512]{1,0:T(8,128)(2,1)S(1)}, bf16[320,512]{1,0:T(8,128)(2,1)}, u32[]{:S(2)}) copy-start(bf16[320,512]{1,0:T(8,128)(2,1)} %get-tuple-element.50.own_up_ref) | copy-start | bytes 983044
  20.9 8.3 %copy-start.11 = (f32[512]{0:T(512)S(1)}, f32[512]{0:T(512)}, u32[]{:S(2)}) copy-start(f32[512]{0:T(512)} %param.9) | copy-start | bytes 6148
  26.4 5.9 %collective-permute-start.2 = (f32[32,128]{1,0:T(8,128)S(1)}, f32[32,128]{1,0:T(8,128)S(1)}, u32[]{:S(2)}, u32[]{:S(2)}) collective-permute-start(f32[32,128]{1,0:T(8,128)S(1)} %get-tuple-element.54), channel_id=1, source_target_pairs={{0,192},{8,200},{16,208},{24,216},{32,224},{40,232},{48,240},{56,2... | collective-permute-start | bytes 49160 | tf_op jit(solution)/shard_map/ppermute | solution.py:487
  31.5 0.8 copy-start.6
  32.3 3.8 %collective-permute-start.3 = (f32[32,128]{1,0:T(8,128)S(1)}, f32[32,128]{1,0:T(8,128)S(1)}, u32[]{:S(2)}, u32[]{:S(2)}) collective-permute-start(f32[32,128]{1,0:T(8,128)S(1)} %add.30), channel_id=1, source_target_pairs={{0,64},{8,72},{16,80},{24,88},{32,96},{40,104},{48,112},{56,120},{... | collective-permute-start | bytes 49160 | tf_op jit(solution)/shard_map/ppermute | solution.py:487
  34.9 0.8 %copy-start.8 = (bf16[2,3,272,128]{3,2,1,0:T(8,128)(2,1)}, bf16[2,3,272,128]{3,2,1,0:T(8,128)(2,1)S(1)}, u32[]{:S(2)}) copy-start(bf16[2,3,272,128]{3,2,1,0:T(8,128)(2,1)S(1)} %get-tuple-element.77.refs_1_) | copy-start | bytes 1253380
  36.1 8.6 %collective-permute-start.4 = (f32[32,128]{1,0:T(8,128)S(1)}, f32[32,128]{1,0:T(8,128)S(1)}, u32[]{:S(2)}, u32[]{:S(2)}) collective-permute-start(f32[32,128]{1,0:T(8,128)S(1)} %add.31), channel_id=1, source_target_pairs={{0,8},{8,0},{16,24},{24,16},{32,40},{40,32},{48,56},{56,48},{64,72... | collective-permute-start | bytes 49160 | tf_op jit(solution)/shard_map/ppermute | solution.py:487
  43.8 0.9 %copy-start.4 = (bf16[2,3,272,256]{3,2,1,0:T(8,128)(2,1)}, bf16[2,3,272,256]{3,2,1,0:T(8,128)(2,1)S(1)}, u32[]{:S(2)}) copy-start(bf16[2,3,272,256]{3,2,1,0:T(8,128)(2,1)S(1)} %get-tuple-element.80.refs_0_) | copy-start | bytes 2506756
  44.7 5.3 %collective-permute-start.5 = (f32[32,512]{1,0:T(8,128)S(1)}, f32[32,512]{1,0:T(8,128)S(1)}, u32[]{:S(2)}, u32[]{:S(2)}) collective-permute-start(f32[32,512]{1,0:T(8,128)S(1)} %pad_maximum_fusion), channel_id=1, source_target_pairs={{0,16},{8,24},{16,0},{24,8},{32,48},{40,56},{48,32},{56,40},{64,80... | collective-permute-start | bytes 196616 | tf_op jit(solution)/shard_map/ppermute | solution.py:487
  44.8 1.0 %copy-start.7 = (bf16[2,3,272,128]{3,2,1,0:T(8,128)(2,1)S(1)}, bf16[2,3,272,128]{3,2,1,0:T(8,128)(2,1)}, u32[]{:S(2)}) copy-start(bf16[2,3,272,128]{3,2,1,0:T(8,128)(2,1)} %copy-done.6) | copy-start | bytes 1253380
  45.8 1.0 %copy-start.9 = (bf16[2,3,272,128]{3,2,1,0:T(8,128)(2,1)S(1)}, bf16[2,3,272,128]{3,2,1,0:T(8,128)(2,1)}, u32[]{:S(2)}) copy-start(bf16[2,3,272,128]{3,2,1,0:T(8,128)(2,1)} %copy-done.8) | copy-start | bytes 1253380
  50.1 7.5 %collective-permute-start.6 = (f32[32,512]{1,0:T(8,128)S(1)}, f32[32,512]{1,0:T(8,128)S(1)}, u32[]{:S(2)}, u32[]{:S(2)}) collective-permute-start(f32[32,512]{1,0:T(8,128)S(1)} %constant_dynamic-update-slice_fusion), channel_id=1, source_target_pairs={{0,56},{8,48},{16,40},{24,32},{32,24},{40,16},{48,8},{56,0},{64,12... | collective-permute-start | bytes 196616 | tf_op jit(solution)/shard_map/ppermute | solution.py:487
  51.8 1.1 %copy-start.5 = (bf16[2,3,272,256]{3,2,1,0:T(8,128)(2,1)S(1)}, bf16[2,3,272,256]{3,2,1,0:T(8,128)(2,1)}, u32[]{:S(2)}) copy-start(bf16[2,3,272,256]{3,2,1,0:T(8,128)(2,1)} %copy-done.4) | copy-start | bytes 2506756
  57.7 1.3 %collective-permute-start.8 = (f32[32,128]{1,0:T(8,128)S(1)}, f32[32,128]{1,0:T(8,128)S(1)}, u32[]{:S(2)}, u32[]{:S(2)}) collective-permute-start(f32[32,128]{1,0:T(8,128)S(1)} %reshape.32), channel_id=1, source_target_pairs={{0,1},{1,0},{2,3},{3,2},{4,5},{5,4},{6,7},{7,6},{8,9},{9,8},{10,11... | collective-permute-start | bytes 49160 | tf_op jit(solution)/shard_map/ppermute | solution.py:487
  57.8 4.2 %collective-permute-start.7 = (f32[24,512]{1,0:T(8,128)S(1)}, f32[24,512]{1,0:T(8,128)S(1)}, u32[]{:S(2)}, u32[]{:S(2)}) collective-permute-start(f32[24,512]{1,0:T(8,128)S(1)} %slice.18), channel_id=1, source_target_pairs={{0,8},{8,0},{16,24},{24,16},{32,40},{40,32},{48,56},{56,48},{64,72... | collective-permute-start | bytes 147464 | tf_op jit(solution)/shard_map/ppermute | solution.py:487
  62.0 4.0 %collective-permute-start.10 = (f32[64,128]{1,0:T(8,128)S(1)}, f32[64,128]{1,0:T(8,128)S(1)}, u32[]{:S(2)}, u32[]{:S(2)}) collective-permute-start(f32[64,128]{1,0:T(8,128)S(1)} %pad_maximum_fusion.2), channel_id=1, source_target_pairs={{0,2},{1,3},{2,0},{3,1},{4,6},{5,7},{6,4},{7,5},{8,10},{9,11},{10,... | collective-permute-start | bytes 98312 | tf_op jit(solution)/shard_map/ppermute | solution.py:487
  63.6 5.3 %collective-permute-start.9 = (f32[24,512]{1,0:T(8,128)S(1)}, f32[24,512]{1,0:T(8,128)S(1)}, u32[]{:S(2)}, u32[]{:S(2)}) collective-permute-start(f32[24,512]{1,0:T(8,128)S(1)} %add.35), channel_id=1, source_target_pairs={{0,192},{8,200},{16,208},{24,216},{32,224},{40,232},{48,240},{56,2... | collective-permute-start | bytes 147464 | tf_op jit(solution)/shard_map/ppermute | solution.py:487
  68.9 7.1 %collective-permute-start.11 = (f32[128,128]{1,0:T(8,128)S(1)}, f32[128,128]{1,0:T(8,128)S(1)}, u32[]{:S(2)}, u32[]{:S(2)}) collective-permute-start(f32[128,128]{1,0:T(8,128)S(1)} %pad_maximum_fusion.1.taps_ref), channel_id=1, source_target_pairs={{0,4},{1,5},{2,6},{3,7},{4,0},{5,1},{6,2},{7,3},{8,12},{9,13},{10,... | collective-permute-start | bytes 196616 | tf_op jit(solution)/shard_map/ppermute | solution.py:487
  71.9 4.1 %collective-permute-start.12 = (f32[24,512]{1,0:T(8,128)S(1)}, f32[24,512]{1,0:T(8,128)S(1)}, u32[]{:S(2)}, u32[]{:S(2)}) collective-permute-start(f32[24,512]{1,0:T(8,128)S(1)} %add.37.sums_ref), channel_id=1, source_target_pairs={{0,64},{8,72},{16,80},{24,88},{32,96},{40,104},{48,112},{56,120},{... | collective-permute-start | bytes 147464 | tf_op jit(solution)/shard_map/ppermute | solution.py:487

commit v5 on v4

--- a/solution.py
+++ b/solution.py
@@ -356,7 +356,7 @@
                 pair = jnp.where(near, pair[:, :128], pair[:, 128:])
                 total = total + pair * keep_r_ref[member, block]
         lined_up = pltpu.roll(total, 1, 1, stride=1, stride_axis=0)
-        sums_ref[pl.ds(tile * PER_TILE + group, 1), :] = jnp.sum(lined_up, axis=0, keepdims=True)
+        sums_ref[pl.ds(group, 1), lanes] = jnp.sum(lined_up, axis=0, keepdims=True)
 
 
 def conv_kernel(
@@ -464,18 +464,27 @@
 
 
 def final_kernel(scale, flip, taps_ref, next_taps_ref, sums_ref, other_ref, medium_ref, short_ref, bias_ref):
-    half = taps_ref.shape[0]
+    half = medium_ref.shape[1] // 2
+
+    def by_group(ref):
+        pieces = [
+            ref[first : first + PER_TILE, tile * TILE : (tile + 1) * TILE]
+            for first in range(0, ref.shape[0], PER_TILE)
+            for tile in range(ref.shape[1] // TILE)
+        ]
+        return jnp.concatenate(pieces, axis=0).T * scale
+
     upper = (lax.axis_index("tp") // flip) % 2 == 1
 
     @pl.when(upper)
     def _():
-        medium_ref[:, pl.ds(half, half)] = taps_ref[...].T * scale
-        medium_ref[:, pl.ds(0, half)] = next_taps_ref[...].T * scale
+        medium_ref[:, pl.ds(half, half)] = by_group(taps_ref)
+        medium_ref[:, pl.ds(0, half)] = by_group(next_taps_ref)
 
     @pl.when(jnp.logical_not(upper))
     def _():
-        medium_ref[:, pl.ds(0, half)] = taps_ref[...].T * scale
-        medium_ref[:, pl.ds(half, half)] = next_taps_ref[...].T * scale
+        medium_ref[:, pl.ds(0, half)] = by_group(taps_ref)
+        medium_ref[:, pl.ds(half, half)] = by_group(next_taps_ref)
 
     total = (sums_ref[...] + other_ref[...]) * scale
     for stream in range(3):
@@ -603,7 +612,7 @@
             shape((2, 512, channels), BF16),
             shape((2, 512, channels), BF16),
             shape((2, 2, STRETCH + EDGE, channels), BF16),
-            shape((groups, LAGS), F32),
+            shape((PER_TILE, channels), F32),
         ],
         scratch_shapes=[
             pltpu.VMEM((TAIL, TILE), BF16),
@@ -671,10 +680,10 @@
     flip = 1
     for step, route in enumerate(routes):
         if step < 2:
-            both = jnp.concatenate([sums, taps.reshape(8, channels)], axis=0)
+            both = jnp.concatenate([sums, taps], axis=0)
             other = along(both, "ctx", route)
             both = both + other
-            sums, taps = both[:24], both[24:].reshape(groups, LAGS)
+            sums, taps = both[:24], both[24:]
         else:
             other = along(sums, "ctx", route)
             next_taps = along(taps, "tp", [(i, i ^ flip) for i in range(lax.axis_size("tp"))])

time: 77.7 us -> 76 us (0.978)
  local copies, waits for them, and re-layouts: 6.54 us -> 0.95 us
  waiting for transfers between devices: 18 us -> 20.9 us
  Pallas kernels: 30.5 us -> 32.1 us
    unnamed x27 -> x15, local copies, waits for them, and re-layouts: 6.5 us -> 0.93 us
    ppermute x11, waiting for transfers between devices: 15.2 us -> 18 us  [along(): return lax.ppermute(block, axis, route)]
    pallas_call x3, Pallas kernels: 9.28 us -> 10.3 us  [convolve(): pl.pallas_call(functools.partial(conv_kernel, members, first), grid=(coun...]
  transfers between devices with their start and end apart: 13 -> 13, of which waited for: 9 -> 9; matrix products, arithmetic and copies ran while one was open for 0% -> 0% of each run, Pallas kernels for 27% -> 29%
where the time goes in v5:
time: 76 us; the launch traced here: 75.9 us
  Pallas kernels  32.1 us (42%)
  starting transfers between devices  20.9 us (28%)
  waiting for transfers between devices  20.9 us (28%)
  local copies, waits for them, and re-layouts  0.95 us (1%)
  between operations  0.95 us (1%)
    ppermute x11, waiting for transfers between devices, along(): return lax.ppermute(block, axis, route)  18 us
    ppermute x11, starting transfers between devices, along(): return lax.ppermute(block, axis, route)  15 us
    pallas_call x3, Pallas kernels, convolve(): pl.pallas_call(functools.partial(conv_kernel, members, first), grid=(coun...  10.3 us
    pallas_call x1, Pallas kernels, shards(): pl.pallas_call(functools.partial(pair_kernel, members), grid=(tiles, 2),...  5.46 us
    pallas_call x2, Pallas kernels, adjoint(): pl.pallas_call(functools.partial(adjoint_kernel, len(pieces)), grid=(2, 2...  5.09 us
    pallas_call x1, Pallas kernels, shards(): pl.pallas_call(functools.partial(own_kernel, members), grid=(tiles,), in_...  3.91 us
    ppermute x1, starting transfers between devices, shards(): lax.ppermute(pay_up, 'ctx', [(i, i + 1) for i in range(members - 1)])  3.83 us
    pallas_call x1, Pallas kernels, shards(): pl.pallas_call(functools.partial(payload_kernel, members), in_specs=[anyw...  3.72 us
  transfers between devices with their start and end apart: 13, of which 9 were waited for; matrix products, arithmetic and copies ran while one was open for 0% of the time, Pallas kernels for 29%

profile of v5, /device:TPU:64, one launch (start us, length us, event | category | flops | bytes accessed | tf_op | source)
XLA Modules:
  0.0 75.9 jit_solution(17058249972772708995)
XLA Ops:
  0.6 0.0 copy-start
  0.6 0.0 copy-start.6
  0.7 0.0 copy-start.1
  0.7 0.0 copy-start.3
  0.7 3.7 %payload_rows.1 = (bf16[320,512]{1,0:T(8,128)(2,1)}, bf16[320,512]{1,0:T(8,128)(2,1)}) custom-call(s32[64]{0:T(128)} %lengths_ref.3, bf16[3,512,512]{2,1,0:T(8,128)(2,1)} %bitcast.6, bf16[512,512]{1,0:T(8,128)(2,1)} %cot_ref.9, f32[3,7,512]{2,1,0:T(8,128)} %bitcast.12), custom_call_target="tpu_custom_call" | custom-call | flops 20000000 | bytes 2800000 | tf_op jit(solution)/shard_map/payload_rows/pallas_call | solution.py:525
  4.4 3.8 %collective-permute-start = (bf16[320,512]{1,0:T(8,128)(2,1)}, bf16[320,512]{1,0:T(8,128)(2,1)S(1)}, u32[]{:S(2)}, u32[]{:S(2)}) collective-permute-start(bf16[320,512]{1,0:T(8,128)(2,1)} %get-tuple-element.50.own_up_ref), channel_id=1, source_target_pairs={{0,8},{8,16},{16,24},{24,32},{32,40},{40,48},{48,56},{56,64},{64,7... | collective-permute-start | bytes 983048 | tf_op jit(solution)/shard_map/ppermute | solution.py:547
  8.2 2.0 %collective-permute-start.1 = (bf16[320,512]{1,0:T(8,128)(2,1)}, bf16[320,512]{1,0:T(8,128)(2,1)S(1)}, u32[]{:S(2)}, u32[]{:S(2)}) collective-permute-start(bf16[320,512]{1,0:T(8,128)(2,1)} %get-tuple-element.51), channel_id=1, source_target_pairs={{8,0},{16,8},{24,16},{32,24},{40,32},{48,40},{56,48},{64,56},{72,6... | collective-permute-start | bytes 983048 | tf_op jit(solution)/shard_map/ppermute | solution.py:548
  10.3 0.0 copy-done.6
  10.3 0.0 copy-start.4
  10.3 0.9 %copy-done.4 = f32[128,256]{1,0:T(8,128)S(1)} copy-done((f32[128,256]{1,0:T(8,128)S(1)}, f32[128,256]{1,0:T(8,128)}, u32[]{:S(2)}) %copy-start.4) | copy-done | bytes 131096
  11.2 2.9 %tables.1 = (bf16[32,128,256]{2,1,0:T(8,128)(2,1)S(1)}, bf16[32,128,256]{2,1,0:T(8,128)(2,1)S(1)}, bf16[2,3,128,256]{3,2,1,0:T(8,128)(2,1)S(1)}, bf16[2,3,128,25...) custom-call(s32[64]{0:T(128)S(1)} %copy-done.6, ...), custom_call_target="tpu_custom_call" | custom-call | flops 20000000 | bytes 7000000 | tf_op jit(solution)/shard_map/tables/pallas_call | solution.py:571
  14.1 0.0 copy-done
  14.1 0.0 copy-done.1
  14.1 0.0 copy-done.3
  14.1 0.0 copy-start.2
  14.1 3.9 %own_rows.1.kvg_ref.refs_4_ = bf16[3,512,512]{2,1,0:T(8,128)(2,1)S(1)} custom-call(s32[64]{0:T(128)S(1)} %copy-done.6, bf16[3,512,512]{2,1,0:T(8,128)(2,1)S(1)} %bitcast.7, bf16[512,512]{1,0:T(8,128)(2,1)S(1)} %copy-done.1, f32[3,7,512]{2,1,0:T(8,128)S(1)} %bitcast.13), custom_call_target="tpu_custom_call" | custom-call | flops 40000000 | bytes 4500000 | tf_op jit(solution)/shard_map/own_rows/pallas_call | solution.py:550
  18.0 0.0 collective-permute-done.up_ref
  18.0 2.8 %collective-permute-done.1.down_ref = bf16[320,512]{1,0:T(8,128)(2,1)S(1)} collective-permute-done((bf16[320,512]{1,0:T(8,128)(2,1)}, bf16[320,512]{1,0:T(8,128)(2,1)S(1)}, u32[]{:S(2)}, u32[]{:S(2)}) %collective-permute-start.1) | collective-permute-done | bytes 327712 | tf_op jit(solution)/shard_map/ppermute | solution.py:548
  20.9 0.0 copy-done.2
  20.9 0.0 copy-start.5
  20.9 5.5 %pair_rows.1 = (bf16[2,512,512]{2,1,0:T(8,128)(2,1)S(1)}, bf16[2,512,512]{2,1,0:T(8,128)(2,1)S(1)}, bf16[2,2,272,512]{3,2,1,0:T(8,128)(2,1)S(1)}, f32[8,512]{1,0:T(8,128)S(1)}) custom-call(bf16[3,512,512]{2,1,0:T(8,128)(2,1)S(1)} %bitcast.8, bf16[3,512,512]{2,1,0:T(8,128)(2,1)S(1)} %own_rows.1.kvg_ref.refs_4_, bf16[512,512]{1,0:T(8,128)(2,1)S(1)} %copy-done.1, ...), custom_call_target="tpu_custom_call" | custom-call | flops 500000000 | bytes 10000000 | tf_op jit(solution)/shard_map/pair_rows/pallas_call | solution.py:606
  26.4 2.8 %collective-permute-start.2 = (f32[8,512]{1,0:T(8,128)S(1)}, f32[8,512]{1,0:T(8,128)S(1)}, u32[]{:S(2)}, u32[]{:S(2)}) collective-permute-start(f32[8,512]{1,0:T(8,128)S(1)} %get-tuple-element.54), channel_id=1, source_target_pairs={{0,192},{8,200},{16,208},{24,216},{32,224},{40,232},{48,240},{56,2... | collective-permute-start | bytes 49160 | tf_op jit(solution)/shard_map/ppermute | solution.py:496
  29.2 0.0 copy-done.5
  29.2 2.5 %conv_rows_0.1 = (bf16[2,3,272,128]{3,2,1,0:T(8,128)(2,1)S(1)}, f32[24,128]{1,0:T(8,128)S(1)}) custom-call(bf16[3,512,512]{2,1,0:T(8,128)(2,1)S(1)} %bitcast.9, bf16[2,512,512]{2,1,0:T(8,128)(2,1)S(1)} %get-tuple-element.71.mixed_ref, bf16[2,512,512]{2,1,0:T(8,128)(2,1)S(1)} %get-tuple-element.72.grads_ref, ...), custom_call_target="tpu_custom_call" | custom-call | flops 100000000 | bytes 2500000 | tf_op jit(solution)/shard_map/conv_rows_0/pallas_call | solution.py:629
  31.8 0.0 collective-permute-done.2
  31.8 0.3 collective-permute-start.3
  32.1 2.5 %conv_rows_1.1 = (bf16[2,3,272,128]{3,2,1,0:T(8,128)(2,1)S(1)}, f32[24,128]{1,0:T(8,128)S(1)}) custom-call(bf16[3,512,512]{2,1,0:T(8,128)(2,1)S(1)} %bitcast.10, bf16[2,512,512]{2,1,0:T(8,128)(2,1)S(1)} %get-tuple-element.71.mixed_ref, bf16[2,512,512]{2,1,0:T(8,128)(2,1)S(1)} %get-tuple-element.72.grads_ref, ...), custom_call_target="tpu_custom_call" | custom-call | flops 100000000 | bytes 2500000 | tf_op jit(solution)/shard_map/conv_rows_1/pallas_call | solution.py:629
  34.6 1.0 %collective-permute-done.3 = f32[8,512]{1,0:T(8,128)S(1)} collective-permute-done((f32[8,512]{1,0:T(8,128)S(1)}, f32[8,512]{1,0:T(8,128)S(1)}, u32[]{:S(2)}, u32[]{:S(2)}) %collective-permute-start.3) | collective-permute-done | bytes 16416 | tf_op jit(solution)/shard_map/ppermute | solution.py:496
  35.6 2.9 %collective-permute-start.4 = (f32[8,512]{1,0:T(8,128)S(1)}, f32[8,512]{1,0:T(8,128)S(1)}, u32[]{:S(2)}, u32[]{:S(2)}) collective-permute-start(f32[8,512]{1,0:T(8,128)S(1)} %add.31), channel_id=1, source_target_pairs={{0,8},{8,0},{16,24},{24,16},{32,40},{40,32},{48,56},{56,48},{64,72... | collective-permute-start | bytes 49160 | tf_op jit(solution)/shard_map/ppermute | solution.py:496
  38.6 5.2 %conv_rows_2.1 = (bf16[2,3,272,256]{3,2,1,0:T(8,128)(2,1)S(1)}, f32[24,256]{1,0:T(8,128)S(1)}) custom-call(bf16[3,512,512]{2,1,0:T(8,128)(2,1)S(1)} %bitcast.11, bf16[2,512,512]{2,1,0:T(8,128)(2,1)S(1)} %get-tuple-element.71.mixed_ref, bf16[2,512,512]{2,1,0:T(8,128)(2,1)S(1)} %get-tuple-element.72.grads_ref, ...), custom_call_target="tpu_custom_call" | custom-call | flops 200000000 | bytes 5000000 | tf_op jit(solution)/shard_map/conv_rows_2/pallas_call | solution.py:629
  43.8 0.0 collective-permute-done.4
  43.8 0.1 collective-permute-start.5
  43.9 2.6 %adjoint_rows_0.1.refs_3_ = bf16[3,512,512]{2,1,0:T(8,128)(2,1)} custom-call(bf16[2,3,272,128]{3,2,1,0:T(8,128)(2,1)S(1)} %get-tuple-element.76.refs_0_, bf16[2,3,272,128]{3,2,1,0:T(8,128)(2,1)S(1)} %get-tuple-element.77.refs_1_, f32[3,7,512]{2,1,0:T(8,128)S(1)} %bitcast.18, f32[2,6,256,128]{3,2,1,0:T(8,128)S(1)} %get-tuple-element.62.shifted_ref.refs_3_.refs_2_, ...), custom_call_target="tpu_custom_call" | custom-call | flops 20000000 | bytes 4000000 | tf_op jit(solution)/shard_map/adjoint_rows_0/pallas_call | solution.py:662
  46.6 2.5 %collective-permute-done.5 = f32[32,512]{1,0:T(8,128)S(1)} collective-permute-done((f32[32,512]{1,0:T(8,128)S(1)}, f32[32,512]{1,0:T(8,128)S(1)}, u32[]{:S(2)}, u32[]{:S(2)}) %collective-permute-start.5) | collective-permute-done | bytes 65568 | tf_op jit(solution)/shard_map/ppermute | solution.py:496
  49.1 1.7 %collective-permute-start.6 = (f32[32,512]{1,0:T(8,128)S(1)}, f32[32,512]{1,0:T(8,128)S(1)}, u32[]{:S(2)}, u32[]{:S(2)}) collective-permute-start(f32[32,512]{1,0:T(8,128)S(1)} %constant_dynamic-update-slice_fusion), channel_id=1, source_target_pairs={{0,56},{8,48},{16,40},{24,32},{32,24},{40,16},{48,8},{56,0},{64,12... | collective-permute-start | bytes 196616 | tf_op jit(solution)/shard_map/ppermute | solution.py:496
  50.8 2.5 %adjoint_rows_2.1 = bf16[3,512,512]{2,1,0:T(8,128)(2,1)} custom-call(bf16[2,3,272,256]{3,2,1,0:T(8,128)(2,1)S(1)} %get-tuple-element.80.refs_0_, f32[3,7,512]{2,1,0:T(8,128)S(1)} %bitcast.19, f32[2,6,256,128]{3,2,1,0:T(8,128)S(1)} %get-tuple-element.62.shifted_ref.refs_3_.refs_2_, ...), custom_call_target="tpu_custom_call", output_to_operand_aliasing={{}: (3, {})} | custom-call | flops 20000000 | bytes 4000000 | tf_op jit(solution)/shard_map/adjoint_rows_2/pallas_call | solution.py:662
  53.3 3.4 %collective-permute-done.6 = f32[32,512]{1,0:T(8,128)S(1)} collective-permute-done((f32[32,512]{1,0:T(8,128)S(1)}, f32[32,512]{1,0:T(8,128)S(1)}, u32[]{:S(2)}, u32[]{:S(2)}) %collective-permute-start.6) | collective-permute-done | bytes 65568 | tf_op jit(solution)/shard_map/ppermute | solution.py:496
  56.7 0.1 collective-permute-start.8
  56.8 0.1 collective-permute-start.7
  56.9 1.1 %collective-permute-done.8 = f32[8,512]{1,0:T(8,128)S(1)} collective-permute-done((f32[8,512]{1,0:T(8,128)S(1)}, f32[8,512]{1,0:T(8,128)S(1)}, u32[]{:S(2)}, u32[]{:S(2)}) %collective-permute-start.8) | collective-permute-done | bytes 16416 | tf_op jit(solution)/shard_map/ppermute | solution.py:496
  58.0 3.0 %collective-permute-done.7 = f32[24,512]{1,0:T(8,128)S(1)} collective-permute-done((f32[24,512]{1,0:T(8,128)S(1)}, f32[24,512]{1,0:T(8,128)S(1)}, u32[]{:S(2)}, u32[]{:S(2)}) %collective-permute-start.7) | collective-permute-done | bytes 49184 | tf_op jit(solution)/shard_map/ppermute | solution.py:496
  61.0 1.7 %collective-permute-start.10 = (f32[16,512]{1,0:T(8,128)S(1)}, f32[16,512]{1,0:T(8,128)S(1)}, u32[]{:S(2)}, u32[]{:S(2)}) collective-permute-start(f32[16,512]{1,0:T(8,128)S(1)} %pad_maximum_fusion.2), channel_id=1, source_target_pairs={{0,2},{1,3},{2,0},{3,1},{4,6},{5,7},{6,4},{7,5},{8,10},{9,11},{10,... | collective-permute-start | bytes 98312 | tf_op jit(solution)/shard_map/ppermute | solution.py:496
  62.7 2.3 %collective-permute-start.9 = (f32[24,512]{1,0:T(8,128)S(1)}, f32[24,512]{1,0:T(8,128)S(1)}, u32[]{:S(2)}, u32[]{:S(2)}) collective-permute-start(f32[24,512]{1,0:T(8,128)S(1)} %add.35), channel_id=1, source_target_pairs={{0,192},{8,200},{16,208},{24,216},{32,224},{40,232},{48,240},{56,2... | collective-permute-start | bytes 147464 | tf_op jit(solution)/shard_map/ppermute | solution.py:496
  65.0 0.1 collective-permute-done.10
  65.0 2.9 %collective-permute-done.9 = f32[24,512]{1,0:T(8,128)S(1)} collective-permute-done((f32[24,512]{1,0:T(8,128)S(1)}, f32[24,512]{1,0:T(8,128)S(1)}, u32[]{:S(2)}, u32[]{:S(2)}) %collective-permute-start.9) | collective-permute-done | bytes 49184 | tf_op jit(solution)/shard_map/ppermute | solution.py:496
  68.0 3.0 %collective-permute-start.11 = (f32[32,512]{1,0:T(8,128)S(1)}, f32[32,512]{1,0:T(8,128)S(1)}, u32[]{:S(2)}, u32[]{:S(2)}) collective-permute-start(f32[32,512]{1,0:T(8,128)S(1)} %pad_maximum_fusion.1.taps_ref), channel_id=1, source_target_pairs={{0,4},{1,5},{2,6},{3,7},{4,0},{5,1},{6,2},{7,3},{8,12},{9,13},{10,... | collective-permute-start | bytes 196616 | tf_op jit(solution)/shard_map/ppermute | solution.py:496
  71.0 0.0 collective-permute-start.12
  71.0 4.1 %collective-permute-done.12.other_ref = f32[24,512]{1,0:T(8,128)S(1)} collective-permute-done((f32[24,512]{1,0:T(8,128)S(1)}, f32[24,512]{1,0:T(8,128)S(1)}, u32[]{:S(2)}, u32[]{:S(2)}) %collective-permute-start.12) | collective-permute-done | bytes 49184 | tf_op jit(solution)/shard_map/ppermute | solution.py:496
  75.1 0.0 collective-permute-done.11.next_taps_ref
  75.1 0.8 %final.1 = (f32[128,256]{1,0:T(8,128)}, f32[3,7,512]{2,1,0:T(8,128)}, f32[1,512]{1,0:T(1,128)}) custom-call(f32[32,512]{1,0:T(8,128)S(1)} %pad_maximum_fusion.1.taps_ref, f32[32,512]{1,0:T(8,128)S(1)} %collective-permute-done.11.next_taps_ref, f32[24,512]{1,0:T(8,128)S(1)} %add.37.sums_ref, f32[24,512]{1,0:T(8,128)S(1)} %collective-permute-done.12.other_ref), custom_call_target="tpu_custom_call" | custom-call | tf_op jit(solution)/shard_map/final/pallas_call | solution.py:700
  (18 shorter events, 0.1 us)
Async XLA Ops:
  0.6 13.4 %copy-start = (bf16[512,3,512]{2,0,1:T(8,128)(2,1)S(1)}, bf16[512,3,512]{2,0,1:T(8,128)(2,1)}, u32[]{:S(2)}) copy-start(bf16[512,3,512]{2,0,1:T(8,128)(2,1)} %param.6) | copy-start | bytes 4718596
  0.6 9.6 %copy-start.6 = (s32[64]{0:T(128)S(1)}, s32[64]{0:T(128)}, u32[]{:S(2)}) copy-start(s32[64]{0:T(128)} %lengths_ref.3) | copy-start | bytes 772
  0.7 13.4 %copy-start.1 = (bf16[512,512]{1,0:T(8,128)(2,1)S(1)}, bf16[512,512]{1,0:T(8,128)(2,1)}, u32[]{:S(2)}) copy-start(bf16[512,512]{1,0:T(8,128)(2,1)} %cot_ref.9) | copy-start | bytes 1572868
  0.7 13.4 %copy-start.3 = (f32[7,3,512]{2,0,1:T(8,128)S(1)}, f32[7,3,512]{2,0,1:T(8,128)}, u32[]{:S(2)}) copy-start(f32[7,3,512]{2,0,1:T(8,128)} %param.7) | copy-start | bytes 129028
  4.4 13.6 %collective-permute-start = (bf16[320,512]{1,0:T(8,128)(2,1)}, bf16[320,512]{1,0:T(8,128)(2,1)S(1)}, u32[]{:S(2)}, u32[]{:S(2)}) collective-permute-start(bf16[320,512]{1,0:T(8,128)(2,1)} %get-tuple-element.50.own_up_ref), channel_id=1, source_target_pairs={{0,8},{8,16},{16,24},{24,32},{32,40},{40,48},{48,56},{56,64},{64,7... | collective-permute-start | bytes 983048 | tf_op jit(solution)/shard_map/ppermute | solution.py:547
  8.2 12.7 %collective-permute-start.1 = (bf16[320,512]{1,0:T(8,128)(2,1)}, bf16[320,512]{1,0:T(8,128)(2,1)S(1)}, u32[]{:S(2)}, u32[]{:S(2)}) collective-permute-start(bf16[320,512]{1,0:T(8,128)(2,1)} %get-tuple-element.51), channel_id=1, source_target_pairs={{8,0},{16,8},{24,16},{32,24},{40,32},{48,40},{56,48},{64,56},{72,6... | collective-permute-start | bytes 983048 | tf_op jit(solution)/shard_map/ppermute | solution.py:548
  10.3 0.9 %copy-start.4 = (f32[128,256]{1,0:T(8,128)S(1)}, f32[128,256]{1,0:T(8,128)}, u32[]{:S(2)}) copy-start(f32[128,256]{1,0:T(8,128)} %medium_ref.1) | copy-start | bytes 393220
  14.1 6.8 %copy-start.2 = (bf16[320,512]{1,0:T(8,128)(2,1)S(1)}, bf16[320,512]{1,0:T(8,128)(2,1)}, u32[]{:S(2)}) copy-start(bf16[320,512]{1,0:T(8,128)(2,1)} %get-tuple-element.50.own_up_ref) | copy-start | bytes 983044
  20.9 8.3 %copy-start.5 = (f32[512]{0:T(512)S(1)}, f32[512]{0:T(512)}, u32[]{:S(2)}) copy-start(f32[512]{0:T(512)} %param.9) | copy-start | bytes 6148
  26.4 5.4 %collective-permute-start.2 = (f32[8,512]{1,0:T(8,128)S(1)}, f32[8,512]{1,0:T(8,128)S(1)}, u32[]{:S(2)}, u32[]{:S(2)}) collective-permute-start(f32[8,512]{1,0:T(8,128)S(1)} %get-tuple-element.54), channel_id=1, source_target_pairs={{0,192},{8,200},{16,208},{24,216},{32,224},{40,232},{48,240},{56,2... | collective-permute-start | bytes 49160 | tf_op jit(solution)/shard_map/ppermute | solution.py:496
  31.8 3.8 %collective-permute-start.3 = (f32[8,512]{1,0:T(8,128)S(1)}, f32[8,512]{1,0:T(8,128)S(1)}, u32[]{:S(2)}, u32[]{:S(2)}) collective-permute-start(f32[8,512]{1,0:T(8,128)S(1)} %add.30), channel_id=1, source_target_pairs={{0,64},{8,72},{16,80},{24,88},{32,96},{40,104},{48,112},{56,120},{... | collective-permute-start | bytes 49160 | tf_op jit(solution)/shard_map/ppermute | solution.py:496
  35.6 8.2 %collective-permute-start.4 = (f32[8,512]{1,0:T(8,128)S(1)}, f32[8,512]{1,0:T(8,128)S(1)}, u32[]{:S(2)}, u32[]{:S(2)}) collective-permute-start(f32[8,512]{1,0:T(8,128)S(1)} %add.31), channel_id=1, source_target_pairs={{0,8},{8,0},{16,24},{24,16},{32,40},{40,32},{48,56},{56,48},{64,72... | collective-permute-start | bytes 49160 | tf_op jit(solution)/shard_map/ppermute | solution.py:496
  43.8 5.3 %collective-permute-start.5 = (f32[32,512]{1,0:T(8,128)S(1)}, f32[32,512]{1,0:T(8,128)S(1)}, u32[]{:S(2)}, u32[]{:S(2)}) collective-permute-start(f32[32,512]{1,0:T(8,128)S(1)} %pad_maximum_fusion), channel_id=1, source_target_pairs={{0,16},{8,24},{16,0},{24,8},{32,48},{40,56},{48,32},{56,40},{64,80... | collective-permute-start | bytes 196616 | tf_op jit(solution)/shard_map/ppermute | solution.py:496
  49.1 7.5 %collective-permute-start.6 = (f32[32,512]{1,0:T(8,128)S(1)}, f32[32,512]{1,0:T(8,128)S(1)}, u32[]{:S(2)}, u32[]{:S(2)}) collective-permute-start(f32[32,512]{1,0:T(8,128)S(1)} %constant_dynamic-update-slice_fusion), channel_id=1, source_target_pairs={{0,56},{8,48},{16,40},{24,32},{32,24},{40,16},{48,8},{56,0},{64,12... | collective-permute-start | bytes 196616 | tf_op jit(solution)/shard_map/ppermute | solution.py:496
  56.7 1.3 %collective-permute-start.8 = (f32[8,512]{1,0:T(8,128)S(1)}, f32[8,512]{1,0:T(8,128)S(1)}, u32[]{:S(2)}, u32[]{:S(2)}) collective-permute-start(f32[8,512]{1,0:T(8,128)S(1)} %slice.19), channel_id=1, source_target_pairs={{0,1},{1,0},{2,3},{3,2},{4,5},{5,4},{6,7},{7,6},{8,9},{9,8},{10,11... | collective-permute-start | bytes 49160 | tf_op jit(solution)/shard_map/ppermute | solution.py:496
  56.8 4.2 %collective-permute-start.7 = (f32[24,512]{1,0:T(8,128)S(1)}, f32[24,512]{1,0:T(8,128)S(1)}, u32[]{:S(2)}, u32[]{:S(2)}) collective-permute-start(f32[24,512]{1,0:T(8,128)S(1)} %slice.18), channel_id=1, source_target_pairs={{0,8},{8,0},{16,24},{24,16},{32,40},{40,32},{48,56},{56,48},{64,72... | collective-permute-start | bytes 147464 | tf_op jit(solution)/shard_map/ppermute | solution.py:496
  61.0 4.0 %collective-permute-start.10 = (f32[16,512]{1,0:T(8,128)S(1)}, f32[16,512]{1,0:T(8,128)S(1)}, u32[]{:S(2)}, u32[]{:S(2)}) collective-permute-start(f32[16,512]{1,0:T(8,128)S(1)} %pad_maximum_fusion.2), channel_id=1, source_target_pairs={{0,2},{1,3},{2,0},{3,1},{4,6},{5,7},{6,4},{7,5},{8,10},{9,11},{10,... | collective-permute-start | bytes 98312 | tf_op jit(solution)/shard_map/ppermute | solution.py:496
  62.7 5.3 %collective-permute-start.9 = (f32[24,512]{1,0:T(8,128)S(1)}, f32[24,512]{1,0:T(8,128)S(1)}, u32[]{:S(2)}, u32[]{:S(2)}) collective-permute-start(f32[24,512]{1,0:T(8,128)S(1)} %add.35), channel_id=1, source_target_pairs={{0,192},{8,200},{16,208},{24,216},{32,224},{40,232},{48,240},{56,2... | collective-permute-start | bytes 147464 | tf_op jit(solution)/shard_map/ppermute | solution.py:496
  68.0 7.1 %collective-permute-start.11 = (f32[32,512]{1,0:T(8,128)S(1)}, f32[32,512]{1,0:T(8,128)S(1)}, u32[]{:S(2)}, u32[]{:S(2)}) collective-permute-start(f32[32,512]{1,0:T(8,128)S(1)} %pad_maximum_fusion.1.taps_ref), channel_id=1, source_target_pairs={{0,4},{1,5},{2,6},{3,7},{4,0},{5,1},{6,2},{7,3},{8,12},{9,13},{10,... | collective-permute-start | bytes 196616 | tf_op jit(solution)/shard_map/ppermute | solution.py:496
  71.0 4.1 %collective-permute-start.12 = (f32[24,512]{1,0:T(8,128)S(1)}, f32[24,512]{1,0:T(8,128)S(1)}, u32[]{:S(2)}, u32[]{:S(2)}) collective-permute-start(f32[24,512]{1,0:T(8,128)S(1)} %add.37.sums_ref), channel_id=1, source_target_pairs={{0,64},{8,72},{16,80},{24,88},{32,96},{40,104},{48,112},{56,120},{... | collective-permute-start | bytes 147464 | tf_op jit(solution)/shard_map/ppermute | solution.py:496

commit v6 on v5

--- a/solution.py
+++ b/solution.py
@@ -568,6 +568,7 @@
     )(doc_lengths, streams, cotangent, weights)
 
     groups = channels // GROUP
+    medium_filter, doc_lengths, kvg = lax.optimization_barrier((medium_filter, doc_lengths, kvg))
     tables = pl.pallas_call(
         functools.partial(tables_kernel, members),
         grid=(tiles,),

time: 76 us -> 76.1 us (level)
  waiting for transfers between devices: 20.9 us -> 22.4 us
  local copies, waits for them, and re-layouts: 0.95 us -> 0.06 us
    unnamed x15, local copies, waits for them, and re-layouts: 0.93 us -> 0.04 us
    ppermute x1, waiting for transfers between devices: 2.85 us -> 3.72 us  [shards(): lax.ppermute(pay_down, 'ctx', [(i + 1, i) for i in range(members - 1)])]
  transfers between devices with their start and end apart: 13 -> 13, of which waited for: 9 -> 8; matrix products, arithmetic and copies ran while one was open for 0% -> 0% of each run, Pallas kernels for 29% -> 29%
where the time goes in v6:
time: 76.1 us; the launch traced here: 76 us
  Pallas kernels  32.2 us (42%)
  waiting for transfers between devices  22.4 us (29%)
  starting transfers between devices  20.4 us (27%)
  between operations  0.96 us (1%)
    ppermute x11, waiting for transfers between devices, along(): return lax.ppermute(block, axis, route)  18.6 us
    ppermute x11, starting transfers between devices, along(): return lax.ppermute(block, axis, route)  14.4 us
    pallas_call x3, Pallas kernels, convolve(): pl.pallas_call(functools.partial(conv_kernel, members, first), grid=(coun...  10.3 us
    pallas_call x1, Pallas kernels, shards(): pl.pallas_call(functools.partial(pair_kernel, members), grid=(tiles, 2),...  5.45 us
    pallas_call x2, Pallas kernels, adjoint(): pl.pallas_call(functools.partial(adjoint_kernel, len(pieces)), grid=(2, 2...  5.09 us
    pallas_call x1, Pallas kernels, shards(): pl.pallas_call(functools.partial(own_kernel, members), grid=(tiles,), in_...  3.91 us
    ppermute x1, starting transfers between devices, shards(): lax.ppermute(pay_up, 'ctx', [(i, i + 1) for i in range(members - 1)])  3.83 us
    ppermute x1, waiting for transfers between devices, shards(): lax.ppermute(pay_down, 'ctx', [(i + 1, i) for i in range(members - 1)])  3.72 us
  transfers between devices with their start and end apart: 13, of which 8 were waited for; matrix products, arithmetic and copies ran while one was open for 0% of the time, Pallas kernels for 29%

profile of v6, /device:TPU:64, one launch (start us, length us, event | category | flops | bytes accessed | tf_op | source)
XLA Modules:
  0.0 76.0 jit_solution(3688980554098149615)
XLA Ops:
  0.6 0.0 copy-start
  0.6 0.0 copy-start.6
  0.7 0.0 copy-start.1
  0.7 0.0 copy-start.3
  0.7 3.7 %payload_rows.1 = (bf16[320,512]{1,0:T(8,128)(2,1)}, bf16[320,512]{1,0:T(8,128)(2,1)}) custom-call(s32[64]{0:T(128)} %lengths_ref.2, bf16[3,512,512]{2,1,0:T(8,128)(2,1)} %bitcast.6, bf16[512,512]{1,0:T(8,128)(2,1)} %cot_ref.9, f32[3,7,512]{2,1,0:T(8,128)} %bitcast.12), custom_call_target="tpu_custom_call" | custom-call | flops 20000000 | bytes 2800000 | tf_op jit(solution)/shard_map/payload_rows/pallas_call | solution.py:525
  4.4 3.8 %collective-permute-start = (bf16[320,512]{1,0:T(8,128)(2,1)}, bf16[320,512]{1,0:T(8,128)(2,1)S(1)}, u32[]{:S(2)}, u32[]{:S(2)}) collective-permute-start(bf16[320,512]{1,0:T(8,128)(2,1)} %get-tuple-element.54.own_up_ref), channel_id=1, source_target_pairs={{0,8},{8,16},{16,24},{24,32},{32,40},{40,48},{48,56},{56,64},{64,7... | collective-permute-start | bytes 983048 | tf_op jit(solution)/shard_map/ppermute | solution.py:547
  8.2 0.0 copy-start.4
  8.2 0.0 copy-start.2
  8.3 2.1 %collective-permute-start.1 = (bf16[320,512]{1,0:T(8,128)(2,1)}, bf16[320,512]{1,0:T(8,128)(2,1)S(1)}, u32[]{:S(2)}, u32[]{:S(2)}) collective-permute-start(bf16[320,512]{1,0:T(8,128)(2,1)} %get-tuple-element.55), channel_id=1, source_target_pairs={{8,0},{16,8},{24,16},{32,24},{40,32},{48,40},{56,48},{64,56},{72,6... | collective-permute-start | bytes 983048 | tf_op jit(solution)/shard_map/ppermute | solution.py:548
  10.4 0.0 copy-done
  10.4 0.0 copy-done.6
  10.4 0.0 copy-done.1
  10.4 0.0 copy-done.3
  10.4 3.9 %own_rows.1.kvg_ref.refs_4_ = bf16[3,512,512]{2,1,0:T(8,128)(2,1)S(1)} custom-call(s32[64]{0:T(128)S(1)} %copy-done.6, bf16[3,512,512]{2,1,0:T(8,128)(2,1)S(1)} %bitcast.7, bf16[512,512]{1,0:T(8,128)(2,1)S(1)} %copy-done.1, f32[3,7,512]{2,1,0:T(8,128)S(1)} %bitcast.13), custom_call_target="tpu_custom_call" | custom-call | flops 40000000 | bytes 4500000 | tf_op jit(solution)/shard_map/own_rows/pallas_call | solution.py:550
  14.4 0.0 copy-done.4
  14.4 2.9 %tables.1 = (bf16[32,128,256]{2,1,0:T(8,128)(2,1)S(1)}, bf16[32,128,256]{2,1,0:T(8,128)(2,1)S(1)}, bf16[2,3,128,256]{3,2,1,0:T(8,128)(2,1)S(1)}, bf16[2,3,128,25...) custom-call(s32[64]{0:T(128)S(1)} %copy-done.6, ...), custom_call_target="tpu_custom_call" | custom-call | flops 20000000 | bytes 7000000 | tf_op jit(solution)/shard_map/tables/pallas_call | solution.py:572
  17.3 0.0 collective-permute-done.up_ref
  17.3 3.7 %collective-permute-done.1.down_ref = bf16[320,512]{1,0:T(8,128)(2,1)S(1)} collective-permute-done((bf16[320,512]{1,0:T(8,128)(2,1)}, bf16[320,512]{1,0:T(8,128)(2,1)S(1)}, u32[]{:S(2)}, u32[]{:S(2)}) %collective-permute-start.1) | collective-permute-done | bytes 327712 | tf_op jit(solution)/shard_map/ppermute | solution.py:548
  21.1 0.0 copy-done.2
  21.1 0.0 copy-start.5
  21.1 5.5 %pair_rows.1 = (bf16[2,512,512]{2,1,0:T(8,128)(2,1)S(1)}, bf16[2,512,512]{2,1,0:T(8,128)(2,1)S(1)}, bf16[2,2,272,512]{3,2,1,0:T(8,128)(2,1)S(1)}, f32[8,512]{1,0:T(8,128)S(1)}) custom-call(bf16[3,512,512]{2,1,0:T(8,128)(2,1)S(1)} %bitcast.8, bf16[3,512,512]{2,1,0:T(8,128)(2,1)S(1)} %own_rows.1.kvg_ref.refs_4_, bf16[512,512]{1,0:T(8,128)(2,1)S(1)} %copy-done.1, ...), custom_call_target="tpu_custom_call" | custom-call | flops 500000000 | bytes 10000000 | tf_op jit(solution)/shard_map/pair_rows/pallas_call | solution.py:607
  26.5 2.8 %collective-permute-start.2 = (f32[8,512]{1,0:T(8,128)S(1)}, f32[8,512]{1,0:T(8,128)S(1)}, u32[]{:S(2)}, u32[]{:S(2)}) collective-permute-start(f32[8,512]{1,0:T(8,128)S(1)} %get-tuple-element.60), channel_id=1, source_target_pairs={{0,192},{8,200},{16,208},{24,216},{32,224},{40,232},{48,240},{56,2... | collective-permute-start | bytes 49160 | tf_op jit(solution)/shard_map/ppermute | solution.py:496
  29.4 0.0 copy-done.5
  29.4 2.5 %conv_rows_0.1 = (bf16[2,3,272,128]{3,2,1,0:T(8,128)(2,1)S(1)}, f32[24,128]{1,0:T(8,128)S(1)}) custom-call(bf16[3,512,512]{2,1,0:T(8,128)(2,1)S(1)} %bitcast.9, bf16[2,512,512]{2,1,0:T(8,128)(2,1)S(1)} %get-tuple-element.77.mixed_ref, bf16[2,512,512]{2,1,0:T(8,128)(2,1)S(1)} %get-tuple-element.78.grads_ref, ...), custom_call_target="tpu_custom_call" | custom-call | flops 100000000 | bytes 2500000 | tf_op jit(solution)/shard_map/conv_rows_0/pallas_call | solution.py:630
  31.9 0.0 collective-permute-done.2
  31.9 0.3 collective-permute-start.3
  32.3 2.5 %conv_rows_1.1 = (bf16[2,3,272,128]{3,2,1,0:T(8,128)(2,1)S(1)}, f32[24,128]{1,0:T(8,128)S(1)}) custom-call(bf16[3,512,512]{2,1,0:T(8,128)(2,1)S(1)} %bitcast.10, bf16[2,512,512]{2,1,0:T(8,128)(2,1)S(1)} %get-tuple-element.77.mixed_ref, bf16[2,512,512]{2,1,0:T(8,128)(2,1)S(1)} %get-tuple-element.78.grads_ref, ...), custom_call_target="tpu_custom_call" | custom-call | flops 100000000 | bytes 2500000 | tf_op jit(solution)/shard_map/conv_rows_1/pallas_call | solution.py:630
  34.8 1.0 %collective-permute-done.3 = f32[8,512]{1,0:T(8,128)S(1)} collective-permute-done((f32[8,512]{1,0:T(8,128)S(1)}, f32[8,512]{1,0:T(8,128)S(1)}, u32[]{:S(2)}, u32[]{:S(2)}) %collective-permute-start.3) | collective-permute-done | bytes 16416 | tf_op jit(solution)/shard_map/ppermute | solution.py:496
  35.8 2.9 %collective-permute-start.4 = (f32[8,512]{1,0:T(8,128)S(1)}, f32[8,512]{1,0:T(8,128)S(1)}, u32[]{:S(2)}, u32[]{:S(2)}) collective-permute-start(f32[8,512]{1,0:T(8,128)S(1)} %add.31), channel_id=1, source_target_pairs={{0,8},{8,0},{16,24},{24,16},{32,40},{40,32},{48,56},{56,48},{64,72... | collective-permute-start | bytes 49160 | tf_op jit(solution)/shard_map/ppermute | solution.py:496
  38.7 5.2 %conv_rows_2.1 = (bf16[2,3,272,256]{3,2,1,0:T(8,128)(2,1)S(1)}, f32[24,256]{1,0:T(8,128)S(1)}) custom-call(bf16[3,512,512]{2,1,0:T(8,128)(2,1)S(1)} %bitcast.11, bf16[2,512,512]{2,1,0:T(8,128)(2,1)S(1)} %get-tuple-element.77.mixed_ref, bf16[2,512,512]{2,1,0:T(8,128)(2,1)S(1)} %get-tuple-element.78.grads_ref, ...), custom_call_target="tpu_custom_call" | custom-call | flops 200000000 | bytes 5000000 | tf_op jit(solution)/shard_map/conv_rows_2/pallas_call | solution.py:630
  43.9 0.0 collective-permute-done.4
  44.0 0.1 collective-permute-start.5
  44.1 2.6 %adjoint_rows_0.1.refs_3_ = bf16[3,512,512]{2,1,0:T(8,128)(2,1)} custom-call(bf16[2,3,272,128]{3,2,1,0:T(8,128)(2,1)S(1)} %get-tuple-element.82.refs_0_, bf16[2,3,272,128]{3,2,1,0:T(8,128)(2,1)S(1)} %get-tuple-element.83.refs_1_, f32[3,7,512]{2,1,0:T(8,128)S(1)} %bitcast.18, f32[2,6,256,128]{3,2,1,0:T(8,128)S(1)} %get-tuple-element.68.shifted_ref.refs_3_.refs_2_, ...), custom_call_target="tpu_custom_call" | custom-call | flops 20000000 | bytes 4000000 | tf_op jit(solution)/shard_map/adjoint_rows_0/pallas_call | solution.py:663
  46.7 2.5 %collective-permute-done.5 = f32[32,512]{1,0:T(8,128)S(1)} collective-permute-done((f32[32,512]{1,0:T(8,128)S(1)}, f32[32,512]{1,0:T(8,128)S(1)}, u32[]{:S(2)}, u32[]{:S(2)}) %collective-permute-start.5) | collective-permute-done | bytes 65568 | tf_op jit(solution)/shard_map/ppermute | solution.py:496
  49.3 1.1 %collective-permute-start.6 = (f32[32,512]{1,0:T(8,128)S(1)}, f32[32,512]{1,0:T(8,128)S(1)}, u32[]{:S(2)}, u32[]{:S(2)}) collective-permute-start(f32[32,512]{1,0:T(8,128)S(1)} %constant_dynamic-update-slice_fusion), channel_id=1, source_target_pairs={{0,56},{8,48},{16,40},{24,32},{32,24},{40,16},{48,8},{56,0},{64,12... | collective-permute-start | bytes 196616 | tf_op jit(solution)/shard_map/ppermute | solution.py:496
  50.4 2.5 %adjoint_rows_2.1 = bf16[3,512,512]{2,1,0:T(8,128)(2,1)} custom-call(bf16[2,3,272,256]{3,2,1,0:T(8,128)(2,1)S(1)} %get-tuple-element.86.refs_0_, f32[3,7,512]{2,1,0:T(8,128)S(1)} %bitcast.19, f32[2,6,256,128]{3,2,1,0:T(8,128)S(1)} %get-tuple-element.68.shifted_ref.refs_3_.refs_2_, ...), custom_call_target="tpu_custom_call", output_to_operand_aliasing={{}: (3, {})} | custom-call | flops 20000000 | bytes 4000000 | tf_op jit(solution)/shard_map/adjoint_rows_2/pallas_call | solution.py:663
  52.8 4.0 %collective-permute-done.6 = f32[32,512]{1,0:T(8,128)S(1)} collective-permute-done((f32[32,512]{1,0:T(8,128)S(1)}, f32[32,512]{1,0:T(8,128)S(1)}, u32[]{:S(2)}, u32[]{:S(2)}) %collective-permute-start.6) | collective-permute-done | bytes 65568 | tf_op jit(solution)/shard_map/ppermute | solution.py:496
  56.9 0.1 collective-permute-start.8
  57.0 0.1 collective-permute-start.7
  57.1 1.1 %collective-permute-done.8 = f32[8,512]{1,0:T(8,128)S(1)} collective-permute-done((f32[8,512]{1,0:T(8,128)S(1)}, f32[8,512]{1,0:T(8,128)S(1)}, u32[]{:S(2)}, u32[]{:S(2)}) %collective-permute-start.8) | collective-permute-done | bytes 16416 | tf_op jit(solution)/shard_map/ppermute | solution.py:496
  58.2 3.0 %collective-permute-done.7 = f32[24,512]{1,0:T(8,128)S(1)} collective-permute-done((f32[24,512]{1,0:T(8,128)S(1)}, f32[24,512]{1,0:T(8,128)S(1)}, u32[]{:S(2)}, u32[]{:S(2)}) %collective-permute-start.7) | collective-permute-done | bytes 49184 | tf_op jit(solution)/shard_map/ppermute | solution.py:496
  61.2 1.7 %collective-permute-start.10 = (f32[16,512]{1,0:T(8,128)S(1)}, f32[16,512]{1,0:T(8,128)S(1)}, u32[]{:S(2)}, u32[]{:S(2)}) collective-permute-start(f32[16,512]{1,0:T(8,128)S(1)} %pad_maximum_fusion.2), channel_id=1, source_target_pairs={{0,2},{1,3},{2,0},{3,1},{4,6},{5,7},{6,4},{7,5},{8,10},{9,11},{10,... | collective-permute-start | bytes 98312 | tf_op jit(solution)/shard_map/ppermute | solution.py:496
  62.8 2.3 %collective-permute-start.9 = (f32[24,512]{1,0:T(8,128)S(1)}, f32[24,512]{1,0:T(8,128)S(1)}, u32[]{:S(2)}, u32[]{:S(2)}) collective-permute-start(f32[24,512]{1,0:T(8,128)S(1)} %add.35), channel_id=1, source_target_pairs={{0,192},{8,200},{16,208},{24,216},{32,224},{40,232},{48,240},{56,2... | collective-permute-start | bytes 147464 | tf_op jit(solution)/shard_map/ppermute | solution.py:496
  65.1 0.0 collective-permute-done.10
  65.2 2.9 %collective-permute-done.9 = f32[24,512]{1,0:T(8,128)S(1)} collective-permute-done((f32[24,512]{1,0:T(8,128)S(1)}, f32[24,512]{1,0:T(8,128)S(1)}, u32[]{:S(2)}, u32[]{:S(2)}) %collective-permute-start.9) | collective-permute-done | bytes 49184 | tf_op jit(solution)/shard_map/ppermute | solution.py:496
  68.2 3.0 %collective-permute-start.11 = (f32[32,512]{1,0:T(8,128)S(1)}, f32[32,512]{1,0:T(8,128)S(1)}, u32[]{:S(2)}, u32[]{:S(2)}) collective-permute-start(f32[32,512]{1,0:T(8,128)S(1)} %pad_maximum_fusion.1.taps_ref), channel_id=1, source_target_pairs={{0,4},{1,5},{2,6},{3,7},{4,0},{5,1},{6,2},{7,3},{8,12},{9,13},{10,... | collective-permute-start | bytes 196616 | tf_op jit(solution)/shard_map/ppermute | solution.py:496
  71.1 0.0 collective-permute-start.12
  71.2 4.1 %collective-permute-done.12.other_ref = f32[24,512]{1,0:T(8,128)S(1)} collective-permute-done((f32[24,512]{1,0:T(8,128)S(1)}, f32[24,512]{1,0:T(8,128)S(1)}, u32[]{:S(2)}, u32[]{:S(2)}) %collective-permute-start.12) | collective-permute-done | bytes 49184 | tf_op jit(solution)/shard_map/ppermute | solution.py:496
  75.2 0.0 collective-permute-done.11.next_taps_ref
  75.2 0.8 %final.1 = (f32[128,256]{1,0:T(8,128)}, f32[3,7,512]{2,1,0:T(8,128)}, f32[1,512]{1,0:T(1,128)}) custom-call(f32[32,512]{1,0:T(8,128)S(1)} %pad_maximum_fusion.1.taps_ref, f32[32,512]{1,0:T(8,128)S(1)} %collective-permute-done.11.next_taps_ref, f32[24,512]{1,0:T(8,128)S(1)} %add.37.sums_ref, f32[24,512]{1,0:T(8,128)S(1)} %collective-permute-done.12.other_ref), custom_call_target="tpu_custom_call" | custom-call | tf_op jit(solution)/shard_map/final/pallas_call | solution.py:701
  (18 shorter events, 0.1 us)
Async XLA Ops:
  0.6 9.8 %copy-start = (bf16[512,3,512]{2,0,1:T(8,128)(2,1)S(1)}, bf16[512,3,512]{2,0,1:T(8,128)(2,1)}, u32[]{:S(2)}) copy-start(bf16[512,3,512]{2,0,1:T(8,128)(2,1)} %param.6) | copy-start | bytes 4718596
  0.6 9.8 %copy-start.6 = (s32[64]{0:T(128)S(1)}, s32[64]{0:T(128)}, u32[]{:S(2)}) copy-start(s32[64]{0:T(128)} %lengths_ref.2) | copy-start | bytes 772
  0.7 9.8 %copy-start.1 = (bf16[512,512]{1,0:T(8,128)(2,1)S(1)}, bf16[512,512]{1,0:T(8,128)(2,1)}, u32[]{:S(2)}) copy-start(bf16[512,512]{1,0:T(8,128)(2,1)} %cot_ref.9) | copy-start | bytes 1572868
  0.7 9.8 %copy-start.3 = (f32[7,3,512]{2,0,1:T(8,128)S(1)}, f32[7,3,512]{2,0,1:T(8,128)}, u32[]{:S(2)}) copy-start(f32[7,3,512]{2,0,1:T(8,128)} %param.7) | copy-start | bytes 129028
  4.4 12.9 %collective-permute-start = (bf16[320,512]{1,0:T(8,128)(2,1)}, bf16[320,512]{1,0:T(8,128)(2,1)S(1)}, u32[]{:S(2)}, u32[]{:S(2)}) collective-permute-start(bf16[320,512]{1,0:T(8,128)(2,1)} %get-tuple-element.54.own_up_ref), channel_id=1, source_target_pairs={{0,8},{8,16},{16,24},{24,32},{32,40},{40,48},{48,56},{56,64},{64,7... | collective-permute-start | bytes 983048 | tf_op jit(solution)/shard_map/ppermute | solution.py:547
  8.2 6.1 %copy-start.4 = (f32[128,256]{1,0:T(8,128)S(1)}, f32[128,256]{1,0:T(8,128)}, u32[]{:S(2)}) copy-start(f32[128,256]{1,0:T(8,128)} %medium_ref) | copy-start | bytes 393220
  8.2 12.8 %copy-start.2 = (bf16[320,512]{1,0:T(8,128)(2,1)S(1)}, bf16[320,512]{1,0:T(8,128)(2,1)}, u32[]{:S(2)}) copy-start(bf16[320,512]{1,0:T(8,128)(2,1)} %get-tuple-element.54.own_up_ref) | copy-start | bytes 983044
  8.3 12.8 %collective-permute-start.1 = (bf16[320,512]{1,0:T(8,128)(2,1)}, bf16[320,512]{1,0:T(8,128)(2,1)S(1)}, u32[]{:S(2)}, u32[]{:S(2)}) collective-permute-start(bf16[320,512]{1,0:T(8,128)(2,1)} %get-tuple-element.55), channel_id=1, source_target_pairs={{8,0},{16,8},{24,16},{32,24},{40,32},{48,40},{56,48},{64,56},{72,6... | collective-permute-start | bytes 983048 | tf_op jit(solution)/shard_map/ppermute | solution.py:548
  21.1 8.3 %copy-start.5 = (f32[512]{0:T(512)S(1)}, f32[512]{0:T(512)}, u32[]{:S(2)}) copy-start(f32[512]{0:T(512)} %param.9) | copy-start | bytes 6148
  26.5 5.4 %collective-permute-start.2 = (f32[8,512]{1,0:T(8,128)S(1)}, f32[8,512]{1,0:T(8,128)S(1)}, u32[]{:S(2)}, u32[]{:S(2)}) collective-permute-start(f32[8,512]{1,0:T(8,128)S(1)} %get-tuple-element.60), channel_id=1, source_target_pairs={{0,192},{8,200},{16,208},{24,216},{32,224},{40,232},{48,240},{56,2... | collective-permute-start | bytes 49160 | tf_op jit(solution)/shard_map/ppermute | solution.py:496
  31.9 3.8 %collective-permute-start.3 = (f32[8,512]{1,0:T(8,128)S(1)}, f32[8,512]{1,0:T(8,128)S(1)}, u32[]{:S(2)}, u32[]{:S(2)}) collective-permute-start(f32[8,512]{1,0:T(8,128)S(1)} %add.30), channel_id=1, source_target_pairs={{0,64},{8,72},{16,80},{24,88},{32,96},{40,104},{48,112},{56,120},{... | collective-permute-start | bytes 49160 | tf_op jit(solution)/shard_map/ppermute | solution.py:496
  35.8 8.2 %collective-permute-start.4 = (f32[8,512]{1,0:T(8,128)S(1)}, f32[8,512]{1,0:T(8,128)S(1)}, u32[]{:S(2)}, u32[]{:S(2)}) collective-permute-start(f32[8,512]{1,0:T(8,128)S(1)} %add.31), channel_id=1, source_target_pairs={{0,8},{8,0},{16,24},{24,16},{32,40},{40,32},{48,56},{56,48},{64,72... | collective-permute-start | bytes 49160 | tf_op jit(solution)/shard_map/ppermute | solution.py:496
  44.0 5.3 %collective-permute-start.5 = (f32[32,512]{1,0:T(8,128)S(1)}, f32[32,512]{1,0:T(8,128)S(1)}, u32[]{:S(2)}, u32[]{:S(2)}) collective-permute-start(f32[32,512]{1,0:T(8,128)S(1)} %pad_maximum_fusion), channel_id=1, source_target_pairs={{0,16},{8,24},{16,0},{24,8},{32,48},{40,56},{48,32},{56,40},{64,80... | collective-permute-start | bytes 196616 | tf_op jit(solution)/shard_map/ppermute | solution.py:496
  49.3 7.5 %collective-permute-start.6 = (f32[32,512]{1,0:T(8,128)S(1)}, f32[32,512]{1,0:T(8,128)S(1)}, u32[]{:S(2)}, u32[]{:S(2)}) collective-permute-start(f32[32,512]{1,0:T(8,128)S(1)} %constant_dynamic-update-slice_fusion), channel_id=1, source_target_pairs={{0,56},{8,48},{16,40},{24,32},{32,24},{40,16},{48,8},{56,0},{64,12... | collective-permute-start | bytes 196616 | tf_op jit(solution)/shard_map/ppermute | solution.py:496
  56.9 1.3 %collective-permute-start.8 = (f32[8,512]{1,0:T(8,128)S(1)}, f32[8,512]{1,0:T(8,128)S(1)}, u32[]{:S(2)}, u32[]{:S(2)}) collective-permute-start(f32[8,512]{1,0:T(8,128)S(1)} %slice.19), channel_id=1, source_target_pairs={{0,1},{1,0},{2,3},{3,2},{4,5},{5,4},{6,7},{7,6},{8,9},{9,8},{10,11... | collective-permute-start | bytes 49160 | tf_op jit(solution)/shard_map/ppermute | solution.py:496
  57.0 4.2 %collective-permute-start.7 = (f32[24,512]{1,0:T(8,128)S(1)}, f32[24,512]{1,0:T(8,128)S(1)}, u32[]{:S(2)}, u32[]{:S(2)}) collective-permute-start(f32[24,512]{1,0:T(8,128)S(1)} %slice.18), channel_id=1, source_target_pairs={{0,8},{8,0},{16,24},{24,16},{32,40},{40,32},{48,56},{56,48},{64,72... | collective-permute-start | bytes 147464 | tf_op jit(solution)/shard_map/ppermute | solution.py:496
  61.2 4.0 %collective-permute-start.10 = (f32[16,512]{1,0:T(8,128)S(1)}, f32[16,512]{1,0:T(8,128)S(1)}, u32[]{:S(2)}, u32[]{:S(2)}) collective-permute-start(f32[16,512]{1,0:T(8,128)S(1)} %pad_maximum_fusion.2), channel_id=1, source_target_pairs={{0,2},{1,3},{2,0},{3,1},{4,6},{5,7},{6,4},{7,5},{8,10},{9,11},{10,... | collective-permute-start | bytes 98312 | tf_op jit(solution)/shard_map/ppermute | solution.py:496
  62.8 5.3 %collective-permute-start.9 = (f32[24,512]{1,0:T(8,128)S(1)}, f32[24,512]{1,0:T(8,128)S(1)}, u32[]{:S(2)}, u32[]{:S(2)}) collective-permute-start(f32[24,512]{1,0:T(8,128)S(1)} %add.35), channel_id=1, source_target_pairs={{0,192},{8,200},{16,208},{24,216},{32,224},{40,232},{48,240},{56,2... | collective-permute-start | bytes 147464 | tf_op jit(solution)/shard_map/ppermute | solution.py:496
  68.2 7.1 %collective-permute-start.11 = (f32[32,512]{1,0:T(8,128)S(1)}, f32[32,512]{1,0:T(8,128)S(1)}, u32[]{:S(2)}, u32[]{:S(2)}) collective-permute-start(f32[32,512]{1,0:T(8,128)S(1)} %pad_maximum_fusion.1.taps_ref), channel_id=1, source_target_pairs={{0,4},{1,5},{2,6},{3,7},{4,0},{5,1},{6,2},{7,3},{8,12},{9,13},{10,... | collective-permute-start | bytes 196616 | tf_op jit(solution)/shard_map/ppermute | solution.py:496
  71.1 4.1 %collective-permute-start.12 = (f32[24,512]{1,0:T(8,128)S(1)}, f32[24,512]{1,0:T(8,128)S(1)}, u32[]{:S(2)}, u32[]{:S(2)}) collective-permute-start(f32[24,512]{1,0:T(8,128)S(1)} %add.37.sums_ref), channel_id=1, source_target_pairs={{0,64},{8,72},{16,80},{24,88},{32,96},{40,104},{48,112},{56,120},{... | collective-permute-start | bytes 147464 | tf_op jit(solution)/shard_map/ppermute | solution.py:496

commit v7 on v6

--- a/solution.py
+++ b/solution.py
@@ -677,7 +677,7 @@
 
     sums = jnp.concatenate(parts, axis=1)
     grad_streams = kvg
-    routes = routes_z()[2:] + routes_z()[:2] + routes_x()
+    routes = routes_z()[:1] + routes_z()[2:] + routes_z()[1:2] + routes_x()
     flip = 1
     for step, route in enumerate(routes):
         if step < 2:

time: 76.1 us -> 76.8 us (level)
  waiting for transfers between devices: 22.4 us -> 23.6 us
    ppermute x11, waiting for transfers between devices: 18.6 us -> 19.9 us  [along(): return lax.ppermute(block, axis, route)]
  transfers between devices with their start and end apart: 13 -> 13, of which waited for: 8 -> 9; matrix products, arithmetic and copies ran while one was open for 0% -> 0% of each run, Pallas kernels for 29% -> 29%
where the time goes in v7:
time: 76.8 us; the launch traced here: 76.6 us
  Pallas kernels  32.2 us (42%)
  waiting for transfers between devices  23.6 us (31%)
  starting transfers between devices  19.7 us (26%)
  between operations  0.96 us (1%)
    ppermute x11, waiting for transfers between devices, along(): return lax.ppermute(block, axis, route)  19.9 us
    ppermute x11, starting transfers between devices, along(): return lax.ppermute(block, axis, route)  13.8 us
    pallas_call x3, Pallas kernels, convolve(): pl.pallas_call(functools.partial(conv_kernel, members, first), grid=(coun...  10.3 us
    pallas_call x1, Pallas kernels, shards(): pl.pallas_call(functools.partial(pair_kernel, members), grid=(tiles, 2),...  5.45 us
    pallas_call x2, Pallas kernels, adjoint(): pl.pallas_call(functools.partial(adjoint_kernel, len(pieces)), grid=(2, 2...  5.09 us
    pallas_call x1, Pallas kernels, shards(): pl.pallas_call(functools.partial(own_kernel, members), grid=(tiles,), in_...  3.91 us
    ppermute x1, starting transfers between devices, shards(): lax.ppermute(pay_up, 'ctx', [(i, i + 1) for i in range(members - 1)])  3.83 us
    ppermute x1, waiting for transfers between devices, shards(): lax.ppermute(pay_down, 'ctx', [(i + 1, i) for i in range(members - 1)])  3.72 us
  transfers between devices with their start and end apart: 13, of which 9 were waited for; matrix products, arithmetic and copies ran while one was open for 0% of the time, Pallas kernels for 29%

profile of v7, /device:TPU:64, one launch (start us, length us, event | category | flops | bytes accessed | tf_op | source)
XLA Modules:
  0.0 76.6 jit_solution(12378374844690364689)
XLA Ops:
  0.6 0.0 copy-start
  0.6 0.0 copy-start.6
  0.7 0.0 copy-start.1
  0.7 0.0 copy-start.3
  0.7 3.7 %payload_rows.1 = (bf16[320,512]{1,0:T(8,128)(2,1)}, bf16[320,512]{1,0:T(8,128)(2,1)}) custom-call(s32[64]{0:T(128)} %lengths_ref.2, bf16[3,512,512]{2,1,0:T(8,128)(2,1)} %bitcast.6, bf16[512,512]{1,0:T(8,128)(2,1)} %cot_ref.9, f32[3,7,512]{2,1,0:T(8,128)} %bitcast.12), custom_call_target="tpu_custom_call" | custom-call | flops 20000000 | bytes 2800000 | tf_op jit(solution)/shard_map/payload_rows/pallas_call | solution.py:525
  4.4 3.8 %collective-permute-start = (bf16[320,512]{1,0:T(8,128)(2,1)}, bf16[320,512]{1,0:T(8,128)(2,1)S(1)}, u32[]{:S(2)}, u32[]{:S(2)}) collective-permute-start(bf16[320,512]{1,0:T(8,128)(2,1)} %get-tuple-element.54.own_up_ref), channel_id=1, source_target_pairs={{0,8},{8,16},{16,24},{24,32},{32,40},{40,48},{48,56},{56,64},{64,7... | collective-permute-start | bytes 983048 | tf_op jit(solution)/shard_map/ppermute | solution.py:547
  8.2 0.0 copy-start.4
  8.2 0.0 copy-start.2
  8.3 2.1 %collective-permute-start.1 = (bf16[320,512]{1,0:T(8,128)(2,1)}, bf16[320,512]{1,0:T(8,128)(2,1)S(1)}, u32[]{:S(2)}, u32[]{:S(2)}) collective-permute-start(bf16[320,512]{1,0:T(8,128)(2,1)} %get-tuple-element.55), channel_id=1, source_target_pairs={{8,0},{16,8},{24,16},{32,24},{40,32},{48,40},{56,48},{64,56},{72,6... | collective-permute-start | bytes 983048 | tf_op jit(solution)/shard_map/ppermute | solution.py:548
  10.4 0.0 copy-done
  10.4 0.0 copy-done.6
  10.4 0.0 copy-done.1
  10.4 0.0 copy-done.3
  10.4 3.9 %own_rows.1.kvg_ref.refs_4_ = bf16[3,512,512]{2,1,0:T(8,128)(2,1)S(1)} custom-call(s32[64]{0:T(128)S(1)} %copy-done.6, bf16[3,512,512]{2,1,0:T(8,128)(2,1)S(1)} %bitcast.7, bf16[512,512]{1,0:T(8,128)(2,1)S(1)} %copy-done.1, f32[3,7,512]{2,1,0:T(8,128)S(1)} %bitcast.13), custom_call_target="tpu_custom_call" | custom-call | flops 40000000 | bytes 4500000 | tf_op jit(solution)/shard_map/own_rows/pallas_call | solution.py:550
  14.4 0.0 copy-done.4
  14.4 2.9 %tables.1 = (bf16[32,128,256]{2,1,0:T(8,128)(2,1)S(1)}, bf16[32,128,256]{2,1,0:T(8,128)(2,1)S(1)}, bf16[2,3,128,256]{3,2,1,0:T(8,128)(2,1)S(1)}, bf16[2,3,128,25...) custom-call(s32[64]{0:T(128)S(1)} %copy-done.6, ...), custom_call_target="tpu_custom_call" | custom-call | flops 20000000 | bytes 7000000 | tf_op jit(solution)/shard_map/tables/pallas_call | solution.py:572
  17.3 0.0 collective-permute-done.up_ref
  17.3 3.7 %collective-permute-done.1.down_ref = bf16[320,512]{1,0:T(8,128)(2,1)S(1)} collective-permute-done((bf16[320,512]{1,0:T(8,128)(2,1)}, bf16[320,512]{1,0:T(8,128)(2,1)S(1)}, u32[]{:S(2)}, u32[]{:S(2)}) %collective-permute-start.1) | collective-permute-done | bytes 327712 | tf_op jit(solution)/shard_map/ppermute | solution.py:548
  21.1 0.0 copy-done.2
  21.1 0.0 copy-start.5
  21.1 5.5 %pair_rows.1 = (bf16[2,512,512]{2,1,0:T(8,128)(2,1)S(1)}, bf16[2,512,512]{2,1,0:T(8,128)(2,1)S(1)}, bf16[2,2,272,512]{3,2,1,0:T(8,128)(2,1)S(1)}, f32[8,512]{1,0:T(8,128)S(1)}) custom-call(bf16[3,512,512]{2,1,0:T(8,128)(2,1)S(1)} %bitcast.8, bf16[3,512,512]{2,1,0:T(8,128)(2,1)S(1)} %own_rows.1.kvg_ref.refs_4_, bf16[512,512]{1,0:T(8,128)(2,1)S(1)} %copy-done.1, ...), custom_call_target="tpu_custom_call" | custom-call | flops 500000000 | bytes 10000000 | tf_op jit(solution)/shard_map/pair_rows/pallas_call | solution.py:607
  26.5 2.8 %collective-permute-start.2 = (f32[8,512]{1,0:T(8,128)S(1)}, f32[8,512]{1,0:T(8,128)S(1)}, u32[]{:S(2)}, u32[]{:S(2)}) collective-permute-start(f32[8,512]{1,0:T(8,128)S(1)} %get-tuple-element.60), channel_id=1, source_target_pairs={{0,192},{8,200},{16,208},{24,216},{32,224},{40,232},{48,240},{56,2... | collective-permute-start | bytes 49160 | tf_op jit(solution)/shard_map/ppermute | solution.py:496
  29.4 0.0 copy-done.5
  29.4 2.5 %conv_rows_0.1 = (bf16[2,3,272,128]{3,2,1,0:T(8,128)(2,1)S(1)}, f32[24,128]{1,0:T(8,128)S(1)}) custom-call(bf16[3,512,512]{2,1,0:T(8,128)(2,1)S(1)} %bitcast.9, bf16[2,512,512]{2,1,0:T(8,128)(2,1)S(1)} %get-tuple-element.77.mixed_ref, bf16[2,512,512]{2,1,0:T(8,128)(2,1)S(1)} %get-tuple-element.78.grads_ref, ...), custom_call_target="tpu_custom_call" | custom-call | flops 100000000 | bytes 2500000 | tf_op jit(solution)/shard_map/conv_rows_0/pallas_call | solution.py:630
  31.9 0.0 collective-permute-done.2
  31.9 0.3 collective-permute-start.3
  32.3 2.5 %conv_rows_1.1 = (bf16[2,3,272,128]{3,2,1,0:T(8,128)(2,1)S(1)}, f32[24,128]{1,0:T(8,128)S(1)}) custom-call(bf16[3,512,512]{2,1,0:T(8,128)(2,1)S(1)} %bitcast.10, bf16[2,512,512]{2,1,0:T(8,128)(2,1)S(1)} %get-tuple-element.77.mixed_ref, bf16[2,512,512]{2,1,0:T(8,128)(2,1)S(1)} %get-tuple-element.78.grads_ref, ...), custom_call_target="tpu_custom_call" | custom-call | flops 100000000 | bytes 2500000 | tf_op jit(solution)/shard_map/conv_rows_1/pallas_call | solution.py:630
  34.8 1.0 %collective-permute-done.3 = f32[8,512]{1,0:T(8,128)S(1)} collective-permute-done((f32[8,512]{1,0:T(8,128)S(1)}, f32[8,512]{1,0:T(8,128)S(1)}, u32[]{:S(2)}, u32[]{:S(2)}) %collective-permute-start.3) | collective-permute-done | bytes 16416 | tf_op jit(solution)/shard_map/ppermute | solution.py:496
  35.8 2.9 %collective-permute-start.4 = (f32[8,512]{1,0:T(8,128)S(1)}, f32[8,512]{1,0:T(8,128)S(1)}, u32[]{:S(2)}, u32[]{:S(2)}) collective-permute-start(f32[8,512]{1,0:T(8,128)S(1)} %add.31), channel_id=1, source_target_pairs={{0,8},{8,0},{16,24},{24,16},{32,40},{40,32},{48,56},{56,48},{64,72... | collective-permute-start | bytes 49160 | tf_op jit(solution)/shard_map/ppermute | solution.py:496
  38.7 5.2 %conv_rows_2.1 = (bf16[2,3,272,256]{3,2,1,0:T(8,128)(2,1)S(1)}, f32[24,256]{1,0:T(8,128)S(1)}) custom-call(bf16[3,512,512]{2,1,0:T(8,128)(2,1)S(1)} %bitcast.11, bf16[2,512,512]{2,1,0:T(8,128)(2,1)S(1)} %get-tuple-element.77.mixed_ref, bf16[2,512,512]{2,1,0:T(8,128)(2,1)S(1)} %get-tuple-element.78.grads_ref, ...), custom_call_target="tpu_custom_call" | custom-call | flops 200000000 | bytes 5000000 | tf_op jit(solution)/shard_map/conv_rows_2/pallas_call | solution.py:630
  43.9 0.0 collective-permute-done.4
  44.0 0.8 %collective-permute-start.5 = (f32[32,512]{1,0:T(8,128)S(1)}, f32[32,512]{1,0:T(8,128)S(1)}, u32[]{:S(2)}, u32[]{:S(2)}) collective-permute-start(f32[32,512]{1,0:T(8,128)S(1)} %pad_maximum_fusion), channel_id=1, source_target_pairs={{0,56},{8,48},{16,40},{24,32},{32,24},{40,16},{48,8},{56,0},{64,12... | collective-permute-start | bytes 196616 | tf_op jit(solution)/shard_map/ppermute | solution.py:496
  44.8 2.6 %adjoint_rows_0.1.refs_3_ = bf16[3,512,512]{2,1,0:T(8,128)(2,1)} custom-call(bf16[2,3,272,128]{3,2,1,0:T(8,128)(2,1)S(1)} %get-tuple-element.82.refs_0_, bf16[2,3,272,128]{3,2,1,0:T(8,128)(2,1)S(1)} %get-tuple-element.83.refs_1_, f32[3,7,512]{2,1,0:T(8,128)S(1)} %bitcast.18, f32[2,6,256,128]{3,2,1,0:T(8,128)S(1)} %get-tuple-element.68.shifted_ref.refs_3_.refs_2_, ...), custom_call_target="tpu_custom_call" | custom-call | flops 20000000 | bytes 4000000 | tf_op jit(solution)/shard_map/adjoint_rows_0/pallas_call | solution.py:663
  47.4 4.6 %collective-permute-done.5 = f32[32,512]{1,0:T(8,128)S(1)} collective-permute-done((f32[32,512]{1,0:T(8,128)S(1)}, f32[32,512]{1,0:T(8,128)S(1)}, u32[]{:S(2)}, u32[]{:S(2)}) %collective-permute-start.5) | collective-permute-done | bytes 65568 | tf_op jit(solution)/shard_map/ppermute | solution.py:496
  52.0 0.3 collective-permute-start.6
  52.3 2.5 %adjoint_rows_2.1 = bf16[3,512,512]{2,1,0:T(8,128)(2,1)} custom-call(bf16[2,3,272,256]{3,2,1,0:T(8,128)(2,1)S(1)} %get-tuple-element.86.refs_0_, f32[3,7,512]{2,1,0:T(8,128)S(1)} %bitcast.19, f32[2,6,256,128]{3,2,1,0:T(8,128)S(1)} %get-tuple-element.68.shifted_ref.refs_3_.refs_2_, ...), custom_call_target="tpu_custom_call", output_to_operand_aliasing={{}: (3, {})} | custom-call | flops 20000000 | bytes 4000000 | tf_op jit(solution)/shard_map/adjoint_rows_2/pallas_call | solution.py:663
  54.8 2.6 %collective-permute-done.6 = f32[32,512]{1,0:T(8,128)S(1)} collective-permute-done((f32[32,512]{1,0:T(8,128)S(1)}, f32[32,512]{1,0:T(8,128)S(1)}, u32[]{:S(2)}, u32[]{:S(2)}) %collective-permute-start.6) | collective-permute-done | bytes 65568 | tf_op jit(solution)/shard_map/ppermute | solution.py:496
  57.5 0.1 collective-permute-start.8
  57.6 0.1 collective-permute-start.7
  57.7 1.1 %collective-permute-done.8 = f32[8,512]{1,0:T(8,128)S(1)} collective-permute-done((f32[8,512]{1,0:T(8,128)S(1)}, f32[8,512]{1,0:T(8,128)S(1)}, u32[]{:S(2)}, u32[]{:S(2)}) %collective-permute-start.8) | collective-permute-done | bytes 16416 | tf_op jit(solution)/shard_map/ppermute | solution.py:496
  58.8 3.0 %collective-permute-done.7 = f32[24,512]{1,0:T(8,128)S(1)} collective-permute-done((f32[24,512]{1,0:T(8,128)S(1)}, f32[24,512]{1,0:T(8,128)S(1)}, u32[]{:S(2)}, u32[]{:S(2)}) %collective-permute-start.7) | collective-permute-done | bytes 49184 | tf_op jit(solution)/shard_map/ppermute | solution.py:496
  61.8 1.7 %collective-permute-start.10 = (f32[16,512]{1,0:T(8,128)S(1)}, f32[16,512]{1,0:T(8,128)S(1)}, u32[]{:S(2)}, u32[]{:S(2)}) collective-permute-start(f32[16,512]{1,0:T(8,128)S(1)} %pad_maximum_fusion.2), channel_id=1, source_target_pairs={{0,2},{1,3},{2,0},{3,1},{4,6},{5,7},{6,4},{7,5},{8,10},{9,11},{10,... | collective-permute-start | bytes 98312 | tf_op jit(solution)/shard_map/ppermute | solution.py:496
  63.5 1.8 %collective-permute-start.9 = (f32[24,512]{1,0:T(8,128)S(1)}, f32[24,512]{1,0:T(8,128)S(1)}, u32[]{:S(2)}, u32[]{:S(2)}) collective-permute-start(f32[24,512]{1,0:T(8,128)S(1)} %add.35), channel_id=1, source_target_pairs={{0,192},{8,200},{16,208},{24,216},{32,224},{40,232},{48,240},{56,2... | collective-permute-start | bytes 147464 | tf_op jit(solution)/shard_map/ppermute | solution.py:496
  65.2 0.6 collective-permute-done.10
  65.8 2.9 %collective-permute-done.9 = f32[24,512]{1,0:T(8,128)S(1)} collective-permute-done((f32[24,512]{1,0:T(8,128)S(1)}, f32[24,512]{1,0:T(8,128)S(1)}, u32[]{:S(2)}, u32[]{:S(2)}) %collective-permute-start.9) | collective-permute-done | bytes 49184 | tf_op jit(solution)/shard_map/ppermute | solution.py:496
  68.8 3.0 %collective-permute-start.11 = (f32[32,512]{1,0:T(8,128)S(1)}, f32[32,512]{1,0:T(8,128)S(1)}, u32[]{:S(2)}, u32[]{:S(2)}) collective-permute-start(f32[32,512]{1,0:T(8,128)S(1)} %pad_maximum_fusion.1.taps_ref), channel_id=1, source_target_pairs={{0,4},{1,5},{2,6},{3,7},{4,0},{5,1},{6,2},{7,3},{8,12},{9,13},{10,... | collective-permute-start | bytes 196616 | tf_op jit(solution)/shard_map/ppermute | solution.py:496
  71.8 0.0 collective-permute-start.12
  71.8 4.1 %collective-permute-done.12.other_ref = f32[24,512]{1,0:T(8,128)S(1)} collective-permute-done((f32[24,512]{1,0:T(8,128)S(1)}, f32[24,512]{1,0:T(8,128)S(1)}, u32[]{:S(2)}, u32[]{:S(2)}) %collective-permute-start.12) | collective-permute-done | bytes 49184 | tf_op jit(solution)/shard_map/ppermute | solution.py:496
  75.9 0.0 collective-permute-done.11.next_taps_ref
  75.9 0.8 %final.1 = (f32[128,256]{1,0:T(8,128)}, f32[3,7,512]{2,1,0:T(8,128)}, f32[1,512]{1,0:T(1,128)}) custom-call(f32[32,512]{1,0:T(8,128)S(1)} %pad_maximum_fusion.1.taps_ref, f32[32,512]{1,0:T(8,128)S(1)} %collective-permute-done.11.next_taps_ref, f32[24,512]{1,0:T(8,128)S(1)} %add.37.sums_ref, f32[24,512]{1,0:T(8,128)S(1)} %collective-permute-done.12.other_ref), custom_call_target="tpu_custom_call" | custom-call | tf_op jit(solution)/shard_map/final/pallas_call | solution.py:701
  (18 shorter events, 0.1 us)
Async XLA Ops:
  0.6 9.8 %copy-start = (bf16[512,3,512]{2,0,1:T(8,128)(2,1)S(1)}, bf16[512,3,512]{2,0,1:T(8,128)(2,1)}, u32[]{:S(2)}) copy-start(bf16[512,3,512]{2,0,1:T(8,128)(2,1)} %param.6) | copy-start | bytes 4718596
  0.6 9.8 %copy-start.6 = (s32[64]{0:T(128)S(1)}, s32[64]{0:T(128)}, u32[]{:S(2)}) copy-start(s32[64]{0:T(128)} %lengths_ref.2) | copy-start | bytes 772
  0.7 9.8 %copy-start.1 = (bf16[512,512]{1,0:T(8,128)(2,1)S(1)}, bf16[512,512]{1,0:T(8,128)(2,1)}, u32[]{:S(2)}) copy-start(bf16[512,512]{1,0:T(8,128)(2,1)} %cot_ref.9) | copy-start | bytes 1572868
  0.7 9.8 %copy-start.3 = (f32[7,3,512]{2,0,1:T(8,128)S(1)}, f32[7,3,512]{2,0,1:T(8,128)}, u32[]{:S(2)}) copy-start(f32[7,3,512]{2,0,1:T(8,128)} %param.7) | copy-start | bytes 129028
  4.4 12.9 %collective-permute-start = (bf16[320,512]{1,0:T(8,128)(2,1)}, bf16[320,512]{1,0:T(8,128)(2,1)S(1)}, u32[]{:S(2)}, u32[]{:S(2)}) collective-permute-start(bf16[320,512]{1,0:T(8,128)(2,1)} %get-tuple-element.54.own_up_ref), channel_id=1, source_target_pairs={{0,8},{8,16},{16,24},{24,32},{32,40},{40,48},{48,56},{56,64},{64,7... | collective-permute-start | bytes 983048 | tf_op jit(solution)/shard_map/ppermute | solution.py:547
  8.2 6.1 %copy-start.4 = (f32[128,256]{1,0:T(8,128)S(1)}, f32[128,256]{1,0:T(8,128)}, u32[]{:S(2)}) copy-start(f32[128,256]{1,0:T(8,128)} %medium_ref) | copy-start | bytes 393220
  8.2 12.8 %copy-start.2 = (bf16[320,512]{1,0:T(8,128)(2,1)S(1)}, bf16[320,512]{1,0:T(8,128)(2,1)}, u32[]{:S(2)}) copy-start(bf16[320,512]{1,0:T(8,128)(2,1)} %get-tuple-element.54.own_up_ref) | copy-start | bytes 983044
  8.3 12.8 %collective-permute-start.1 = (bf16[320,512]{1,0:T(8,128)(2,1)}, bf16[320,512]{1,0:T(8,128)(2,1)S(1)}, u32[]{:S(2)}, u32[]{:S(2)}) collective-permute-start(bf16[320,512]{1,0:T(8,128)(2,1)} %get-tuple-element.55), channel_id=1, source_target_pairs={{8,0},{16,8},{24,16},{32,24},{40,32},{48,40},{56,48},{64,56},{72,6... | collective-permute-start | bytes 983048 | tf_op jit(solution)/shard_map/ppermute | solution.py:548
  21.1 8.3 %copy-start.5 = (f32[512]{0:T(512)S(1)}, f32[512]{0:T(512)}, u32[]{:S(2)}) copy-start(f32[512]{0:T(512)} %param.9) | copy-start | bytes 6148
  26.5 5.4 %collective-permute-start.2 = (f32[8,512]{1,0:T(8,128)S(1)}, f32[8,512]{1,0:T(8,128)S(1)}, u32[]{:S(2)}, u32[]{:S(2)}) collective-permute-start(f32[8,512]{1,0:T(8,128)S(1)} %get-tuple-element.60), channel_id=1, source_target_pairs={{0,192},{8,200},{16,208},{24,216},{32,224},{40,232},{48,240},{56,2... | collective-permute-start | bytes 49160 | tf_op jit(solution)/shard_map/ppermute | solution.py:496
  31.9 3.8 %collective-permute-start.3 = (f32[8,512]{1,0:T(8,128)S(1)}, f32[8,512]{1,0:T(8,128)S(1)}, u32[]{:S(2)}, u32[]{:S(2)}) collective-permute-start(f32[8,512]{1,0:T(8,128)S(1)} %add.30), channel_id=1, source_target_pairs={{0,64},{8,72},{16,80},{24,88},{32,96},{40,104},{48,112},{56,120},{... | collective-permute-start | bytes 49160 | tf_op jit(solution)/shard_map/ppermute | solution.py:496
  35.8 8.2 %collective-permute-start.4 = (f32[8,512]{1,0:T(8,128)S(1)}, f32[8,512]{1,0:T(8,128)S(1)}, u32[]{:S(2)}, u32[]{:S(2)}) collective-permute-start(f32[8,512]{1,0:T(8,128)S(1)} %add.31), channel_id=1, source_target_pairs={{0,8},{8,0},{16,24},{24,16},{32,40},{40,32},{48,56},{56,48},{64,72... | collective-permute-start | bytes 49160 | tf_op jit(solution)/shard_map/ppermute | solution.py:496
  44.0 8.0 %collective-permute-start.5 = (f32[32,512]{1,0:T(8,128)S(1)}, f32[32,512]{1,0:T(8,128)S(1)}, u32[]{:S(2)}, u32[]{:S(2)}) collective-permute-start(f32[32,512]{1,0:T(8,128)S(1)} %pad_maximum_fusion), channel_id=1, source_target_pairs={{0,56},{8,48},{16,40},{24,32},{32,24},{40,16},{48,8},{56,0},{64,12... | collective-permute-start | bytes 196616 | tf_op jit(solution)/shard_map/ppermute | solution.py:496
  52.0 5.4 %collective-permute-start.6 = (f32[32,512]{1,0:T(8,128)S(1)}, f32[32,512]{1,0:T(8,128)S(1)}, u32[]{:S(2)}, u32[]{:S(2)}) collective-permute-start(f32[32,512]{1,0:T(8,128)S(1)} %constant_dynamic-update-slice_fusion), channel_id=1, source_target_pairs={{0,16},{8,24},{16,0},{24,8},{32,48},{40,56},{48,32},{56,40},{64,80... | collective-permute-start | bytes 196616 | tf_op jit(solution)/shard_map/ppermute | solution.py:496
  57.5 1.3 %collective-permute-start.8 = (f32[8,512]{1,0:T(8,128)S(1)}, f32[8,512]{1,0:T(8,128)S(1)}, u32[]{:S(2)}, u32[]{:S(2)}) collective-permute-start(f32[8,512]{1,0:T(8,128)S(1)} %slice.19), channel_id=1, source_target_pairs={{0,1},{1,0},{2,3},{3,2},{4,5},{5,4},{6,7},{7,6},{8,9},{9,8},{10,11... | collective-permute-start | bytes 49160 | tf_op jit(solution)/shard_map/ppermute | solution.py:496
  57.6 4.2 %collective-permute-start.7 = (f32[24,512]{1,0:T(8,128)S(1)}, f32[24,512]{1,0:T(8,128)S(1)}, u32[]{:S(2)}, u32[]{:S(2)}) collective-permute-start(f32[24,512]{1,0:T(8,128)S(1)} %slice.18), channel_id=1, source_target_pairs={{0,8},{8,0},{16,24},{24,16},{32,40},{40,32},{48,56},{56,48},{64,72... | collective-permute-start | bytes 147464 | tf_op jit(solution)/shard_map/ppermute | solution.py:496
  61.8 4.0 %collective-permute-start.10 = (f32[16,512]{1,0:T(8,128)S(1)}, f32[16,512]{1,0:T(8,128)S(1)}, u32[]{:S(2)}, u32[]{:S(2)}) collective-permute-start(f32[16,512]{1,0:T(8,128)S(1)} %pad_maximum_fusion.2), channel_id=1, source_target_pairs={{0,2},{1,3},{2,0},{3,1},{4,6},{5,7},{6,4},{7,5},{8,10},{9,11},{10,... | collective-permute-start | bytes 98312 | tf_op jit(solution)/shard_map/ppermute | solution.py:496
  63.5 5.3 %collective-permute-start.9 = (f32[24,512]{1,0:T(8,128)S(1)}, f32[24,512]{1,0:T(8,128)S(1)}, u32[]{:S(2)}, u32[]{:S(2)}) collective-permute-start(f32[24,512]{1,0:T(8,128)S(1)} %add.35), channel_id=1, source_target_pairs={{0,192},{8,200},{16,208},{24,216},{32,224},{40,232},{48,240},{56,2... | collective-permute-start | bytes 147464 | tf_op jit(solution)/shard_map/ppermute | solution.py:496
  68.8 7.1 %collective-permute-start.11 = (f32[32,512]{1,0:T(8,128)S(1)}, f32[32,512]{1,0:T(8,128)S(1)}, u32[]{:S(2)}, u32[]{:S(2)}) collective-permute-start(f32[32,512]{1,0:T(8,128)S(1)} %pad_maximum_fusion.1.taps_ref), channel_id=1, source_target_pairs={{0,4},{1,5},{2,6},{3,7},{4,0},{5,1},{6,2},{7,3},{8,12},{9,13},{10,... | collective-permute-start | bytes 196616 | tf_op jit(solution)/shard_map/ppermute | solution.py:496
  71.8 4.1 %collective-permute-start.12 = (f32[24,512]{1,0:T(8,128)S(1)}, f32[24,512]{1,0:T(8,128)S(1)}, u32[]{:S(2)}, u32[]{:S(2)}) collective-permute-start(f32[24,512]{1,0:T(8,128)S(1)} %add.37.sums_ref), channel_id=1, source_target_pairs={{0,64},{8,72},{16,80},{24,88},{32,96},{40,104},{48,112},{56,120},{... | collective-permute-start | bytes 147464 | tf_op jit(solution)/shard_map/ppermute | solution.py:496
